TPU v7x, 32 devices: a whole 2x2x4 slice. The times are simulated.
32 devices in a mesh: ctx: 8 (over y, x, core), head: 4 (over z).
Axes of the slice: x: 2, y: 2, z: 4, core: 2. Of those that a mesh axis runs over, the one named last changes fastest.
Arguments:
- queries: bfloat16 [4, 8, 8192], P(None, 'ctx', 'head')
- kv_cache: bfloat16 [8, 64, 2, 64, 1024], P(None, 'ctx', None, None, 'head'), may hold values from -6 to 6
- new_kv: bfloat16 [4, 8, 2, 1024], P(None, 'ctx', None, 'head'), may hold values from -6 to 6
- selected: int32 [4, 8, 8, 8], P(None, None, 'head'), may hold values from 0 to 63, as said below
- out_weight: bfloat16 [8192, 8192], P('head', 'ctx'), may hold values from -0.0625 to 0.0625
Outputs:
- mixed: bfloat16 [8, 4, 8192], P('head', None, 'ctx')
Inputs may be any that keep to these rules, and one draw needn't show every extreme that they name: Each list selected[s, b, k] names 8 distinct pages; at most 4 of them lie in one aligned block of pages 8 * i to 8 * i + 8 - 1 (the pages of one index of ctx), and exactly 4 in some such block of every list.
All inputs are finite; a program needn't handle non-finite values.
Results may differ from a plain program's by a relative error of at most 0.022.
Values may be sent and summed in bfloat16 or wider, within the bound.
No kernel may reach another device: no remote copies, remote signals or barrier semaphores. Data moves between devices by JAX's collectives and lax.ppermute only.
A program may use at most 128 MiB of HBM per device.

v0:
```python
import jax
import jax.numpy as jnp
from jax import lax
from jax.sharding import PartitionSpec as P

HQ = 64
KVH = 8
HD = 128
PAGE = 64


NEG = -1e30


def merged(part, axis, combine):
    gathered = jax.tree.map(lambda a: lax.all_gather(a, axis), part)

    def take(source):
        return jax.tree.map(lambda a: lax.dynamic_index_in_dim(a, source, 0, False), gathered)

    return lax.fori_loop(
        1, lax.axis_size(axis), lambda source, state: combine(state, take(source)), take(0)
    )


def combine(former, latter):
    top_one, total_one, sum_one = former
    top_two, total_two, sum_two = latter
    top_both = jnp.maximum(top_one, top_two)
    factor_one = jnp.exp(top_one - top_both)
    factor_two = jnp.exp(top_two - top_both)
    return (
        top_both,
        total_one * factor_one + total_two * factor_two,
        sum_one * factor_one[..., None] + sum_two * factor_two[..., None],
    )


def partial_of(scores, allowed, values, form):
    masked = jnp.where(allowed, scores, NEG)
    top_score = jnp.max(masked, axis=-1)
    expo = jnp.where(allowed, jnp.exp(masked - top_score[..., None]), 0.0)
    total = jnp.sum(expo, axis=-1)
    weighted = jnp.einsum(
        form, expo.astype(jnp.bfloat16), values, preferred_element_type=jnp.float32
    )
    return (top_score, total, weighted)


def local(queries, kv_cache, new_kv, selected, out_weight):
    steps, own_rows, width = queries.shape
    heads_kv = kv_cache.shape[4] // HD
    groups = HQ // KVH
    pages_dev = kv_cache.shape[1]
    scale = HD ** (-0.5)
    everyone = lax.all_gather(queries, "ctx", axis=1, tiled=True)
    batch = everyone.shape[1]
    q_heads = everyone.reshape(steps, batch, heads_kv, groups, HD)
    first_page = lax.axis_index("ctx") * pages_dev
    keys = kv_cache[:, :, 0].reshape(batch, pages_dev * PAGE, heads_kv, HD)
    values = kv_cache[:, :, 1].reshape(batch, pages_dev * PAGE, heads_kv, HD)
    scores = (
        jnp.einsum("sbkgd,btkd->sbkgt", q_heads, keys, preferred_element_type=jnp.float32) * scale
    )
    numbers = first_page + jnp.arange(pages_dev)
    chosen = jnp.any(selected[..., None] == numbers, axis=3)
    allowed = jnp.repeat(chosen, PAGE, axis=3)[:, :, :, None, :]
    partial_value = partial_of(scores, allowed, values, "sbkgt,btkd->sbkgd")
    own_q = queries.reshape(steps, own_rows, heads_kv, groups, HD)
    new_keys = new_kv[:, :, 0].reshape(steps, own_rows, heads_kv, HD)
    new_values = new_kv[:, :, 1].reshape(steps, own_rows, heads_kv, HD)
    new_scores = (
        jnp.einsum("sbkgd,rbkd->sbkgr", own_q, new_keys, preferred_element_type=jnp.float32) * scale
    )
    causal = (jnp.arange(steps)[None, :] <= jnp.arange(steps)[:, None])[:, None, None, None, :]
    fresh = partial_of(new_scores, causal, new_values, "sbkgr,rbkd->sbkgd")
    own_start = lax.axis_index("ctx") * own_rows
    mine = tuple(
        (lax.dynamic_slice_in_dim(member, own_start, own_rows, 1) for member in partial_value)
    )
    joined = combine(mine, fresh)
    partial_value = tuple(
        (
            lax.dynamic_update_slice_in_dim(member, part_new, own_start, 1)
            for member, part_new in zip(partial_value, joined)
        )
    )
    top_score, total, weighted = merged(partial_value, "ctx", combine)
    attention = (weighted / total[..., None]).astype(jnp.bfloat16).reshape(steps, batch, width)
    by_sequence = jnp.transpose(attention, (1, 0, 2))
    return lax.psum_scatter(
        jnp.einsum(
            "bsf,fd->bsd", by_sequence, out_weight, preferred_element_type=jnp.float32
        ).astype(jnp.bfloat16),
        "head",
        scatter_dimension=0,
        tiled=True,
    )


def solution(mesh):
    return jax.shard_map(
        local,
        mesh=mesh,
        in_specs=(
            P(None, "ctx", "head"),
            P(None, "ctx", None, None, "head"),
            P(None, "ctx", None, "head"),
            P(None, None, "head", None),
            P("head", "ctx"),
        ),
        out_specs=P("head", None, "ctx"),
        check_vma=False,
    )
```

profile of v0, /device:TPU:0, one launch (start us, length us, event | category | flops | bytes accessed | tf_op | source)
XLA Modules:
  0.0 118.2 jit_solution(5114165719840967352)
XLA Ops:
  6.5 0.9 compare_reduce_fusion
  7.5 0.1 broadcast_in_dim.59
  7.7 0.2 broadcast_in_dim.60
  7.8 4.0 %fusion.54 = (bf16[8,8,1,64,256]{4,3,2,1,0:T(8,128)(2,1)S(1)}, bf16[8,8,1,64,256]{4,3,2,1,0:T(8,128)(2,1)}) fusion(bf16[8,8,2,64,256]{4,3,2,1,0:T(8,128)(2,1)} %param.8), kind=kLoop, calls=%fused_computation.71 | loop fusion | bytes 8388608 | tf_op jit(solution)/shard_map/slice | solution.py:61
  11.8 4.0 %reshape_squeeze.8 = bf16[8,512,2,128]{3,2,1,0:T(2,128)(2,1)} reshape(bf16[8,8,1,64,256]{4,3,2,1,0:T(8,128)(2,1)} %get-tuple-element.233) | data formatting | bytes 4194304 | tf_op jit(solution)/shard_map/reshape;squeeze | solution.py:60
  15.8 10.7 %all_gather.27 = bf16[4,8,2048]{2,0,1:T(4,128)(2,1)S(1)} all-gather(bf16[4,1,2048]{2,0,1:T(4,128)(2,1)S(1)} %copy-done.1), channel_id=1, replica_groups=mesh['ctx'=8,'head'=4] {'ctx'}, dimensions={1}, use_global_device_ids=true | all-gather | bytes 147456 | tf_op jit(solution)/shard_map/all_gather | solution.py:56
  26.6 0.2 fusion.57
  26.8 2.1 %reshape_squeeze.9 = bf16[8,512,2,128]{3,2,1,0:T(2,128)(2,1)} reshape(bf16[8,8,1,64,256]{4,3,2,1,0:T(8,128)(2,1)S(1)} %get-tuple-element.232) | data formatting | bytes 4194304 | tf_op jit(solution)/shard_map/reshape;squeeze | solution.py:61
  28.8 2.6 %fusion.56 = (f32[4,8,2,8]{3,0,2,1:T(4,128)S(1)}, f32[4,8,2,8,512]{4,3,0,2,1:T(8,128)S(1)}) fusion(bf16[4,8,2,8,128]{4,3,2,0,1:T(8,128)(2,1)S(1)} %reshape.78, bf16[8,512,2,128,1]{3,2,1,0,4:T(2,128)(2,1)} %bitcast.132, pred[4,8,2,512]{3,0,2,1:T(4,128)(4,1)S(1)} %broadcast_in_dim.60), kind=kOutput, calls=%fused_computation.73 | convolution fusion | flops 67894784 | bytes 3311616 | tf_op jit(solution)/shard_map/sbkgd,btkd->sbkgt/dot_general | solution.py:63
  31.5 0.6 fusion.6
  32.1 0.2 fusion.25
  32.4 0.8 copy.87
  33.2 0.4 fusion.29
  33.7 0.1 fusion.38
  33.8 9.3 %all_gather.30 = f32[8,4,8,2,8]{4,2,3,1,0:T(8,128)S(1)} all-gather(f32[1,4,8,2,8]{4,2,3,1,0:T(8,128)S(1)} %copy.74), channel_id=1, replica_groups=mesh['ctx'=8,'head'=4] {'ctx'}, dimensions={0}, use_global_device_ids=true | all-gather | bytes 18432 | tf_op jit(solution)/shard_map/all_gather | solution.py:16
  43.1 8.3 %all_gather.33 = f32[8,4,8,2,8]{4,2,3,1,0:T(8,128)S(1)} all-gather(f32[1,4,8,2,8]{4,2,3,1,0:T(8,128)S(1)} %copy.80), channel_id=1, replica_groups=mesh['ctx'=8,'head'=4] {'ctx'}, dimensions={0}, use_global_device_ids=true | all-gather | bytes 18432 | tf_op jit(solution)/shard_map/all_gather | solution.py:16
  51.5 10.0 %all-gather.2.cloned.1.call-done = f32[8,4,8,2,8,128]{5,4,3,2,1,0:T(8,128)} async-done(((f32[1,4,8,2,8,128]{5,4,3,2,1,0:T(8,128)}), f32[8,4,8,2,8,128]{5,4,3,2,1,0:T(8,128)}) %all-gather.2.cloned.1.call-update) | async-done | bytes 2097168 | tf_op jit(solution)/shard_map/all_gather | solution.py:16
  61.5 1.0 slice_bitcast_fusion
  62.5 9.4 %while.19 = (s32[]{:T(128)}, f32[4,8,2,8]{3,2,1,0:T(2,128)S(1)}, f32[4,8,2,8]{3,2,1,0:T(2,128)S(1)}, f32[4,8,2,8,128]{4,3,2,1,0:T(8,128)S(1)}, f32[8,4,8,2,8]{4,...) while((s32[]{:T(128)}, f32[4,8,2,8]{3,2,1,0:T(2,128)S(1)}, ...), condition=%wide.region_6.7_spmd, body=%wide.region_5.6_spmd.sunk | while | flops 199685 | bytes 815255 | solution.py:21
  62.6 1.2 %fusion.61 = f32[4,8,2,8,128]{4,3,2,1,0:T(8,128)S(1)} fusion(f32[8,4,8,2,8,128]{5,4,3,2,1,0:T(8,128)} %get-tuple-element.325, s32[]{:T(128)S(6)} %select_n.61, f32[4,8,2,8,128]{4,3,2,1,0:T(8,128)S(1)} %get-tuple-element.312, f32[4,8,2,8]{3,2,1,0:T(2,128)S(1)} %get-tuple-element.297, f32[4,8,2,8]{3,2,1,0:T(2,128)S(1)} %get-tuple-element.298), kind=kLoop, calls=%fused_computation.1.clone.1 | loop fusion | flops 196608 | bytes 790532 | tf_op jit(solution)/shard_map/while/body/eval_jaxpr/add | solution.py:35
  64.0 1.2 %fusion.61 = f32[4,8,2,8,128]{4,3,2,1,0:T(8,128)S(1)} fusion(f32[8,4,8,2,8,128]{5,4,3,2,1,0:T(8,128)} %get-tuple-element.325, s32[]{:T(128)S(6)} %select_n.61, f32[4,8,2,8,128]{4,3,2,1,0:T(8,128)S(1)} %get-tuple-element.312, f32[4,8,2,8]{3,2,1,0:T(2,128)S(1)} %get-tuple-element.297, f32[4,8,2,8]{3,2,1,0:T(2,128)S(1)} %get-tuple-element.298), kind=kLoop, calls=%fused_computation.1.clone.1 | loop fusion | flops 196608 | bytes 790532 | tf_op jit(solution)/shard_map/while/body/eval_jaxpr/add | solution.py:35
  65.3 1.2 %fusion.61 = f32[4,8,2,8,128]{4,3,2,1,0:T(8,128)S(1)} fusion(f32[8,4,8,2,8,128]{5,4,3,2,1,0:T(8,128)} %get-tuple-element.325, s32[]{:T(128)S(6)} %select_n.61, f32[4,8,2,8,128]{4,3,2,1,0:T(8,128)S(1)} %get-tuple-element.312, f32[4,8,2,8]{3,2,1,0:T(2,128)S(1)} %get-tuple-element.297, f32[4,8,2,8]{3,2,1,0:T(2,128)S(1)} %get-tuple-element.298), kind=kLoop, calls=%fused_computation.1.clone.1 | loop fusion | flops 196608 | bytes 790532 | tf_op jit(solution)/shard_map/while/body/eval_jaxpr/add | solution.py:35
  66.7 1.2 %fusion.61 = f32[4,8,2,8,128]{4,3,2,1,0:T(8,128)S(1)} fusion(f32[8,4,8,2,8,128]{5,4,3,2,1,0:T(8,128)} %get-tuple-element.325, s32[]{:T(128)S(6)} %select_n.61, f32[4,8,2,8,128]{4,3,2,1,0:T(8,128)S(1)} %get-tuple-element.312, f32[4,8,2,8]{3,2,1,0:T(2,128)S(1)} %get-tuple-element.297, f32[4,8,2,8]{3,2,1,0:T(2,128)S(1)} %get-tuple-element.298), kind=kLoop, calls=%fused_computation.1.clone.1 | loop fusion | flops 196608 | bytes 790532 | tf_op jit(solution)/shard_map/while/body/eval_jaxpr/add | solution.py:35
  68.0 1.2 %fusion.61 = f32[4,8,2,8,128]{4,3,2,1,0:T(8,128)S(1)} fusion(f32[8,4,8,2,8,128]{5,4,3,2,1,0:T(8,128)} %get-tuple-element.325, s32[]{:T(128)S(6)} %select_n.61, f32[4,8,2,8,128]{4,3,2,1,0:T(8,128)S(1)} %get-tuple-element.312, f32[4,8,2,8]{3,2,1,0:T(2,128)S(1)} %get-tuple-element.297, f32[4,8,2,8]{3,2,1,0:T(2,128)S(1)} %get-tuple-element.298), kind=kLoop, calls=%fused_computation.1.clone.1 | loop fusion | flops 196608 | bytes 790532 | tf_op jit(solution)/shard_map/while/body/eval_jaxpr/add | solution.py:35
  69.4 1.2 %fusion.61 = f32[4,8,2,8,128]{4,3,2,1,0:T(8,128)S(1)} fusion(f32[8,4,8,2,8,128]{5,4,3,2,1,0:T(8,128)} %get-tuple-element.325, s32[]{:T(128)S(6)} %select_n.61, f32[4,8,2,8,128]{4,3,2,1,0:T(8,128)S(1)} %get-tuple-element.312, f32[4,8,2,8]{3,2,1,0:T(2,128)S(1)} %get-tuple-element.297, f32[4,8,2,8]{3,2,1,0:T(2,128)S(1)} %get-tuple-element.298), kind=kLoop, calls=%fused_computation.1.clone.1 | loop fusion | flops 196608 | bytes 790532 | tf_op jit(solution)/shard_map/while/body/eval_jaxpr/add | solution.py:35
  70.7 1.2 %fusion.61 = f32[4,8,2,8,128]{4,3,2,1,0:T(8,128)S(1)} fusion(f32[8,4,8,2,8,128]{5,4,3,2,1,0:T(8,128)} %get-tuple-element.325, s32[]{:T(128)S(6)} %select_n.61, f32[4,8,2,8,128]{4,3,2,1,0:T(8,128)S(1)} %get-tuple-element.312, f32[4,8,2,8]{3,2,1,0:T(2,128)S(1)} %get-tuple-element.297, f32[4,8,2,8]{3,2,1,0:T(2,128)S(1)} %get-tuple-element.298), kind=kLoop, calls=%fused_computation.1.clone.1 | loop fusion | flops 196608 | bytes 790532 | tf_op jit(solution)/shard_map/while/body/eval_jaxpr/add | solution.py:35
  71.9 0.1 divide_convert_fusion
  72.2 3.0 %fusion.19 = bf16[8,4,1024]{2,0,1:T(8,128)(2,1)S(1)} fusion(bf16[2048,1024]{1,0:T(8,128)(2,1)} %param.11, bf16[4,8,2048]{2,1,0:T(8,128)(2,1)S(1)} %reshape.72), kind=kOutput, calls=%fused_computation.20 | convolution fusion | flops 134250496 | bytes 4390912 | tf_op jit(solution)/shard_map/bsf,fd->bsd/dot_general | solution.py:92
  75.2 0.7 copy.92
  75.9 0.6 dynamic-slice.4
  77.1 32.9 %all-reduce.3.cloned.1.call-done = bf16[8,4,1024]{2,1,0:T(4,128)(2,1)} async-done(((bf16[8,4,1024]{2,1,0:T(4,128)(2,1)}), bf16[8,4,1024]{2,1,0:T(4,128)(2,1)}) %all-reduce.3.cloned.1.call-update) | async-done | bytes 65552
  110.0 1.3 %constant_dynamic-slice_fusion.2 = bf16[2,4,1024]{2,1,0:T(4,128)(2,1)} fusion(bf16[8,4,1024]{2,1,0:T(4,128)(2,1)} %all-reduce.3.cloned.1.call-done, u32[]{:T(128)S(6)} %multiply.5), kind=kLoop, calls=%fused_computation.67 | loop fusion | bytes 32772
  (44 shorter events, 1.1 us)
Async XLA Ops:
  6.5 55.0 %all-gather.2.cloned.1.call-start = ((), (), s32[]{:S(2)}) async-start(), calls=%async_computation | async-start | bytes 2359296 | tf_op jit(solution)/shard_map/all_gather | solution.py:16
  11.8 4.0 %copy-start.1 = (bf16[4,1,2048]{2,0,1:T(4,128)(2,1)S(1)}, bf16[4,1,2048]{2,0,1:T(4,128)(2,1)}, u32[]{:S(2)}) copy-start(bf16[4,1,2048]{2,0,1:T(4,128)(2,1)} %param.7) | copy-start | bytes 49156
  11.8 14.7 %copy-start.2 = (bf16[4,1,2,256]{3,2,1,0:T(2,128)(2,1)S(1)}, bf16[4,1,2,256]{3,2,1,0:T(2,128)(2,1)}, u32[]{:S(2)}) copy-start(bf16[4,1,2,256]{3,2,1,0:T(2,128)(2,1)} %param.9) | copy-start | bytes 12292
  28.8 2.6 %copy-start = (bf16[8,512,2,128]{3,2,1,0:T(2,128)(2,1)S(1)}, bf16[8,512,2,128]{3,2,1,0:T(2,128)(2,1)}, u32[]{:S(2)}) copy-start(bf16[8,512,2,128]{3,2,1,0:T(2,128)(2,1)} %reshape_squeeze.9) | copy-start | bytes 6291460
  33.2 76.8 %all-reduce.3.cloned.1.call-start = ((), (), s32[]{:S(2)}) async-start(), calls=%async_computation.1 | async-start | bytes 131072
  72.2 3.7 %copy-start.3 = (u32[32]{0:T(128)S(1)}, u32[32]{0:T(128)}, u32[]{:S(2)}) copy-start(u32[32]{0:T(128)} %constant.80) | copy-start | bytes 388
Sparse Core Ops, SparseCore 0:
  33.3 28.2 all-gather.1
  76.0 33.9 all-reduce.2
where the time goes:
time: 119 us; the launch traced here: 118 us
  waiting for transfers between devices  43 us (36%)
  blocking collectives  28.3 us (24%)
  local copies, waits for them, and re-layouts  15 us (13%)
  between operations  14.2 us (12%)
  other arithmetic  10.8 us (9%)
  matrix products  6.64 us (6%)
    unnamed x3, waiting for transfers between devices  32.9 us
    all_gather x2, blocking collectives, merged(): gathered = jax.tree.map(lambda a: lax.all_gather(a, axis), part)  17.6 us
    all_gather x1, blocking collectives, local(): everyone = lax.all_gather(queries, 'ctx', axis=1, tiled=True)  10.7 us
    all_gather x1, waiting for transfers between devices, merged(): gathered = jax.tree.map(lambda a: lax.all_gather(a, axis), part)  10 us
    add x7, other arithmetic, combine(): sum_one * factor_one[..., None] + sum_two * factor_two[..., None]  8.48 us
    slice x1, local copies, waits for them, and re-layouts, local(): values = kv_cache[:, :, 1].reshape(batch, pages_dev * PAGE, heads_kv, HD)  4 us
    another operation x1, local copies, waits for them, and re-layouts, local(): keys = kv_cache[:, :, 0].reshape(batch, pages_dev * PAGE, heads_kv, HD)  3.97 us
    dot_general x1, matrix products, local(): jnp.einsum('bsf,fd->bsd', by_sequence, out_weight, preferred_element_type...  2.99 us
  transfers between devices with their start and end apart: 2, of which 2 were waited for; matrix products, arithmetic and copies ran while one was open for 1% of the time, Pallas kernels for 0%

commit v1 on v0

v1 whole, which is shorter than its diff:
```python
import functools

import jax
import jax.numpy as jnp
from jax import lax
from jax.experimental import pallas as pl
from jax.experimental.pallas import tpu as pltpu
from jax.sharding import PartitionSpec as P

HQ = 64
KVH = 8
HD = 128
PAGE = 64
GROUPS = HQ // KVH
STAT_ROWS = 16
NEG = -1e30
WEIGHT_PIECES = 4
VMEM_LIMIT = 24 * 1024 * 1024

VMEM = pl.BlockSpec(memory_space=pltpu.VMEM)
ANY = pl.BlockSpec(memory_space=pl.ANY)
HBM = pl.BlockSpec(memory_space=pltpu.HBM)
NT = (((1,), (1,)), ((), ()))


def query_rows(q_ref, slot, turned):
    steps, width = q_ref.shape[1:]
    for j in range(width // HD):
        piece = q_ref[slot, :, j * HD : (j + 1) * HD]
        turned[j * steps : (j + 1) * steps, :] = piece.astype(jnp.float32)
    return turned[...].astype(jnp.bfloat16)


def spread_heads(query, heads):
    rows = query.shape[0]
    row_head = lax.broadcasted_iota(jnp.int32, (rows, heads * HD), 0) // (rows // heads)
    lane_head = lax.broadcasted_iota(jnp.int32, (rows, heads * HD), 1) // HD
    wide = jnp.concatenate([query] * heads, axis=1)
    return jnp.where(row_head == lane_head, wide, jnp.zeros_like(wide))


def own_heads(weighted, heads):
    span = weighted.shape[0] // heads
    return jnp.concatenate(
        [weighted[h * span : (h + 1) * span, h * HD : (h + 1) * HD] for h in range(heads)], axis=0
    )


def three_parts(x):
    high = x.astype(jnp.bfloat16).astype(jnp.float32)
    rest = x - high
    middle = rest.astype(jnp.bfloat16).astype(jnp.float32)
    return high, middle, rest - middle


def stat_rows(slots):
    return -(-3 * slots // STAT_ROWS) * STAT_ROWS


def columns_to_rows(columns):
    rows = columns[0].shape[0]
    lane = lax.broadcasted_iota(jnp.int32, (rows, 128), 1)
    sheet = jnp.zeros((rows, 128), jnp.float32)
    for i, column in enumerate(columns):
        sheet = jnp.where(lane == i, column, sheet)
    sheet = jnp.concatenate([sheet, jnp.zeros((128 - rows, 128), jnp.float32)], axis=0)
    turned = jnp.transpose(sheet)
    return [turned[i : i + 1] for i in range(len(columns))]


def rows_to_columns(listed, rows):
    columns = []
    for first in range(0, len(listed), 128):
        some = listed[first : first + 128]
        blank = [jnp.zeros((128 - len(some), 128), jnp.float32)] if len(some) < 128 else []
        turned = jnp.transpose(jnp.concatenate(some + blank, axis=0))
        columns += [turned[:rows, i : i + 1] for i in range(len(some))]
    return columns


def page_masks(bits_ref, seq, steps, page_bit):
    masks = []
    for h in range(bits_ref.shape[1]):
        bits = jnp.concatenate([bits_ref[seq, h]] * (page_bit.shape[1] // 128), axis=1)
        masks += [(page_bit & bits) != 0] * steps
    return jnp.concatenate(masks, axis=0)


def own_kernel(
    q_in, kv_in, selected_in, new_in, q_out, kv_out, bits_out, new_out, selected_ref, new_ref, sems
):
    steps, _, heads, _ = selected_ref.shape
    m, pages = kv_out.shape[:2]
    me = lax.axis_index("ctx")
    pairs = [(selected_in, selected_ref), (new_in, new_ref), (q_in, q_out)]
    pairs += [(kv_in.at[me ^ (2 * i)], kv_out.at[i]) for i in range(m)]
    copies = [pltpu.make_async_copy(*pair, sems.at[i]) for i, pair in enumerate(pairs)]
    for copy in copies:
        copy.start()
    for copy in copies[:2]:
        copy.wait()
    by_step = []
    for s in range(steps):
        lists = jnp.concatenate([selected_ref[s, me ^ (2 * i)] for i in range(m)], axis=0)
        for core in range(2):
            page = lists - (me ^ core) * pages
            here = (page >= 0) & (page < pages)
            bit = jnp.where(here, jnp.left_shift(1, page & 31), 0).astype(jnp.float32)
            total = jnp.sum(bit, axis=1, keepdims=True).astype(jnp.int32)
            by_step.append(jnp.broadcast_to(total, (m * heads, 128)))
    step_of = lax.broadcasted_iota(jnp.int32, (8, 128), 0) % steps
    for core in range(2):
        for i in range(m):
            for h in range(heads):
                row = i * heads + h
                bits = jnp.zeros((8, 128), jnp.int32)
                for s in range(steps):
                    bits = jnp.where(step_of == s, by_step[2 * s + core][row : row + 1], bits)
                bits_out[core, i, h] = bits
    for part in range(2):
        tokens = [new_ref[s, part : part + 1].astype(jnp.float32) for s in range(steps)]
        blank = jnp.zeros((16 - steps, new_ref.shape[2]), jnp.float32)
        new_out[part] = jnp.concatenate(tokens + [blank], axis=0).astype(jnp.bfloat16)
    for copy in copies[2:]:
        copy.wait()


def own_side(queries, kv_cache, selected, new_kv):
    batch, heads = selected.shape[1:3]
    m = batch // 2
    operands = (queries, kv_cache, selected, new_kv)
    return pl.pallas_call(
        own_kernel,
        out_shape=[
            jax.ShapeDtypeStruct(queries.shape, queries.dtype),
            jax.ShapeDtypeStruct((m,) + kv_cache.shape[1:], kv_cache.dtype),
            jax.ShapeDtypeStruct((2, m, heads, 8, 128), jnp.int32),
            jax.ShapeDtypeStruct((2, 16, new_kv.shape[2]), jnp.bfloat16),
        ],
        in_specs=[HBM] * 4,
        out_specs=[VMEM] * 4,
        scratch_shapes=[
            pltpu.VMEM(selected.shape, selected.dtype),
            pltpu.VMEM(new_kv.shape, new_kv.dtype),
            pltpu.SemaphoreType.DMA((3 + m,)),
        ],
        compiler_params=pltpu.CompilerParams(vmem_limit_bytes=VMEM_LIMIT),
        cost_estimate=pl.CostEstimate(
            flops=2**20, bytes_accessed=kv_cache.size * 2, transcendentals=0
        ),
    )(*[pltpu.with_memory_space_constraint(x, pltpu.HBM) for x in operands])


def page_masks(bits_ref, core, i, steps, page_bit):
    masks = []
    for h in range(bits_ref.shape[2]):
        bits = jnp.concatenate([bits_ref[core, i, h]] * (page_bit.shape[1] // 128), axis=1)
        masks += [(page_bit & bits) != 0] * steps
    return jnp.concatenate(masks, axis=0)


def attend(spread, pieces):
    found = []
    for keys, values, allowed in pieces:
        scores = lax.dot_general(spread, keys, NT, preferred_element_type=jnp.float32)
        found.append((allowed, jnp.where(allowed, scores * HD ** (-0.5), NEG), values))

    def finish():
        top = functools.reduce(
            jnp.maximum, [jnp.max(scores, axis=1, keepdims=True) for _, scores, _ in found]
        )
        total, weighted = 0.0, 0.0
        for allowed, scores, values in found:
            expo = jnp.where(allowed, jnp.exp(scores - top), 0.0)
            total = total + jnp.sum(expo, axis=1, keepdims=True)
            weighted = weighted + jnp.dot(
                expo.astype(jnp.bfloat16), values, preferred_element_type=jnp.float32
            )
        return top, total, weighted

    return finish


def page_pieces(kv_ref, where, bits_ref, core, i, steps, heads):
    tokens = kv_ref.shape[1] * PAGE
    page_bit = jnp.left_shift(1, lax.broadcasted_iota(jnp.int32, (8, tokens), 1) // PAGE)
    keys = kv_ref[where, :, 0].reshape(tokens, heads * HD)
    values = kv_ref[where, :, 1].reshape(tokens, heads * HD)
    return keys, values, page_masks(bits_ref, core, i, steps, page_bit)


def staged(count, ahead, begin, end):
    begun = [begin(i) for i in range(min(ahead, count))]
    for i in range(count):
        if i + ahead < count:
            begun.append(begin(i + ahead))
        end(i, begun[i]())


def first_kernel(heads, bits_ref, new_ref, own_ref, *refs):
    *q_refs, spread_ref, sum_ref, stat_ref, turned = refs
    steps = q_refs[0].shape[1]
    rows = turned.shape[1]

    def begin(i):
        spread = spread_heads(query_rows(q_refs[i], 0, turned.at[i]), heads)
        spread_ref[i] = spread
        pieces = [page_pieces(own_ref, i, bits_ref, 0, i, steps, heads)]
        if i == 0:
            step_of = lax.broadcasted_iota(jnp.int32, (rows, 16), 0) % steps
            causal = lax.broadcasted_iota(jnp.int32, (rows, 16), 1) <= step_of
            pieces.append((new_ref[0], new_ref[1], causal))
        return attend(spread, pieces)

    def end(i, state):
        top, total, weighted = state
        lane = lax.broadcasted_iota(jnp.int32, (rows, 128), 1)
        stat_ref[i] = jnp.where(lane == 0, top, total)
        sum_ref[i] = own_heads(weighted, heads)

    staged(len(q_refs), 1, begin, end)


def second_kernel(steps, heads, bits_ref, spread_ref, sum_ref, stat_ref, other_ref, out_ref):
    m, rows = spread_ref.shape[:2]
    me = lax.axis_index("ctx")
    columns = []

    def begin(i):
        pieces = [page_pieces(other_ref, me ^ (2 * i), bits_ref, 1, i, steps, heads)]
        return attend(spread_ref[i], pieces)

    def end(i, state):
        top, total, weighted = state
        stats = stat_ref[i]
        first_top, first_total = stats[:, 0:1], stats[:, 1:2]
        both = jnp.maximum(top, first_top)
        factor, first_factor = jnp.exp(top - both), jnp.exp(first_top - both)
        total = total * factor + first_total * first_factor
        total = jnp.where(total > 0.0, total, 1.0)
        joined = own_heads(weighted, heads) * (factor / total)
        joined = joined + sum_ref[i] * (first_factor / total)
        out_ref[i * rows : (i + 1) * rows, :] = joined.astype(jnp.bfloat16)
        columns.append(both + jnp.log(total))

    staged(m, m if m <= 4 else 2, begin, end)
    count = stat_rows(m)
    stat_row = lax.broadcasted_iota(jnp.int32, (count, 128), 0)
    block = jnp.zeros((count, 128), jnp.float32)
    for i, row in enumerate(columns_to_rows(columns)):
        for j, part in enumerate(three_parts(row)):
            block = jnp.where(stat_row == 3 * i + j, part, block)
    out_ref[m * rows :, :] = block.astype(jnp.bfloat16)


def partials(bits, new_pairs, own_kv, other_kv, queries, rows, heads):
    m, pages = own_kv.shape[:2]
    tokens, width = pages * PAGE, own_kv.shape[4]
    steps = queries[0].shape[1]
    options = dict(
        compiler_params=pltpu.CompilerParams(vmem_limit_bytes=VMEM_LIMIT),
        cost_estimate=pl.CostEstimate(
            flops=4 * m * rows * tokens * width,
            bytes_accessed=2**20,
            transcendentals=m * rows * tokens,
        ),
    )
    state = pl.pallas_call(
        functools.partial(first_kernel, heads),
        out_shape=[
            jax.ShapeDtypeStruct((m, rows, width), jnp.bfloat16),
            jax.ShapeDtypeStruct((m, rows, HD), jnp.float32),
            jax.ShapeDtypeStruct((m, rows, 128), jnp.float32),
        ],
        in_specs=[VMEM] * (3 + m),
        out_specs=[VMEM] * 3,
        scratch_shapes=[pltpu.VMEM((m, rows, HD), jnp.float32)],
        **options,
    )(bits, new_pairs, own_kv, *queries)
    return pl.pallas_call(
        functools.partial(second_kernel, steps, heads),
        out_shape=jax.ShapeDtypeStruct((m * rows + stat_rows(m), HD), jnp.bfloat16),
        in_specs=[VMEM] * 5,
        out_specs=VMEM,
        **options,
    )(bits, *state, other_kv)


def last_merge_kernel(rows, steps, *refs):
    *part_refs, _, out_ref = refs
    m = len(part_refs)
    stats = [ref[m * rows :, :].astype(jnp.float32) for ref in part_refs]
    factors = []
    for i in range(m):
        logs = []
        for j in range(m):
            k = 3 * (i ^ j)
            logs.append(stats[j][k : k + 1] + stats[j][k + 1 : k + 2] + stats[j][k + 2 : k + 3])
        top = functools.reduce(jnp.maximum, logs)
        some = [jnp.exp(x - top) for x in logs]
        total = functools.reduce(jnp.add, some)
        factors += [f / total for f in some]
    columns = rows_to_columns(factors, rows)
    for i in range(m):
        joined = jnp.zeros((rows, HD), jnp.float32)
        for j, ref in enumerate(part_refs):
            span = slice((i ^ j) * rows, ((i ^ j) + 1) * rows)
            joined = joined + columns[i * m + j] * ref[span, :].astype(jnp.float32)
        for j in range(rows // steps):
            piece = joined[j * steps : (j + 1) * steps]
            out_ref[i, :, j * HD : (j + 1) * HD] = piece.astype(jnp.bfloat16)


def last_merge(parts, weight, rows, steps):
    m = len(parts)
    return pl.pallas_call(
        functools.partial(last_merge_kernel, rows, steps),
        out_shape=jax.ShapeDtypeStruct((m, steps, rows // steps * HD), jnp.bfloat16),
        in_specs=[VMEM] * m + [ANY],
        out_specs=VMEM,
        compiler_params=pltpu.CompilerParams(vmem_limit_bytes=VMEM_LIMIT),
        cost_estimate=pl.CostEstimate(
            flops=2 * m * m * rows * HD, bytes_accessed=2**18, transcendentals=0
        ),
    )(*parts, weight)


def load_kernel(weight_ref, _, out_ref, sems):
    piece = out_ref.shape[0] // WEIGHT_PIECES
    copies = []
    for i in range(WEIGHT_PIECES):
        span = pl.ds(i * piece, piece)
        copy = pltpu.make_async_copy(weight_ref.at[span], out_ref.at[span], sems.at[i])
        copy.start()
        copies.append(copy)
    for copy in copies:
        copy.wait()


def load_weight(out_weight, after):
    return pl.pallas_call(
        load_kernel,
        out_shape=jax.ShapeDtypeStruct(out_weight.shape, out_weight.dtype),
        in_specs=[HBM, ANY],
        out_specs=VMEM,
        scratch_shapes=[pltpu.SemaphoreType.DMA((WEIGHT_PIECES,))],
        compiler_params=pltpu.CompilerParams(vmem_limit_bytes=VMEM_LIMIT),
        cost_estimate=pl.CostEstimate(
            flops=0, bytes_accessed=out_weight.size * 4, transcendentals=0
        ),
    )(pltpu.with_memory_space_constraint(out_weight, pltpu.HBM), after)


def project_rows(att_ref, weight_ref, lhs):
    count, _, width = lhs.shape
    steps = att_ref.shape[1]
    lhs[...] = jnp.zeros_like(lhs)
    for i in range(count):
        lhs[i, :steps, :] = att_ref[i].astype(jnp.float32)
    left = lhs[...].reshape(count * 8, width).astype(jnp.bfloat16)
    product = jnp.dot(left, weight_ref[...], preferred_element_type=jnp.float32)
    return product.reshape(count, 8, weight_ref.shape[1])


def half_kernel(att_ref, weight_ref, out_ref, lhs):
    out_ref[...] = project_rows(att_ref, weight_ref, lhs)


def project_kernel(n_head, targets, att_ref, half_ref, weight_ref, *refs):
    lhs, rows_all = refs[-2:]
    out_refs = refs[:-2]
    m, steps, _ = att_ref.shape
    seqs = 2 * m // n_head
    me = lax.axis_index("ctx")
    mine = lax.axis_index("head")
    product = project_rows(att_ref, weight_ref, lhs)
    for i in range(m):
        rows_all[2 * i] = product[i]
        rows_all[2 * i + 1] = half_ref[i]
    for k, ref in enumerate(out_refs):
        target = mine
        if k > 0:
            for core, row in enumerate(targets[k - 1]):
                for z, t in enumerate(row):
                    target = jnp.where((me % 2 == core) & (mine == z), t, target)
        for j in range(seqs):
            found = rows_all[(jnp.maximum(target, 0) * seqs + j) ^ me][:steps]
            if k > 0 and any(t < 0 for row in targets[k - 1] for t in row):
                found = jnp.where(target < 0, 0.0, found)
            ref[j] = found.astype(ref.dtype)


def project_options(att, weight):
    m, _, width = att.shape
    columns = weight.shape[1]
    return dict(
        compiler_params=pltpu.CompilerParams(vmem_limit_bytes=VMEM_LIMIT),
        cost_estimate=pl.CostEstimate(
            flops=2 * m * 8 * width * columns,
            bytes_accessed=width * columns * 2,
            transcendentals=0,
        ),
    )


def project_half(att, weight):
    m, _, width = att.shape
    return pl.pallas_call(
        half_kernel,
        out_shape=jax.ShapeDtypeStruct((m, 8, weight.shape[1]), jnp.float32),
        in_specs=[VMEM] * 2,
        out_specs=VMEM,
        scratch_shapes=[pltpu.VMEM((m, 8, width), jnp.float32)],
        **project_options(att, weight),
    )(att, weight)


def project(att, half, weight, n_head, targets):
    m, steps, width = att.shape
    n = 2 * m
    columns = weight.shape[1]
    outs = [
        jax.ShapeDtypeStruct((n // n_head, steps, columns), jnp.bfloat16 if k else jnp.float32)
        for k in range(1 + len(targets))
    ]
    return pl.pallas_call(
        functools.partial(project_kernel, n_head, targets),
        out_shape=outs,
        in_specs=[VMEM] * 3,
        out_specs=[VMEM] * len(outs),
        scratch_shapes=[
            pltpu.VMEM((m, 8, width), jnp.float32),
            pltpu.VMEM((n, 8, columns), jnp.float32),
        ],
        **project_options(att, weight),
    )(att, half, weight)


def head_plan(n_head):
    if n_head == 4:
        return [
            (((0, 1), (1, 1), (0, 3), (0, 0)), ((1, 2), (1, 3), (0, 2), (1, 0))),
            (((1, 0), (0, 2), (0, 0), (0, 1)), ((1, 1), (1, 2), (1, 3), (0, 3))),
            (((0, 3), (0, 0), (1, 2), (0, 2)), ((1, 3), (0, 1), (1, 0), (1, 1))),
            (((0, 2), (0, 3), (0, 1), (1, 3)), ((0, 0), (1, 0), (1, 1), (1, 2))),
        ]
    return [
        tuple(tuple((core, (z + t) % n_head) for z in range(n_head)) for core in range(2))
        for t in range(1, n_head)
    ]


def plan_targets(plan):
    seen = set()
    targets = []
    for permutation in plan:
        rows = []
        for core, row in enumerate(permutation):
            rows.append([])
            for z, (to_core, t) in enumerate(row):
                useful = to_core == core and (core, z, t) not in seen
                rows[core].append(t if useful else -1)
                if useful:
                    seen.add((core, z, t))
        targets.append(rows)
    return targets


def send_by(permutation, x):
    n, n_head = lax.axis_size("ctx"), lax.axis_size("head")
    pairs = []
    for c in range(n):
        for z in range(n_head):
            core, t = permutation[c % 2][z]
            pairs.append((c * n_head + z, (c - c % 2 + core) * n_head + t))
    return lax.ppermute(x, ("ctx", "head"), pairs)


def swap(x, axis, r):
    size = lax.axis_size(axis)
    return lax.ppermute(x, axis, [(i, i ^ r) for i in range(size)])


def swap_chips(x, n):
    return [swap(x, "ctx", r) for r in range(2, n, 2)]


def swap_other_cores(x, n):
    return [swap(x, "ctx", r) for r in range(1, n, 2)]


def local(queries, kv_cache, new_kv, selected, out_weight):
    steps, _, width = queries.shape
    heads = kv_cache.shape[4] // HD
    rows = steps * heads * GROUPS
    n = lax.axis_size("ctx")
    n_head = lax.axis_size("head")

    first_q = queries.reshape(1, steps, width)
    other_kv = swap(kv_cache, "ctx", 1)
    far_q = swap_chips(first_q, n)
    new_pairs = new_kv.reshape(steps, 2, heads * HD)
    own_q, own_kv, bits, new_pairs = own_side(first_q, kv_cache, selected, new_pairs)
    all_q = [own_q] + far_q
    sent = partials(bits, new_pairs, own_kv, other_kv, all_q, rows, heads)
    parts = swap_other_cores(sent, n)
    weight = load_weight(out_weight, sent)
    odd_att = last_merge(parts, weight, rows, steps)
    even_att = swap(odd_att, "ctx", 1)
    plan = head_plan(n_head)
    half = project_half(odd_att, weight)
    total, *rows_out = project(even_att, half, weight, n_head, plan_targets(plan))
    for chunk, permutation in zip(rows_out, plan):
        total = total + send_by(permutation, chunk).astype(jnp.float32)
    return total.astype(jnp.bfloat16)


def solution(mesh):
    return jax.shard_map(
        local,
        mesh=mesh,
        in_specs=(
            P(None, "ctx", "head"),
            P(None, "ctx", None, None, "head"),
            P(None, "ctx", None, "head"),
            P(None, None, "head", None),
            P("head", "ctx"),
        ),
        out_specs=P("head", None, "ctx"),
        check_vma=False,
    )
```

time: 119 us -> 27.3 us (0.23)
  waiting for transfers between devices: 43 us -> 5.45 us
  blocking collectives: 28.3 us -> 0 us
  local copies, waits for them, and re-layouts: 15 us -> 0 us
  between operations: 14.2 us -> 0.08 us
  starting transfers between devices: 0.04 us -> 12.8 us
  other arithmetic: 10.8 us -> 0.63 us
  Pallas kernels: 0 us -> 7.9 us
  matrix products: 6.64 us -> 0 us
    unnamed x3 -> x0, waiting for transfers between devices: 32.9 us -> none
    all_gather x3 -> x0, blocking collectives: 28.3 us -> none  [the longest x2 17.6 us: merged(): gathered = jax.tree.map(lambda a: lax.all_gather(a, axis), part)]
    ppermute x0 -> x13, starting transfers between devices: none -> 12.8 us  [the longest x9 8.1 us: swap(): return lax.ppermute(x, axis, [(i, i ^ r) for i in range(size)])]
    all_gather x1 -> x0, waiting for transfers between devices: 10 us -> none  [merged(): gathered = jax.tree.map(lambda a: lax.all_gather(a, axis), part)]
    add x15 -> x0, other arithmetic: 9.11 us -> none  [the longest x7 8.48 us: combine(): sum_one * factor_one[..., None] + sum_two * factor_two[..., None]]
    pallas_call x0 -> x7, Pallas kernels: none -> 7.9 us  [the longest x1 2.2 us: load_weight(): pl.pallas_call(load_kernel, out_shape=jax.ShapeDtypeStruct(out_weight.sha...]
    dot_general x5 -> x0, matrix products: 6.64 us -> none  [the longest x1 2.99 us: local(): jnp.einsum('bsf,fd->bsd', by_sequence, out_weight, preferred_element_type...]
    another operation x2 -> x0, local copies, waits for them, and re-layouts: 6.03 us -> none  [the longest x1 3.97 us: local(): keys = kv_cache[:, :, 0].reshape(batch, pages_dev * PAGE, heads_kv, HD)]
  transfers between devices with their start and end apart: 2 -> 13, of which waited for: 2 -> 8; matrix products, arithmetic and copies ran while one was open for 1% -> 0% of each run, Pallas kernels for 0% -> 21%
where the time goes in v1:
time: 27.3 us; the launch traced here: 26.8 us
  starting transfers between devices  12.8 us (47%)
  Pallas kernels  7.9 us (29%)
  waiting for transfers between devices  5.45 us (20%)
  other arithmetic  0.63 us (2%)
    ppermute x9, starting transfers between devices, swap(): return lax.ppermute(x, axis, [(i, i ^ r) for i in range(size)])  8.1 us
    ppermute x4, starting transfers between devices, send_by(): return lax.ppermute(x, ('ctx', 'head'), pairs)  4.68 us
    ppermute x9, waiting for transfers between devices, swap(): return lax.ppermute(x, axis, [(i, i ^ r) for i in range(size)])  3.51 us
    pallas_call x1, Pallas kernels, load_weight(): pl.pallas_call(load_kernel, out_shape=jax.ShapeDtypeStruct(out_weight.sha...  2.2 us
    ppermute x4, waiting for transfers between devices, send_by(): return lax.ppermute(x, ('ctx', 'head'), pairs)  1.95 us
    pallas_call x1, Pallas kernels, own_side(): pl.pallas_call(own_kernel, out_shape=[jax.ShapeDtypeStruct(queries.shape,...  1.63 us
    pallas_call x1, Pallas kernels, partials(): pl.pallas_call(functools.partial(second_kernel, steps, heads), out_shape=...  1.12 us
    pallas_call x1, Pallas kernels, partials(): pl.pallas_call(functools.partial(first_kernel, heads), out_shape=[jax.Sha...  0.91 us
  transfers between devices with their start and end apart: 13, of which 8 were waited for; matrix products, arithmetic and copies ran while one was open for 0% of the time, Pallas kernels for 21%

profile of v1, /device:TPU:0, one launch (start us, length us, event | category | flops | bytes accessed | tf_op | source)
XLA Modules:
  0.0 26.8 jit_solution(7582712044958453671)
XLA Ops:
  0.0 0.5 %collective-permute-start.3 = (bf16[8,8,2,64,256]{4,3,2,1,0:T(8,128)(2,1)}, bf16[8,8,2,64,256]{4,3,2,1,0:T(8,128)(2,1)S(1)}, u32[]{:S(2)}, u32[]{:S(2)}) collective-permute-start(bf16[8,8,2,64,256]{4,3,2,1,0:T(8,128)(2,1)} %kv_in.1), channel_id=1, source_target_pairs={{0,4},{4,0},{8,12},{12,8},{16,20},{20,16},{24,28},{28,24},{1,5},{5... | collective-permute-start | bytes 12582920 | tf_op jit(solution)/shard_map/ppermute | solution.py:481
  0.5 3.4 %collective-permute-start.2 = (bf16[1,4,2048]{2,1,0:T(4,128)(2,1)}, bf16[1,4,2048]{2,1,0:T(4,128)(2,1)S(1)}, u32[]{:S(2)}, u32[]{:S(2)}) collective-permute-start(bf16[1,4,2048]{2,1,0:T(4,128)(2,1)} %bitcast.2), channel_id=1, source_target_pairs={{0,24},{4,28},{8,16},{12,20},{16,8},{20,12},{24,0},{28,4},{1,25},{... | collective-permute-start | bytes 49160 | tf_op jit(solution)/shard_map/ppermute | solution.py:481
  3.9 0.5 %collective-permute-start.1 = (bf16[1,4,2048]{2,1,0:T(4,128)(2,1)}, bf16[1,4,2048]{2,1,0:T(4,128)(2,1)S(1)}, u32[]{:S(2)}, u32[]{:S(2)}) collective-permute-start(bf16[1,4,2048]{2,1,0:T(4,128)(2,1)} %bitcast.3), channel_id=1, source_target_pairs={{0,16},{4,20},{8,24},{12,28},{16,0},{20,4},{24,8},{28,12},{1,17},{... | collective-permute-start | bytes 49160 | tf_op jit(solution)/shard_map/ppermute | solution.py:481
  4.4 0.1 collective-permute-start
  4.5 1.6 %shard_map.55 = (bf16[1,4,2048]{2,1,0:T(4,128)(2,1)S(1)}, bf16[4,8,2,64,256]{4,3,2,1,0:T(8,128)(2,1)S(1)}, s32[2,4,2,8,128]{4,3,2,1,0:T(8,128)S(1)}, bf16[2,16,256]{2,1,0:T(8,128)(2,1)S(1)}) custom-call(bf16[1,4,2048]{2,1,0:T(4,128)(2,1)} %bitcast.5, bf16[8,8,2,64,256]{4,3,2,1,0:T(8,128)(2,1)} %kv_in.1, s32[4,8,2,8]{3,2,1,0:T(2,128)} %selected_in.1, ...), custom_call_target="tpu_custom_call" | custom-call | flops 1048576 | bytes 4194304 | tf_op jit(solution)/shard_map/pallas_call | solution.py:132
  6.2 0.0 collective-permute-done.2.refs_3_
  6.2 1.7 %collective-permute-done.1.refs_2_ = bf16[1,4,2048]{2,1,0:T(4,128)(2,1)S(1)} collective-permute-done((bf16[1,4,2048]{2,1,0:T(4,128)(2,1)}, bf16[1,4,2048]{2,1,0:T(4,128)(2,1)S(1)}, u32[]{:S(2)}, u32[]{:S(2)}) %collective-permute-start.1) | collective-permute-done | bytes 16416 | tf_op jit(solution)/shard_map/ppermute | solution.py:481
  7.8 0.5 %collective-permute-done.refs_1_ = bf16[1,4,2048]{2,1,0:T(4,128)(2,1)S(1)} collective-permute-done((bf16[1,4,2048]{2,1,0:T(4,128)(2,1)}, bf16[1,4,2048]{2,1,0:T(4,128)(2,1)S(1)}, u32[]{:S(2)}, u32[]{:S(2)}) %collective-permute-start) | collective-permute-done | bytes 16416 | tf_op jit(solution)/shard_map/ppermute | solution.py:481
  8.4 0.9 %shard_map.56 = (bf16[4,64,256]{2,1,0:T(8,128)(2,1)S(1)}, f32[4,64,128]{2,1,0:T(8,128)S(1)}, f32[4,64,128]{2,1,0:T(8,128)S(1)}) custom-call(s32[2,4,2,8,128]{4,3,2,1,0:T(8,128)S(1)} %get-tuple-element.17.bits_ref, bf16[2,16,256]{2,1,0:T(8,128)(2,1)S(1)} %get-tuple-element.18.new_ref, bf16[4,8,2,64,256]{4,3,2,1,0:T(8,128)(2,1)S(1)} %get-tuple-element.19.own_ref, ...), custom_call_target="tpu_custom_call" | custom-call | flops 134217728 | bytes 1048576 | tf_op jit(solution)/shard_map/pallas_call | solution.py:268
  9.3 0.0 collective-permute-done.3.other_ref
  9.3 1.1 %shard_map.57._ = bf16[272,128]{1,0:T(8,128)(2,1)S(1)} custom-call(s32[2,4,2,8,128]{4,3,2,1,0:T(8,128)S(1)} %get-tuple-element.17.bits_ref, bf16[4,64,256]{2,1,0:T(8,128)(2,1)S(1)} %get-tuple-element.21.spread_ref, f32[4,64,128]{2,1,0:T(8,128)S(1)} %get-tuple-element.22.sum_ref, f32[4,64,128]{2,1,0:T(8,128)S(1)} %get-tuple-element.23.stat_ref, ...), custom_call_target="tpu_custom_call" | custom-call | flops 134217728 | bytes 1048576 | tf_op jit(solution)/shard_map/pallas_call | solution.py:280
  10.4 1.8 %collective-permute-start.7 = (bf16[272,128]{1,0:T(8,128)(2,1)S(1)}, bf16[272,128]{1,0:T(8,128)(2,1)S(1)}, u32[]{:S(2)}, u32[]{:S(2)}) collective-permute-start(bf16[272,128]{1,0:T(8,128)(2,1)S(1)} %shard_map.57._), channel_id=1, source_target_pairs={{0,28},{4,24},{8,20},{12,16},{16,12},{20,8},{24,4},{28,0},{1,29},{... | collective-permute-start | bytes 208904 | tf_op jit(solution)/shard_map/ppermute | solution.py:481
  12.2 0.5 %collective-permute-start.6 = (bf16[272,128]{1,0:T(8,128)(2,1)S(1)}, bf16[272,128]{1,0:T(8,128)(2,1)S(1)}, u32[]{:S(2)}, u32[]{:S(2)}) collective-permute-start(bf16[272,128]{1,0:T(8,128)(2,1)S(1)} %shard_map.57._), channel_id=1, source_target_pairs={{0,20},{4,16},{8,28},{12,24},{16,4},{20,0},{24,12},{28,8},{1,21},{... | collective-permute-start | bytes 208904 | tf_op jit(solution)/shard_map/ppermute | solution.py:481
  12.7 0.5 %collective-permute-start.5 = (bf16[272,128]{1,0:T(8,128)(2,1)S(1)}, bf16[272,128]{1,0:T(8,128)(2,1)S(1)}, u32[]{:S(2)}, u32[]{:S(2)}) collective-permute-start(bf16[272,128]{1,0:T(8,128)(2,1)S(1)} %shard_map.57._), channel_id=1, source_target_pairs={{0,12},{4,8},{8,4},{12,0},{16,28},{20,24},{24,20},{28,16},{1,13},{... | collective-permute-start | bytes 208904 | tf_op jit(solution)/shard_map/ppermute | solution.py:481
  13.2 0.6 %collective-permute-start.4 = (bf16[272,128]{1,0:T(8,128)(2,1)S(1)}, bf16[272,128]{1,0:T(8,128)(2,1)S(1)}, u32[]{:S(2)}, u32[]{:S(2)}) collective-permute-start(bf16[272,128]{1,0:T(8,128)(2,1)S(1)} %shard_map.57._), channel_id=1, source_target_pairs={{0,4},{4,0},{8,12},{12,8},{16,20},{20,16},{24,28},{28,24},{1,5},{5... | collective-permute-start | bytes 208904 | tf_op jit(solution)/shard_map/ppermute | solution.py:481
  13.8 2.2 %shard_map.58.refs_4_.weight_ref = bf16[2048,1024]{1,0:T(8,128)(2,1)S(1)} custom-call(bf16[2048,1024]{1,0:T(8,128)(2,1)} %weight_ref.1, bf16[272,128]{1,0:T(8,128)(2,1)S(1)} %shard_map.57._), custom_call_target="tpu_custom_call" | custom-call | bytes 8388608 | tf_op jit(solution)/shard_map/pallas_call | solution.py:341
  16.0 0.0 collective-permute-done.7.refs_3_
  16.0 0.7 %collective-permute-done.6.refs_2_ = bf16[272,128]{1,0:T(8,128)(2,1)S(1)} collective-permute-done((bf16[272,128]{1,0:T(8,128)(2,1)S(1)}, bf16[272,128]{1,0:T(8,128)(2,1)S(1)}, u32[]{:S(2)}, u32[]{:S(2)}) %collective-permute-start.6) | collective-permute-done | bytes 69664 | tf_op jit(solution)/shard_map/ppermute | solution.py:481
  16.7 0.3 %collective-permute-done.5.refs_1_ = bf16[272,128]{1,0:T(8,128)(2,1)S(1)} collective-permute-done((bf16[272,128]{1,0:T(8,128)(2,1)S(1)}, bf16[272,128]{1,0:T(8,128)(2,1)S(1)}, u32[]{:S(2)}, u32[]{:S(2)}) %collective-permute-start.5) | collective-permute-done | bytes 69664 | tf_op jit(solution)/shard_map/ppermute | solution.py:481
  17.0 0.4 %shard_map.59.att_ref = bf16[4,4,2048]{2,1,0:T(4,128)(2,1)S(1)} custom-call(bf16[272,128]{1,0:T(8,128)(2,1)S(1)} %collective-permute-done.4.refs_0_, bf16[272,128]{1,0:T(8,128)(2,1)S(1)} %collective-permute-done.5.refs_1_, bf16[272,128]{1,0:T(8,128)(2,1)S(1)} %collective-permute-done.6.refs_2_, bf16[272,128]{1,0:T(8,128)(2,1)S(1)} %collective-permute-done.7.refs_3_, ...), custom_call_target="tpu_custom_call" | custom-call | flops 262144 | bytes 262144 | tf_op jit(solution)/shard_map/pallas_call | solution.py:316
  17.4 0.2 collective-permute-start.8
  17.6 0.8 %shard_map.60.half_ref = f32[4,8,1024]{2,1,0:T(8,128)S(1)} custom-call(bf16[4,4,2048]{2,1,0:T(4,128)(2,1)S(1)} %shard_map.59.att_ref, bf16[2048,1024]{1,0:T(8,128)(2,1)S(1)} %shard_map.58.refs_4_.weight_ref), custom_call_target="tpu_custom_call" | custom-call | flops 134217728 | bytes 4194304 | tf_op jit(solution)/shard_map/pallas_call | solution.py:408
  18.4 0.3 %collective-permute-done.8.att_ref = bf16[4,4,2048]{2,1,0:T(4,128)(2,1)S(1)} collective-permute-done((bf16[4,4,2048]{2,1,0:T(4,128)(2,1)S(1)}, bf16[4,4,2048]{2,1,0:T(4,128)(2,1)S(1)}, u32[]{:S(2)}, u32[]{:S(2)}) %collective-permute-start.8) | collective-permute-done | bytes 65568 | tf_op jit(solution)/shard_map/ppermute | solution.py:481
  18.7 0.9 %shard_map.61 = (f32[2,4,1024]{2,1,0:T(4,128)S(1)}, bf16[2,4,1024]{2,1,0:T(4,128)(2,1)S(1)}, bf16[2,4,1024]{2,1,0:T(4,128)(2,1)S(1)}, bf16[2,4,1024]{2,1,0:T(4,128)(2,1)S(1)}, bf16[2,4,1024]{2,1,0:T(4,128)(2,1)S(1)}) custom-call(bf16[4,4,2048]{2,1,0:T(4,128)(2,1)S(1)} %collective-permute-done.8.att_ref, f32[4,8,1024]{2,1,0:T(8,128)S(1)} %shard_map.60.half_ref, ...), custom_call_target="tpu_custom_call" | custom-call | flops 134217728 | bytes 4194304 | tf_op jit(solution)/shard_map/pallas_call | solution.py:426
  19.6 1.8 %collective-permute-start.9 = (bf16[2,4,1024]{2,1,0:T(4,128)(2,1)S(1)}, bf16[2,4,1024]{2,1,0:T(4,128)(2,1)S(1)}, u32[]{:S(2)}, u32[]{:S(2)}) collective-permute-start(bf16[2,4,1024]{2,1,0:T(4,128)(2,1)S(1)} %get-tuple-element.25), channel_id=1, source_target_pairs={{0,1},{1,5},{2,3},{3,0},{4,6},{5,7},{6,2},{7,4},{8,9},{9,13},{10,1... | collective-permute-start | bytes 49160 | tf_op jit(solution)/shard_map/ppermute | solution.py:476
  21.3 0.9 %collective-permute-start.10 = (bf16[2,4,1024]{2,1,0:T(4,128)(2,1)S(1)}, bf16[2,4,1024]{2,1,0:T(4,128)(2,1)S(1)}, u32[]{:S(2)}, u32[]{:S(2)}) collective-permute-start(bf16[2,4,1024]{2,1,0:T(4,128)(2,1)S(1)} %get-tuple-element.26), channel_id=1, source_target_pairs={{0,4},{1,2},{2,0},{3,1},{4,5},{5,6},{6,7},{7,3},{8,12},{9,10},{10,... | collective-permute-start | bytes 49160 | tf_op jit(solution)/shard_map/ppermute | solution.py:476
  22.2 1.6 %collective-permute-start.11 = (bf16[2,4,1024]{2,1,0:T(4,128)(2,1)S(1)}, bf16[2,4,1024]{2,1,0:T(4,128)(2,1)S(1)}, u32[]{:S(2)}, u32[]{:S(2)}) collective-permute-start(bf16[2,4,1024]{2,1,0:T(4,128)(2,1)S(1)} %get-tuple-element.27), channel_id=1, source_target_pairs={{0,3},{1,0},{2,6},{3,2},{4,7},{5,1},{6,4},{7,5},{8,11},{9,8},{10,1... | collective-permute-start | bytes 49160 | tf_op jit(solution)/shard_map/ppermute | solution.py:476
  23.9 0.4 %collective-permute-start.12 = (bf16[2,4,1024]{2,1,0:T(4,128)(2,1)S(1)}, bf16[2,4,1024]{2,1,0:T(4,128)(2,1)S(1)}, u32[]{:S(2)}, u32[]{:S(2)}) collective-permute-start(bf16[2,4,1024]{2,1,0:T(4,128)(2,1)S(1)} %get-tuple-element.28), channel_id=1, source_target_pairs={{0,2},{1,3},{2,1},{3,7},{4,0},{5,4},{6,5},{7,6},{8,10},{9,11},{10,... | collective-permute-start | bytes 49160 | tf_op jit(solution)/shard_map/ppermute | solution.py:476
  24.3 0.9 %collective-permute-done.9 = bf16[2,4,1024]{2,1,0:T(4,128)(2,1)S(1)} collective-permute-done((bf16[2,4,1024]{2,1,0:T(4,128)(2,1)S(1)}, bf16[2,4,1024]{2,1,0:T(4,128)(2,1)S(1)}, u32[]{:S(2)}, u32[]{:S(2)}) %collective-permute-start.9) | collective-permute-done | bytes 16416 | tf_op jit(solution)/shard_map/ppermute | solution.py:476
  25.2 0.8 %collective-permute-done.10 = bf16[2,4,1024]{2,1,0:T(4,128)(2,1)S(1)} collective-permute-done((bf16[2,4,1024]{2,1,0:T(4,128)(2,1)S(1)}, bf16[2,4,1024]{2,1,0:T(4,128)(2,1)S(1)}, u32[]{:S(2)}, u32[]{:S(2)}) %collective-permute-start.10) | collective-permute-done | bytes 16416 | tf_op jit(solution)/shard_map/ppermute | solution.py:476
  26.0 0.2 collective-permute-done.11
  26.2 0.6 %add_convert_fusion = bf16[2,4,1024]{2,1,0:T(4,128)(2,1)} fusion(bf16[2,4,1024]{2,1,0:T(4,128)(2,1)S(1)} %collective-permute-done.12, bf16[2,4,1024]{2,1,0:T(4,128)(2,1)S(1)} %collective-permute-done.11, bf16[2,4,1024]{2,1,0:T(4,128)(2,1)S(1)} %collective-permute-done.10, f32[2,4,1024]{2,1,0:T(4,128)S(1)} %get-tuple-element.24, ...), kind=kLoop, calls=%fused_computation | loop fusion | flops 73728 | bytes 114688 | tf_op jit(solution)/shard_map/convert_element_type | solution.py:515
  (2 shorter events, 0.0 us)
Async XLA Ops:
  0.0 9.3 %collective-permute-start.3 = (bf16[8,8,2,64,256]{4,3,2,1,0:T(8,128)(2,1)}, bf16[8,8,2,64,256]{4,3,2,1,0:T(8,128)(2,1)S(1)}, u32[]{:S(2)}, u32[]{:S(2)}) collective-permute-start(bf16[8,8,2,64,256]{4,3,2,1,0:T(8,128)(2,1)} %kv_in.1), channel_id=1, source_target_pairs={{0,4},{4,0},{8,12},{12,8},{16,20},{20,16},{24,28},{28,24},{1,5},{5... | collective-permute-start | bytes 12582920 | tf_op jit(solution)/shard_map/ppermute | solution.py:481
  0.5 5.7 %collective-permute-start.2 = (bf16[1,4,2048]{2,1,0:T(4,128)(2,1)}, bf16[1,4,2048]{2,1,0:T(4,128)(2,1)S(1)}, u32[]{:S(2)}, u32[]{:S(2)}) collective-permute-start(bf16[1,4,2048]{2,1,0:T(4,128)(2,1)} %bitcast.2), channel_id=1, source_target_pairs={{0,24},{4,28},{8,16},{12,20},{16,8},{20,12},{24,0},{28,4},{1,25},{... | collective-permute-start | bytes 49160 | tf_op jit(solution)/shard_map/ppermute | solution.py:481
  3.9 3.9 %collective-permute-start.1 = (bf16[1,4,2048]{2,1,0:T(4,128)(2,1)}, bf16[1,4,2048]{2,1,0:T(4,128)(2,1)S(1)}, u32[]{:S(2)}, u32[]{:S(2)}) collective-permute-start(bf16[1,4,2048]{2,1,0:T(4,128)(2,1)} %bitcast.3), channel_id=1, source_target_pairs={{0,16},{4,20},{8,24},{12,28},{16,0},{20,4},{24,8},{28,12},{1,17},{... | collective-permute-start | bytes 49160 | tf_op jit(solution)/shard_map/ppermute | solution.py:481
  4.4 3.9 %collective-permute-start = (bf16[1,4,2048]{2,1,0:T(4,128)(2,1)}, bf16[1,4,2048]{2,1,0:T(4,128)(2,1)S(1)}, u32[]{:S(2)}, u32[]{:S(2)}) collective-permute-start(bf16[1,4,2048]{2,1,0:T(4,128)(2,1)} %bitcast.4), channel_id=1, source_target_pairs={{0,8},{4,12},{8,0},{12,4},{16,24},{20,28},{24,16},{28,20},{1,9},{5... | collective-permute-start | bytes 49160 | tf_op jit(solution)/shard_map/ppermute | solution.py:481
  10.4 5.6 %collective-permute-start.7 = (bf16[272,128]{1,0:T(8,128)(2,1)S(1)}, bf16[272,128]{1,0:T(8,128)(2,1)S(1)}, u32[]{:S(2)}, u32[]{:S(2)}) collective-permute-start(bf16[272,128]{1,0:T(8,128)(2,1)S(1)} %shard_map.57._), channel_id=1, source_target_pairs={{0,28},{4,24},{8,20},{12,16},{16,12},{20,8},{24,4},{28,0},{1,29},{... | collective-permute-start | bytes 208904 | tf_op jit(solution)/shard_map/ppermute | solution.py:481
  12.2 4.5 %collective-permute-start.6 = (bf16[272,128]{1,0:T(8,128)(2,1)S(1)}, bf16[272,128]{1,0:T(8,128)(2,1)S(1)}, u32[]{:S(2)}, u32[]{:S(2)}) collective-permute-start(bf16[272,128]{1,0:T(8,128)(2,1)S(1)} %shard_map.57._), channel_id=1, source_target_pairs={{0,20},{4,16},{8,28},{12,24},{16,4},{20,0},{24,12},{28,8},{1,21},{... | collective-permute-start | bytes 208904 | tf_op jit(solution)/shard_map/ppermute | solution.py:481
  12.7 4.4 %collective-permute-start.5 = (bf16[272,128]{1,0:T(8,128)(2,1)S(1)}, bf16[272,128]{1,0:T(8,128)(2,1)S(1)}, u32[]{:S(2)}, u32[]{:S(2)}) collective-permute-start(bf16[272,128]{1,0:T(8,128)(2,1)S(1)} %shard_map.57._), channel_id=1, source_target_pairs={{0,12},{4,8},{8,4},{12,0},{16,28},{20,24},{24,20},{28,16},{1,13},{... | collective-permute-start | bytes 208904 | tf_op jit(solution)/shard_map/ppermute | solution.py:481
  13.2 3.8 %collective-permute-start.4 = (bf16[272,128]{1,0:T(8,128)(2,1)S(1)}, bf16[272,128]{1,0:T(8,128)(2,1)S(1)}, u32[]{:S(2)}, u32[]{:S(2)}) collective-permute-start(bf16[272,128]{1,0:T(8,128)(2,1)S(1)} %shard_map.57._), channel_id=1, source_target_pairs={{0,4},{4,0},{8,12},{12,8},{16,20},{20,16},{24,28},{28,24},{1,5},{5... | collective-permute-start | bytes 208904 | tf_op jit(solution)/shard_map/ppermute | solution.py:481
  17.4 1.3 %collective-permute-start.8 = (bf16[4,4,2048]{2,1,0:T(4,128)(2,1)S(1)}, bf16[4,4,2048]{2,1,0:T(4,128)(2,1)S(1)}, u32[]{:S(2)}, u32[]{:S(2)}) collective-permute-start(bf16[4,4,2048]{2,1,0:T(4,128)(2,1)S(1)} %shard_map.59.att_ref), channel_id=1, source_target_pairs={{0,4},{4,0},{8,12},{12,8},{16,20},{20,16},{24,28},{28,24},{1,5},{5... | collective-permute-start | bytes 196616 | tf_op jit(solution)/shard_map/ppermute | solution.py:481
  19.6 5.6 %collective-permute-start.9 = (bf16[2,4,1024]{2,1,0:T(4,128)(2,1)S(1)}, bf16[2,4,1024]{2,1,0:T(4,128)(2,1)S(1)}, u32[]{:S(2)}, u32[]{:S(2)}) collective-permute-start(bf16[2,4,1024]{2,1,0:T(4,128)(2,1)S(1)} %get-tuple-element.25), channel_id=1, source_target_pairs={{0,1},{1,5},{2,3},{3,0},{4,6},{5,7},{6,2},{7,4},{8,9},{9,13},{10,1... | collective-permute-start | bytes 49160 | tf_op jit(solution)/shard_map/ppermute | solution.py:476
  21.3 4.6 %collective-permute-start.10 = (bf16[2,4,1024]{2,1,0:T(4,128)(2,1)S(1)}, bf16[2,4,1024]{2,1,0:T(4,128)(2,1)S(1)}, u32[]{:S(2)}, u32[]{:S(2)}) collective-permute-start(bf16[2,4,1024]{2,1,0:T(4,128)(2,1)S(1)} %get-tuple-element.26), channel_id=1, source_target_pairs={{0,4},{1,2},{2,0},{3,1},{4,5},{5,6},{6,7},{7,3},{8,12},{9,10},{10,... | collective-permute-start | bytes 49160 | tf_op jit(solution)/shard_map/ppermute | solution.py:476
  22.2 4.0 %collective-permute-start.11 = (bf16[2,4,1024]{2,1,0:T(4,128)(2,1)S(1)}, bf16[2,4,1024]{2,1,0:T(4,128)(2,1)S(1)}, u32[]{:S(2)}, u32[]{:S(2)}) collective-permute-start(bf16[2,4,1024]{2,1,0:T(4,128)(2,1)S(1)} %get-tuple-element.27), channel_id=1, source_target_pairs={{0,3},{1,0},{2,6},{3,2},{4,7},{5,1},{6,4},{7,5},{8,11},{9,8},{10,1... | collective-permute-start | bytes 49160 | tf_op jit(solution)/shard_map/ppermute | solution.py:476
  23.9 2.4 %collective-permute-start.12 = (bf16[2,4,1024]{2,1,0:T(4,128)(2,1)S(1)}, bf16[2,4,1024]{2,1,0:T(4,128)(2,1)S(1)}, u32[]{:S(2)}, u32[]{:S(2)}) collective-permute-start(bf16[2,4,1024]{2,1,0:T(4,128)(2,1)S(1)} %get-tuple-element.28), channel_id=1, source_target_pairs={{0,2},{1,3},{2,1},{3,7},{4,0},{5,4},{6,5},{7,6},{8,10},{9,11},{10,... | collective-permute-start | bytes 49160 | tf_op jit(solution)/shard_map/ppermute | solution.py:476

commit v2 on v1

--- a/solution.py
+++ b/solution.py
@@ -286,16 +286,24 @@
     )(bits, *state, other_kv)
 
 
-def last_merge_kernel(rows, steps, *refs):
+def last_merge_kernel(rows, steps, chips, *refs):
     *part_refs, _, out_ref = refs
     m = len(part_refs)
     stats = [ref[m * rows :, :].astype(jnp.float32) for ref in part_refs]
+    core = lax.axis_index("ctx") % 2
+
+    def stat_of(k, slot):
+        return stats[k][3 * slot : 3 * slot + 1] + stats[k][3 * slot + 1 : 3 * slot + 2] + (
+            stats[k][3 * slot + 2 : 3 * slot + 3]
+        )
+
     factors = []
     for i in range(m):
         logs = []
-        for j in range(m):
-            k = 3 * (i ^ j)
-            logs.append(stats[j][k : k + 1] + stats[j][k + 1 : k + 2] + stats[j][k + 2 : k + 3])
+        for k in range(m):
+            even, odd = i ^ chips[0][k], i ^ chips[1][k]
+            log = stat_of(k, even)
+            logs.append(log if even == odd else jnp.where(core == 0, log, stat_of(k, odd)))
         top = functools.reduce(jnp.maximum, logs)
         some = [jnp.exp(x - top) for x in logs]
         total = functools.reduce(jnp.add, some)
@@ -303,18 +311,21 @@
     columns = rows_to_columns(factors, rows)
     for i in range(m):
         joined = jnp.zeros((rows, HD), jnp.float32)
-        for j, ref in enumerate(part_refs):
-            span = slice((i ^ j) * rows, ((i ^ j) + 1) * rows)
-            joined = joined + columns[i * m + j] * ref[span, :].astype(jnp.float32)
+        for k, ref in enumerate(part_refs):
+            even, odd = i ^ chips[0][k], i ^ chips[1][k]
+            first = even * rows
+            if even != odd:
+                first = pl.multiple_of(jnp.where(core == 0, even, odd) * rows, rows)
+            joined = joined + columns[i * m + k] * ref[pl.ds(first, rows), :].astype(jnp.float32)
         for j in range(rows // steps):
             piece = joined[j * steps : (j + 1) * steps]
             out_ref[i, :, j * HD : (j + 1) * HD] = piece.astype(jnp.bfloat16)
 
 
-def last_merge(parts, weight, rows, steps):
+def last_merge(parts, weight, rows, steps, chips):
     m = len(parts)
     return pl.pallas_call(
-        functools.partial(last_merge_kernel, rows, steps),
+        functools.partial(last_merge_kernel, rows, steps, chips),
         out_shape=jax.ShapeDtypeStruct((m, steps, rows // steps * HD), jnp.bfloat16),
         in_specs=[VMEM] * m + [ANY],
         out_specs=VMEM,
@@ -486,7 +497,14 @@
 
 
 def swap_other_cores(x, n):
-    return [swap(x, "ctx", r) for r in range(1, n, 2)]
+    sends = [list(range(1, n, 2))] * 2
+    if n == 8:
+        sends = [[1, 3, 5, 7], [1, 5, 3, 7]]
+    got = []
+    for even, odd in zip(*sends):
+        pairs = [(i, i ^ (odd if i % 2 else even)) for i in range(n)]
+        got.append(lax.ppermute(x, "ctx", pairs))
+    return got, [[r // 2 for r in sends[1]], [r // 2 for r in sends[0]]]
 
 
 def local(queries, kv_cache, new_kv, selected, out_weight):
@@ -503,9 +521,9 @@
     own_q, own_kv, bits, new_pairs = own_side(first_q, kv_cache, selected, new_pairs)
     all_q = [own_q] + far_q
     sent = partials(bits, new_pairs, own_kv, other_kv, all_q, rows, heads)
-    parts = swap_other_cores(sent, n)
+    parts, chips = swap_other_cores(sent, n)
     weight = load_weight(out_weight, sent)
-    odd_att = last_merge(parts, weight, rows, steps)
+    odd_att = last_merge(parts, weight, rows, steps, chips)
     even_att = swap(odd_att, "ctx", 1)
     plan = head_plan(n_head)
     half = project_half(odd_att, weight)

time: 27.3 us -> 27.4 us (level)
  waiting for transfers between devices: 5.45 us -> 5 us
  starting transfers between devices: 12.8 us -> 13.2 us
    ppermute x0 -> x4, starting transfers between devices: none -> 3.9 us  [swap_other_cores(): got.append(lax.ppermute(x, 'ctx', pairs))]
    ppermute x9 -> x5, starting transfers between devices: 8.1 us -> 4.72 us  [swap(): return lax.ppermute(x, axis, [(i, i ^ r) for i in range(size)])]
    ppermute x9 -> x5, waiting for transfers between devices: 3.51 us -> 2.5 us  [swap(): return lax.ppermute(x, axis, [(i, i ^ r) for i in range(size)])]
    ppermute x0 -> x4, waiting for transfers between devices: none -> 0.56 us  [swap_other_cores(): got.append(lax.ppermute(x, 'ctx', pairs))]
where the time goes in v2:
time: 27.4 us; the launch traced here: 26.9 us
  starting transfers between devices  13.2 us (48%)
  Pallas kernels  7.91 us (29%)
  waiting for transfers between devices  5 us (18%)
  other arithmetic  0.63 us (2%)
    ppermute x5, starting transfers between devices, swap(): return lax.ppermute(x, axis, [(i, i ^ r) for i in range(size)])  4.72 us
    ppermute x4, starting transfers between devices, send_by(): return lax.ppermute(x, ('ctx', 'head'), pairs)  4.63 us
    ppermute x4, starting transfers between devices, swap_other_cores(): got.append(lax.ppermute(x, 'ctx', pairs))  3.9 us
    ppermute x5, waiting for transfers between devices, swap(): return lax.ppermute(x, axis, [(i, i ^ r) for i in range(size)])  2.5 us
    pallas_call x1, Pallas kernels, load_weight(): pl.pallas_call(load_kernel, out_shape=jax.ShapeDtypeStruct(out_weight.sha...  2.2 us
    ppermute x4, waiting for transfers between devices, send_by(): return lax.ppermute(x, ('ctx', 'head'), pairs)  1.95 us
    pallas_call x1, Pallas kernels, own_side(): pl.pallas_call(own_kernel, out_shape=[jax.ShapeDtypeStruct(queries.shape,...  1.63 us
    pallas_call x1, Pallas kernels, partials(): pl.pallas_call(functools.partial(second_kernel, steps, heads), out_shape=...  1.12 us
  transfers between devices with their start and end apart: 13, of which 8 were waited for; matrix products, arithmetic and copies ran while one was open for 0% of the time, Pallas kernels for 21%

profile of v2, /device:TPU:0, one launch (start us, length us, event | category | flops | bytes accessed | tf_op | source)
XLA Modules:
  0.0 26.9 jit_solution(205321596278723828)
XLA Ops:
  0.0 0.5 %collective-permute-start.3 = (bf16[8,8,2,64,256]{4,3,2,1,0:T(8,128)(2,1)}, bf16[8,8,2,64,256]{4,3,2,1,0:T(8,128)(2,1)S(1)}, u32[]{:S(2)}, u32[]{:S(2)}) collective-permute-start(bf16[8,8,2,64,256]{4,3,2,1,0:T(8,128)(2,1)} %kv_in.1), channel_id=1, source_target_pairs={{0,4},{4,0},{8,12},{12,8},{16,20},{20,16},{24,28},{28,24},{1,5},{5... | collective-permute-start | bytes 12582920 | tf_op jit(solution)/shard_map/ppermute | solution.py:492
  0.5 3.4 %collective-permute-start.2 = (bf16[1,4,2048]{2,1,0:T(4,128)(2,1)}, bf16[1,4,2048]{2,1,0:T(4,128)(2,1)S(1)}, u32[]{:S(2)}, u32[]{:S(2)}) collective-permute-start(bf16[1,4,2048]{2,1,0:T(4,128)(2,1)} %bitcast.2), channel_id=1, source_target_pairs={{0,24},{4,28},{8,16},{12,20},{16,8},{20,12},{24,0},{28,4},{1,25},{... | collective-permute-start | bytes 49160 | tf_op jit(solution)/shard_map/ppermute | solution.py:492
  3.9 0.5 %collective-permute-start.1 = (bf16[1,4,2048]{2,1,0:T(4,128)(2,1)}, bf16[1,4,2048]{2,1,0:T(4,128)(2,1)S(1)}, u32[]{:S(2)}, u32[]{:S(2)}) collective-permute-start(bf16[1,4,2048]{2,1,0:T(4,128)(2,1)} %bitcast.3), channel_id=1, source_target_pairs={{0,16},{4,20},{8,24},{12,28},{16,0},{20,4},{24,8},{28,12},{1,17},{... | collective-permute-start | bytes 49160 | tf_op jit(solution)/shard_map/ppermute | solution.py:492
  4.4 0.1 collective-permute-start
  4.5 1.6 %shard_map.55 = (bf16[1,4,2048]{2,1,0:T(4,128)(2,1)S(1)}, bf16[4,8,2,64,256]{4,3,2,1,0:T(8,128)(2,1)S(1)}, s32[2,4,2,8,128]{4,3,2,1,0:T(8,128)S(1)}, bf16[2,16,256]{2,1,0:T(8,128)(2,1)S(1)}) custom-call(bf16[1,4,2048]{2,1,0:T(4,128)(2,1)} %bitcast.5, bf16[8,8,2,64,256]{4,3,2,1,0:T(8,128)(2,1)} %kv_in.1, s32[4,8,2,8]{3,2,1,0:T(2,128)} %selected_in.1, ...), custom_call_target="tpu_custom_call" | custom-call | flops 1048576 | bytes 4194304 | tf_op jit(solution)/shard_map/pallas_call | solution.py:132
  6.2 0.0 collective-permute-done.2.refs_3_
  6.2 1.7 %collective-permute-done.1.refs_2_ = bf16[1,4,2048]{2,1,0:T(4,128)(2,1)S(1)} collective-permute-done((bf16[1,4,2048]{2,1,0:T(4,128)(2,1)}, bf16[1,4,2048]{2,1,0:T(4,128)(2,1)S(1)}, u32[]{:S(2)}, u32[]{:S(2)}) %collective-permute-start.1) | collective-permute-done | bytes 16416 | tf_op jit(solution)/shard_map/ppermute | solution.py:492
  7.8 0.5 %collective-permute-done.refs_1_ = bf16[1,4,2048]{2,1,0:T(4,128)(2,1)S(1)} collective-permute-done((bf16[1,4,2048]{2,1,0:T(4,128)(2,1)}, bf16[1,4,2048]{2,1,0:T(4,128)(2,1)S(1)}, u32[]{:S(2)}, u32[]{:S(2)}) %collective-permute-start) | collective-permute-done | bytes 16416 | tf_op jit(solution)/shard_map/ppermute | solution.py:492
  8.4 0.9 %shard_map.56 = (bf16[4,64,256]{2,1,0:T(8,128)(2,1)S(1)}, f32[4,64,128]{2,1,0:T(8,128)S(1)}, f32[4,64,128]{2,1,0:T(8,128)S(1)}) custom-call(s32[2,4,2,8,128]{4,3,2,1,0:T(8,128)S(1)} %get-tuple-element.17.bits_ref, bf16[2,16,256]{2,1,0:T(8,128)(2,1)S(1)} %get-tuple-element.18.new_ref, bf16[4,8,2,64,256]{4,3,2,1,0:T(8,128)(2,1)S(1)} %get-tuple-element.19.own_ref, ...), custom_call_target="tpu_custom_call" | custom-call | flops 134217728 | bytes 1048576 | tf_op jit(solution)/shard_map/pallas_call | solution.py:268
  9.3 0.0 collective-permute-done.3.other_ref
  9.3 1.1 %shard_map.57._ = bf16[272,128]{1,0:T(8,128)(2,1)S(1)} custom-call(s32[2,4,2,8,128]{4,3,2,1,0:T(8,128)S(1)} %get-tuple-element.17.bits_ref, bf16[4,64,256]{2,1,0:T(8,128)(2,1)S(1)} %get-tuple-element.21.spread_ref, f32[4,64,128]{2,1,0:T(8,128)S(1)} %get-tuple-element.22.sum_ref, f32[4,64,128]{2,1,0:T(8,128)S(1)} %get-tuple-element.23.stat_ref, ...), custom_call_target="tpu_custom_call" | custom-call | flops 134217728 | bytes 1048576 | tf_op jit(solution)/shard_map/pallas_call | solution.py:280
  10.4 1.8 %collective-permute-start.7 = (bf16[272,128]{1,0:T(8,128)(2,1)S(1)}, bf16[272,128]{1,0:T(8,128)(2,1)S(1)}, u32[]{:S(2)}, u32[]{:S(2)}) collective-permute-start(bf16[272,128]{1,0:T(8,128)(2,1)S(1)} %shard_map.57._), channel_id=1, source_target_pairs={{0,28},{4,24},{8,20},{12,16},{16,12},{20,8},{24,4},{28,0},{1,29},{... | collective-permute-start | bytes 208904 | tf_op jit(solution)/shard_map/ppermute | solution.py:506
  12.2 0.5 %collective-permute-start.6 = (bf16[272,128]{1,0:T(8,128)(2,1)S(1)}, bf16[272,128]{1,0:T(8,128)(2,1)S(1)}, u32[]{:S(2)}, u32[]{:S(2)}) collective-permute-start(bf16[272,128]{1,0:T(8,128)(2,1)S(1)} %shard_map.57._), channel_id=1, source_target_pairs={{0,20},{4,8},{8,28},{12,0},{16,4},{20,24},{24,12},{28,16},{1,21},{... | collective-permute-start | bytes 208904 | tf_op jit(solution)/shard_map/ppermute | solution.py:506
  12.7 1.3 %collective-permute-start.5 = (bf16[272,128]{1,0:T(8,128)(2,1)S(1)}, bf16[272,128]{1,0:T(8,128)(2,1)S(1)}, u32[]{:S(2)}, u32[]{:S(2)}) collective-permute-start(bf16[272,128]{1,0:T(8,128)(2,1)S(1)} %shard_map.57._), channel_id=1, source_target_pairs={{0,12},{4,16},{8,4},{12,24},{16,28},{20,0},{24,20},{28,8},{1,13},{... | collective-permute-start | bytes 208904 | tf_op jit(solution)/shard_map/ppermute | solution.py:506
  13.9 0.4 %collective-permute-start.4 = (bf16[272,128]{1,0:T(8,128)(2,1)S(1)}, bf16[272,128]{1,0:T(8,128)(2,1)S(1)}, u32[]{:S(2)}, u32[]{:S(2)}) collective-permute-start(bf16[272,128]{1,0:T(8,128)(2,1)S(1)} %shard_map.57._), channel_id=1, source_target_pairs={{0,4},{4,0},{8,12},{12,8},{16,20},{20,16},{24,28},{28,24},{1,5},{5... | collective-permute-start | bytes 208904 | tf_op jit(solution)/shard_map/ppermute | solution.py:506
  14.3 2.2 %shard_map.58.refs_4_.weight_ref = bf16[2048,1024]{1,0:T(8,128)(2,1)S(1)} custom-call(bf16[2048,1024]{1,0:T(8,128)(2,1)} %weight_ref.1, bf16[272,128]{1,0:T(8,128)(2,1)S(1)} %shard_map.57._), custom_call_target="tpu_custom_call" | custom-call | bytes 8388608 | tf_op jit(solution)/shard_map/pallas_call | solution.py:352
  16.5 0.0 collective-permute-done.7.refs_3_
  16.5 0.4 %collective-permute-done.6.refs_2_ = bf16[272,128]{1,0:T(8,128)(2,1)S(1)} collective-permute-done((bf16[272,128]{1,0:T(8,128)(2,1)S(1)}, bf16[272,128]{1,0:T(8,128)(2,1)S(1)}, u32[]{:S(2)}, u32[]{:S(2)}) %collective-permute-start.6) | collective-permute-done | bytes 69664 | tf_op jit(solution)/shard_map/ppermute | solution.py:506
  16.9 0.2 collective-permute-done.5.refs_1_
  17.1 0.4 %shard_map.59.att_ref = bf16[4,4,2048]{2,1,0:T(4,128)(2,1)S(1)} custom-call(bf16[272,128]{1,0:T(8,128)(2,1)S(1)} %collective-permute-done.4.refs_0_, bf16[272,128]{1,0:T(8,128)(2,1)S(1)} %collective-permute-done.5.refs_1_, bf16[272,128]{1,0:T(8,128)(2,1)S(1)} %collective-permute-done.6.refs_2_, bf16[272,128]{1,0:T(8,128)(2,1)S(1)} %collective-permute-done.7.refs_3_, ...), custom_call_target="tpu_custom_call" | custom-call | flops 262144 | bytes 262144 | tf_op jit(solution)/shard_map/pallas_call | solution.py:327
  17.5 0.2 collective-permute-start.8
  17.7 0.8 %shard_map.60.half_ref = f32[4,8,1024]{2,1,0:T(8,128)S(1)} custom-call(bf16[4,4,2048]{2,1,0:T(4,128)(2,1)S(1)} %shard_map.59.att_ref, bf16[2048,1024]{1,0:T(8,128)(2,1)S(1)} %shard_map.58.refs_4_.weight_ref), custom_call_target="tpu_custom_call" | custom-call | flops 134217728 | bytes 4194304 | tf_op jit(solution)/shard_map/pallas_call | solution.py:419
  18.5 0.3 %collective-permute-done.8.att_ref = bf16[4,4,2048]{2,1,0:T(4,128)(2,1)S(1)} collective-permute-done((bf16[4,4,2048]{2,1,0:T(4,128)(2,1)S(1)}, bf16[4,4,2048]{2,1,0:T(4,128)(2,1)S(1)}, u32[]{:S(2)}, u32[]{:S(2)}) %collective-permute-start.8) | collective-permute-done | bytes 65568 | tf_op jit(solution)/shard_map/ppermute | solution.py:492
  18.8 0.9 %shard_map.61 = (f32[2,4,1024]{2,1,0:T(4,128)S(1)}, bf16[2,4,1024]{2,1,0:T(4,128)(2,1)S(1)}, bf16[2,4,1024]{2,1,0:T(4,128)(2,1)S(1)}, bf16[2,4,1024]{2,1,0:T(4,128)(2,1)S(1)}, bf16[2,4,1024]{2,1,0:T(4,128)(2,1)S(1)}) custom-call(bf16[4,4,2048]{2,1,0:T(4,128)(2,1)S(1)} %collective-permute-done.8.att_ref, f32[4,8,1024]{2,1,0:T(8,128)S(1)} %shard_map.60.half_ref, ...), custom_call_target="tpu_custom_call" | custom-call | flops 134217728 | bytes 4194304 | tf_op jit(solution)/shard_map/pallas_call | solution.py:437
  19.6 1.7 %collective-permute-start.9 = (bf16[2,4,1024]{2,1,0:T(4,128)(2,1)S(1)}, bf16[2,4,1024]{2,1,0:T(4,128)(2,1)S(1)}, u32[]{:S(2)}, u32[]{:S(2)}) collective-permute-start(bf16[2,4,1024]{2,1,0:T(4,128)(2,1)S(1)} %get-tuple-element.25), channel_id=1, source_target_pairs={{0,1},{1,5},{2,3},{3,0},{4,6},{5,7},{6,2},{7,4},{8,9},{9,13},{10,1... | collective-permute-start | bytes 49160 | tf_op jit(solution)/shard_map/ppermute | solution.py:487
  21.4 0.9 %collective-permute-start.10 = (bf16[2,4,1024]{2,1,0:T(4,128)(2,1)S(1)}, bf16[2,4,1024]{2,1,0:T(4,128)(2,1)S(1)}, u32[]{:S(2)}, u32[]{:S(2)}) collective-permute-start(bf16[2,4,1024]{2,1,0:T(4,128)(2,1)S(1)} %get-tuple-element.26), channel_id=1, source_target_pairs={{0,4},{1,2},{2,0},{3,1},{4,5},{5,6},{6,7},{7,3},{8,12},{9,10},{10,... | collective-permute-start | bytes 49160 | tf_op jit(solution)/shard_map/ppermute | solution.py:487
  22.2 1.6 %collective-permute-start.11 = (bf16[2,4,1024]{2,1,0:T(4,128)(2,1)S(1)}, bf16[2,4,1024]{2,1,0:T(4,128)(2,1)S(1)}, u32[]{:S(2)}, u32[]{:S(2)}) collective-permute-start(bf16[2,4,1024]{2,1,0:T(4,128)(2,1)S(1)} %get-tuple-element.27), channel_id=1, source_target_pairs={{0,3},{1,0},{2,6},{3,2},{4,7},{5,1},{6,4},{7,5},{8,11},{9,8},{10,1... | collective-permute-start | bytes 49160 | tf_op jit(solution)/shard_map/ppermute | solution.py:487
  23.9 0.4 %collective-permute-start.12 = (bf16[2,4,1024]{2,1,0:T(4,128)(2,1)S(1)}, bf16[2,4,1024]{2,1,0:T(4,128)(2,1)S(1)}, u32[]{:S(2)}, u32[]{:S(2)}) collective-permute-start(bf16[2,4,1024]{2,1,0:T(4,128)(2,1)S(1)} %get-tuple-element.28), channel_id=1, source_target_pairs={{0,2},{1,3},{2,1},{3,7},{4,0},{5,4},{6,5},{7,6},{8,10},{9,11},{10,... | collective-permute-start | bytes 49160 | tf_op jit(solution)/shard_map/ppermute | solution.py:487
  24.3 1.0 %collective-permute-done.9 = bf16[2,4,1024]{2,1,0:T(4,128)(2,1)S(1)} collective-permute-done((bf16[2,4,1024]{2,1,0:T(4,128)(2,1)S(1)}, bf16[2,4,1024]{2,1,0:T(4,128)(2,1)S(1)}, u32[]{:S(2)}, u32[]{:S(2)}) %collective-permute-start.9) | collective-permute-done | bytes 16416 | tf_op jit(solution)/shard_map/ppermute | solution.py:487
  25.2 0.7 %collective-permute-done.10 = bf16[2,4,1024]{2,1,0:T(4,128)(2,1)S(1)} collective-permute-done((bf16[2,4,1024]{2,1,0:T(4,128)(2,1)S(1)}, bf16[2,4,1024]{2,1,0:T(4,128)(2,1)S(1)}, u32[]{:S(2)}, u32[]{:S(2)}) %collective-permute-start.10) | collective-permute-done | bytes 16416 | tf_op jit(solution)/shard_map/ppermute | solution.py:487
  26.0 0.2 collective-permute-done.11
  26.2 0.6 %add_convert_fusion = bf16[2,4,1024]{2,1,0:T(4,128)(2,1)} fusion(bf16[2,4,1024]{2,1,0:T(4,128)(2,1)S(1)} %collective-permute-done.12, bf16[2,4,1024]{2,1,0:T(4,128)(2,1)S(1)} %collective-permute-done.11, bf16[2,4,1024]{2,1,0:T(4,128)(2,1)S(1)} %collective-permute-done.10, f32[2,4,1024]{2,1,0:T(4,128)S(1)} %get-tuple-element.24, ...), kind=kLoop, calls=%fused_computation | loop fusion | flops 73728 | bytes 114688 | tf_op jit(solution)/shard_map/convert_element_type | solution.py:533
  (2 shorter events, 0.0 us)
Async XLA Ops:
  0.0 9.3 %collective-permute-start.3 = (bf16[8,8,2,64,256]{4,3,2,1,0:T(8,128)(2,1)}, bf16[8,8,2,64,256]{4,3,2,1,0:T(8,128)(2,1)S(1)}, u32[]{:S(2)}, u32[]{:S(2)}) collective-permute-start(bf16[8,8,2,64,256]{4,3,2,1,0:T(8,128)(2,1)} %kv_in.1), channel_id=1, source_target_pairs={{0,4},{4,0},{8,12},{12,8},{16,20},{20,16},{24,28},{28,24},{1,5},{5... | collective-permute-start | bytes 12582920 | tf_op jit(solution)/shard_map/ppermute | solution.py:492
  0.5 5.7 %collective-permute-start.2 = (bf16[1,4,2048]{2,1,0:T(4,128)(2,1)}, bf16[1,4,2048]{2,1,0:T(4,128)(2,1)S(1)}, u32[]{:S(2)}, u32[]{:S(2)}) collective-permute-start(bf16[1,4,2048]{2,1,0:T(4,128)(2,1)} %bitcast.2), channel_id=1, source_target_pairs={{0,24},{4,28},{8,16},{12,20},{16,8},{20,12},{24,0},{28,4},{1,25},{... | collective-permute-start | bytes 49160 | tf_op jit(solution)/shard_map/ppermute | solution.py:492
  3.9 3.9 %collective-permute-start.1 = (bf16[1,4,2048]{2,1,0:T(4,128)(2,1)}, bf16[1,4,2048]{2,1,0:T(4,128)(2,1)S(1)}, u32[]{:S(2)}, u32[]{:S(2)}) collective-permute-start(bf16[1,4,2048]{2,1,0:T(4,128)(2,1)} %bitcast.3), channel_id=1, source_target_pairs={{0,16},{4,20},{8,24},{12,28},{16,0},{20,4},{24,8},{28,12},{1,17},{... | collective-permute-start | bytes 49160 | tf_op jit(solution)/shard_map/ppermute | solution.py:492
  4.4 3.9 %collective-permute-start = (bf16[1,4,2048]{2,1,0:T(4,128)(2,1)}, bf16[1,4,2048]{2,1,0:T(4,128)(2,1)S(1)}, u32[]{:S(2)}, u32[]{:S(2)}) collective-permute-start(bf16[1,4,2048]{2,1,0:T(4,128)(2,1)} %bitcast.4), channel_id=1, source_target_pairs={{0,8},{4,12},{8,0},{12,4},{16,24},{20,28},{24,16},{28,20},{1,9},{5... | collective-permute-start | bytes 49160 | tf_op jit(solution)/shard_map/ppermute | solution.py:492
  10.4 6.1 %collective-permute-start.7 = (bf16[272,128]{1,0:T(8,128)(2,1)S(1)}, bf16[272,128]{1,0:T(8,128)(2,1)S(1)}, u32[]{:S(2)}, u32[]{:S(2)}) collective-permute-start(bf16[272,128]{1,0:T(8,128)(2,1)S(1)} %shard_map.57._), channel_id=1, source_target_pairs={{0,28},{4,24},{8,20},{12,16},{16,12},{20,8},{24,4},{28,0},{1,29},{... | collective-permute-start | bytes 208904 | tf_op jit(solution)/shard_map/ppermute | solution.py:506
  12.2 4.7 %collective-permute-start.6 = (bf16[272,128]{1,0:T(8,128)(2,1)S(1)}, bf16[272,128]{1,0:T(8,128)(2,1)S(1)}, u32[]{:S(2)}, u32[]{:S(2)}) collective-permute-start(bf16[272,128]{1,0:T(8,128)(2,1)S(1)} %shard_map.57._), channel_id=1, source_target_pairs={{0,20},{4,8},{8,28},{12,0},{16,4},{20,24},{24,12},{28,16},{1,21},{... | collective-permute-start | bytes 208904 | tf_op jit(solution)/shard_map/ppermute | solution.py:506
  12.7 4.4 %collective-permute-start.5 = (bf16[272,128]{1,0:T(8,128)(2,1)S(1)}, bf16[272,128]{1,0:T(8,128)(2,1)S(1)}, u32[]{:S(2)}, u32[]{:S(2)}) collective-permute-start(bf16[272,128]{1,0:T(8,128)(2,1)S(1)} %shard_map.57._), channel_id=1, source_target_pairs={{0,12},{4,16},{8,4},{12,24},{16,28},{20,0},{24,20},{28,8},{1,13},{... | collective-permute-start | bytes 208904 | tf_op jit(solution)/shard_map/ppermute | solution.py:506
  13.9 3.2 %collective-permute-start.4 = (bf16[272,128]{1,0:T(8,128)(2,1)S(1)}, bf16[272,128]{1,0:T(8,128)(2,1)S(1)}, u32[]{:S(2)}, u32[]{:S(2)}) collective-permute-start(bf16[272,128]{1,0:T(8,128)(2,1)S(1)} %shard_map.57._), channel_id=1, source_target_pairs={{0,4},{4,0},{8,12},{12,8},{16,20},{20,16},{24,28},{28,24},{1,5},{5... | collective-permute-start | bytes 208904 | tf_op jit(solution)/shard_map/ppermute | solution.py:506
  17.5 1.3 %collective-permute-start.8 = (bf16[4,4,2048]{2,1,0:T(4,128)(2,1)S(1)}, bf16[4,4,2048]{2,1,0:T(4,128)(2,1)S(1)}, u32[]{:S(2)}, u32[]{:S(2)}) collective-permute-start(bf16[4,4,2048]{2,1,0:T(4,128)(2,1)S(1)} %shard_map.59.att_ref), channel_id=1, source_target_pairs={{0,4},{4,0},{8,12},{12,8},{16,20},{20,16},{24,28},{28,24},{1,5},{5... | collective-permute-start | bytes 196616 | tf_op jit(solution)/shard_map/ppermute | solution.py:492
  19.6 5.6 %collective-permute-start.9 = (bf16[2,4,1024]{2,1,0:T(4,128)(2,1)S(1)}, bf16[2,4,1024]{2,1,0:T(4,128)(2,1)S(1)}, u32[]{:S(2)}, u32[]{:S(2)}) collective-permute-start(bf16[2,4,1024]{2,1,0:T(4,128)(2,1)S(1)} %get-tuple-element.25), channel_id=1, source_target_pairs={{0,1},{1,5},{2,3},{3,0},{4,6},{5,7},{6,2},{7,4},{8,9},{9,13},{10,1... | collective-permute-start | bytes 49160 | tf_op jit(solution)/shard_map/ppermute | solution.py:487
  21.4 4.6 %collective-permute-start.10 = (bf16[2,4,1024]{2,1,0:T(4,128)(2,1)S(1)}, bf16[2,4,1024]{2,1,0:T(4,128)(2,1)S(1)}, u32[]{:S(2)}, u32[]{:S(2)}) collective-permute-start(bf16[2,4,1024]{2,1,0:T(4,128)(2,1)S(1)} %get-tuple-element.26), channel_id=1, source_target_pairs={{0,4},{1,2},{2,0},{3,1},{4,5},{5,6},{6,7},{7,3},{8,12},{9,10},{10,... | collective-permute-start | bytes 49160 | tf_op jit(solution)/shard_map/ppermute | solution.py:487
  22.2 4.0 %collective-permute-start.11 = (bf16[2,4,1024]{2,1,0:T(4,128)(2,1)S(1)}, bf16[2,4,1024]{2,1,0:T(4,128)(2,1)S(1)}, u32[]{:S(2)}, u32[]{:S(2)}) collective-permute-start(bf16[2,4,1024]{2,1,0:T(4,128)(2,1)S(1)} %get-tuple-element.27), channel_id=1, source_target_pairs={{0,3},{1,0},{2,6},{3,2},{4,7},{5,1},{6,4},{7,5},{8,11},{9,8},{10,1... | collective-permute-start | bytes 49160 | tf_op jit(solution)/shard_map/ppermute | solution.py:487
  23.9 2.4 %collective-permute-start.12 = (bf16[2,4,1024]{2,1,0:T(4,128)(2,1)S(1)}, bf16[2,4,1024]{2,1,0:T(4,128)(2,1)S(1)}, u32[]{:S(2)}, u32[]{:S(2)}) collective-permute-start(bf16[2,4,1024]{2,1,0:T(4,128)(2,1)S(1)} %get-tuple-element.28), channel_id=1, source_target_pairs={{0,2},{1,3},{2,1},{3,7},{4,0},{5,4},{6,5},{7,6},{8,10},{9,11},{10,... | collective-permute-start | bytes 49160 | tf_op jit(solution)/shard_map/ppermute | solution.py:487

commit v3 on v1

--- a/solution.py
+++ b/solution.py
@@ -13,7 +13,8 @@
 PAGE = 64
 GROUPS = HQ // KVH
 STAT_ROWS = 16
-NEG = -1e30
+MASKED = -3e38
+FLOOR = -1.5e38
 WEIGHT_PIECES = 4
 VMEM_LIMIT = 24 * 1024 * 1024
 
@@ -57,33 +58,19 @@
     return -(-3 * slots // STAT_ROWS) * STAT_ROWS
 
 
-def columns_to_rows(columns):
+def stat_block(columns):
     rows = columns[0].shape[0]
     lane = lax.broadcasted_iota(jnp.int32, (rows, 128), 1)
     sheet = jnp.zeros((rows, 128), jnp.float32)
     for i, column in enumerate(columns):
         sheet = jnp.where(lane == i, column, sheet)
     sheet = jnp.concatenate([sheet, jnp.zeros((128 - rows, 128), jnp.float32)], axis=0)
-    turned = jnp.transpose(sheet)
-    return [turned[i : i + 1] for i in range(len(columns))]
-
-
-def rows_to_columns(listed, rows):
-    columns = []
-    for first in range(0, len(listed), 128):
-        some = listed[first : first + 128]
-        blank = [jnp.zeros((128 - len(some), 128), jnp.float32)] if len(some) < 128 else []
-        turned = jnp.transpose(jnp.concatenate(some + blank, axis=0))
-        columns += [turned[:rows, i : i + 1] for i in range(len(some))]
-    return columns
-
-
-def page_masks(bits_ref, seq, steps, page_bit):
-    masks = []
-    for h in range(bits_ref.shape[1]):
-        bits = jnp.concatenate([bits_ref[seq, h]] * (page_bit.shape[1] // 128), axis=1)
-        masks += [(page_bit & bits) != 0] * steps
-    return jnp.concatenate(masks, axis=0)
+    count = len(columns)
+    parts = list(three_parts(jnp.transpose(sheet)[:count]))
+    spare = stat_rows(count) - 3 * count
+    if spare:
+        parts.append(jnp.zeros((spare, 128), jnp.float32))
+    return jnp.concatenate(parts, axis=0).astype(jnp.bfloat16)
 
 
 def own_kernel(
@@ -163,15 +150,14 @@
     found = []
     for keys, values, allowed in pieces:
         scores = lax.dot_general(spread, keys, NT, preferred_element_type=jnp.float32)
-        found.append((allowed, jnp.where(allowed, scores * HD ** (-0.5), NEG), values))
+        found.append((jnp.where(allowed, scores * HD ** (-0.5), MASKED), values))
 
     def finish():
-        top = functools.reduce(
-            jnp.maximum, [jnp.max(scores, axis=1, keepdims=True) for _, scores, _ in found]
-        )
+        tops = [jnp.max(scores, axis=1, keepdims=True) for scores, _ in found]
+        top = jnp.maximum(functools.reduce(jnp.maximum, tops), FLOOR)
         total, weighted = 0.0, 0.0
-        for allowed, scores, values in found:
-            expo = jnp.where(allowed, jnp.exp(scores - top), 0.0)
+        for scores, values in found:
+            expo = jnp.exp(scores - top)
             total = total + jnp.sum(expo, axis=1, keepdims=True)
             weighted = weighted + jnp.dot(
                 expo.astype(jnp.bfloat16), values, preferred_element_type=jnp.float32
@@ -194,11 +180,11 @@
     for i in range(count):
         if i + ahead < count:
             begun.append(begin(i + ahead))
-        end(i, begun[i]())
+        end(i, begun[i])
 
 
 def first_kernel(heads, bits_ref, new_ref, own_ref, *refs):
-    *q_refs, spread_ref, sum_ref, stat_ref, turned = refs
+    *q_refs, spread_ref, sum_ref, top_ref, total_ref, turned = refs
     steps = q_refs[0].shape[1]
     rows = turned.shape[1]
 
@@ -212,16 +198,18 @@
             pieces.append((new_ref[0], new_ref[1], causal))
         return attend(spread, pieces)
 
-    def end(i, state):
-        top, total, weighted = state
-        lane = lax.broadcasted_iota(jnp.int32, (rows, 128), 1)
-        stat_ref[i] = jnp.where(lane == 0, top, total)
+    def end(i, finish):
+        top, total, weighted = finish()
+        top_ref[i] = jnp.broadcast_to(top, (rows, 128))
+        total_ref[i] = jnp.broadcast_to(total, (rows, 128))
         sum_ref[i] = own_heads(weighted, heads)
 
     staged(len(q_refs), 1, begin, end)
 
 
-def second_kernel(steps, heads, bits_ref, spread_ref, sum_ref, stat_ref, other_ref, out_ref):
+def second_kernel(
+    steps, heads, bits_ref, spread_ref, sum_ref, top_ref, total_ref, other_ref, out_ref
+):
     m, rows = spread_ref.shape[:2]
     me = lax.axis_index("ctx")
     columns = []
@@ -230,27 +218,22 @@
         pieces = [page_pieces(other_ref, me ^ (2 * i), bits_ref, 1, i, steps, heads)]
         return attend(spread_ref[i], pieces)
 
-    def end(i, state):
-        top, total, weighted = state
-        stats = stat_ref[i]
-        first_top, first_total = stats[:, 0:1], stats[:, 1:2]
+    def end(i, finish):
+        first_top, first_total = top_ref[i], total_ref[i]
+        top, total, weighted = finish()
+        top = jnp.broadcast_to(top, (rows, 128))
         both = jnp.maximum(top, first_top)
         factor, first_factor = jnp.exp(top - both), jnp.exp(first_top - both)
-        total = total * factor + first_total * first_factor
+        total = jnp.broadcast_to(total, (rows, 128)) * factor + first_total * first_factor
         total = jnp.where(total > 0.0, total, 1.0)
-        joined = own_heads(weighted, heads) * (factor / total)
-        joined = joined + sum_ref[i] * (first_factor / total)
+        share = 1.0 / total
+        joined = own_heads(weighted, heads) * (factor * share)
+        joined = joined + sum_ref[i] * (first_factor * share)
         out_ref[i * rows : (i + 1) * rows, :] = joined.astype(jnp.bfloat16)
         columns.append(both + jnp.log(total))
 
     staged(m, m if m <= 4 else 2, begin, end)
-    count = stat_rows(m)
-    stat_row = lax.broadcasted_iota(jnp.int32, (count, 128), 0)
-    block = jnp.zeros((count, 128), jnp.float32)
-    for i, row in enumerate(columns_to_rows(columns)):
-        for j, part in enumerate(three_parts(row)):
-            block = jnp.where(stat_row == 3 * i + j, part, block)
-    out_ref[m * rows :, :] = block.astype(jnp.bfloat16)
+    out_ref[m * rows :, :] = stat_block(columns)
 
 
 def partials(bits, new_pairs, own_kv, other_kv, queries, rows, heads):
@@ -271,16 +254,17 @@
             jax.ShapeDtypeStruct((m, rows, width), jnp.bfloat16),
             jax.ShapeDtypeStruct((m, rows, HD), jnp.float32),
             jax.ShapeDtypeStruct((m, rows, 128), jnp.float32),
+            jax.ShapeDtypeStruct((m, rows, 128), jnp.float32),
         ],
         in_specs=[VMEM] * (3 + m),
-        out_specs=[VMEM] * 3,
+        out_specs=[VMEM] * 4,
         scratch_shapes=[pltpu.VMEM((m, rows, HD), jnp.float32)],
         **options,
     )(bits, new_pairs, own_kv, *queries)
     return pl.pallas_call(
         functools.partial(second_kernel, steps, heads),
         out_shape=jax.ShapeDtypeStruct((m * rows + stat_rows(m), HD), jnp.bfloat16),
-        in_specs=[VMEM] * 5,
+        in_specs=[VMEM] * 6,
         out_specs=VMEM,
         **options,
     )(bits, *state, other_kv)
@@ -289,23 +273,43 @@
 def last_merge_kernel(rows, steps, *refs):
     *part_refs, _, out_ref = refs
     m = len(part_refs)
-    stats = [ref[m * rows :, :].astype(jnp.float32) for ref in part_refs]
-    factors = []
+    logs = []
+    for j, ref in enumerate(part_refs):
+        stats = ref[m * rows :, :].astype(jnp.float32)
+        log = stats[:m] + stats[m : 2 * m] + stats[2 * m : 3 * m]
+        if j:
+            log = jnp.concatenate([log[i ^ j : (i ^ j) + 1] for i in range(m)], axis=0)
+        logs.append(log)
+    top = functools.reduce(jnp.maximum, logs)
+    factors = [jnp.exp(log - top) for log in logs]
+    share = 1.0 / functools.reduce(jnp.add, factors)
+    lane = lax.broadcasted_iota(jnp.int32, (m, 128), 1) // rows
+    beside = 128 // rows
+    packed = []
+    for first in range(0, m, beside):
+        wide = jnp.zeros((m, 128), jnp.float32)
+        for p in range(min(beside, m - first)):
+            weight = factors[first + p] * share
+            if p:
+                weight = jnp.concatenate(
+                    [weight[:, 128 - p * rows :], weight[:, : 128 - p * rows]], axis=1
+                )
+            wide = jnp.where(lane == p, weight, wide)
+        packed.append(wide)
+    on_row = lax.broadcasted_iota(jnp.int32, (rows, 128), 0)
+    diagonal = lax.broadcasted_iota(jnp.int32, (rows, 128), 1) % rows == on_row
     for i in range(m):
-        logs = []
-        for j in range(m):
-            k = 3 * (i ^ j)
-            logs.append(stats[j][k : k + 1] + stats[j][k + 1 : k + 2] + stats[j][k + 2 : k + 3])
-        top = functools.reduce(jnp.maximum, logs)
-        some = [jnp.exp(x - top) for x in logs]
-        total = functools.reduce(jnp.add, some)
-        factors += [f / total for f in some]
-    columns = rows_to_columns(factors, rows)
-    for i in range(m):
-        joined = jnp.zeros((rows, HD), jnp.float32)
-        for j, ref in enumerate(part_refs):
-            span = slice((i ^ j) * rows, ((i ^ j) + 1) * rows)
-            joined = joined + columns[i * m + j] * ref[span, :].astype(jnp.float32)
+        weights = jnp.concatenate(
+            [jnp.where(diagonal, wide[i : i + 1], 0.0) for wide in packed], axis=1
+        )
+        parts = jnp.concatenate(
+            [ref[(i ^ j) * rows : ((i ^ j) + 1) * rows, :] for j, ref in enumerate(part_refs)],
+            axis=0,
+        )
+        high = weights.astype(jnp.bfloat16)
+        low = (weights - high.astype(jnp.float32)).astype(jnp.bfloat16)
+        joined = jnp.dot(high, parts, preferred_element_type=jnp.float32)
+        joined = joined + jnp.dot(low, parts, preferred_element_type=jnp.float32)
         for j in range(rows // steps):
             piece = joined[j * steps : (j + 1) * steps]
             out_ref[i, :, j * HD : (j + 1) * HD] = piece.astype(jnp.bfloat16)
@@ -354,7 +358,6 @@
 def project_rows(att_ref, weight_ref, lhs):
     count, _, width = lhs.shape
     steps = att_ref.shape[1]
-    lhs[...] = jnp.zeros_like(lhs)
     for i in range(count):
         lhs[i, :steps, :] = att_ref[i].astype(jnp.float32)
     left = lhs[...].reshape(count * 8, width).astype(jnp.bfloat16)

time: 27.3 us -> 26.9 us (0.985)
  Pallas kernels: 7.9 us -> 7.5 us
    pallas_call x1, Pallas kernels: 1.12 us -> 0.76 us  [partials(): pl.pallas_call(functools.partial(second_kernel, steps, heads), out_shape=...]
where the time goes in v3:
time: 26.9 us; the launch traced here: 26.4 us
  starting transfers between devices  12.8 us (48%)
  Pallas kernels  7.5 us (28%)
  waiting for transfers between devices  5.45 us (20%)
  other arithmetic  0.63 us (2%)
    ppermute x9, starting transfers between devices, swap(): return lax.ppermute(x, axis, [(i, i ^ r) for i in range(size)])  8.09 us
    ppermute x4, starting transfers between devices, send_by(): return lax.ppermute(x, ('ctx', 'head'), pairs)  4.68 us
    ppermute x9, waiting for transfers between devices, swap(): return lax.ppermute(x, axis, [(i, i ^ r) for i in range(size)])  3.51 us
    pallas_call x1, Pallas kernels, load_weight(): pl.pallas_call(load_kernel, out_shape=jax.ShapeDtypeStruct(out_weight.sha...  2.2 us
    ppermute x4, waiting for transfers between devices, send_by(): return lax.ppermute(x, ('ctx', 'head'), pairs)  1.95 us
    pallas_call x1, Pallas kernels, own_side(): pl.pallas_call(own_kernel, out_shape=[jax.ShapeDtypeStruct(queries.shape,...  1.63 us
    pallas_call x1, Pallas kernels, partials(): pl.pallas_call(functools.partial(first_kernel, heads), out_shape=[jax.Sha...  0.91 us
    pallas_call x1, Pallas kernels, project(): pl.pallas_call(functools.partial(project_kernel, n_head, targets), out_sh...  0.86 us
  transfers between devices with their start and end apart: 13, of which 8 were waited for; matrix products, arithmetic and copies ran while one was open for 0% of the time, Pallas kernels for 21%

profile of v3, /device:TPU:0, one launch (start us, length us, event | category | flops | bytes accessed | tf_op | source)
XLA Modules:
  0.0 26.4 jit_solution(9297795360919261299)
XLA Ops:
  0.0 0.5 %collective-permute-start.3 = (bf16[8,8,2,64,256]{4,3,2,1,0:T(8,128)(2,1)}, bf16[8,8,2,64,256]{4,3,2,1,0:T(8,128)(2,1)S(1)}, u32[]{:S(2)}, u32[]{:S(2)}) collective-permute-start(bf16[8,8,2,64,256]{4,3,2,1,0:T(8,128)(2,1)} %kv_in.1), channel_id=1, source_target_pairs={{0,4},{4,0},{8,12},{12,8},{16,20},{20,16},{24,28},{28,24},{1,5},{5... | collective-permute-start | bytes 12582920 | tf_op jit(solution)/shard_map/ppermute | solution.py:484
  0.5 3.4 %collective-permute-start.2 = (bf16[1,4,2048]{2,1,0:T(4,128)(2,1)}, bf16[1,4,2048]{2,1,0:T(4,128)(2,1)S(1)}, u32[]{:S(2)}, u32[]{:S(2)}) collective-permute-start(bf16[1,4,2048]{2,1,0:T(4,128)(2,1)} %bitcast.2), channel_id=1, source_target_pairs={{0,24},{4,28},{8,16},{12,20},{16,8},{20,12},{24,0},{28,4},{1,25},{... | collective-permute-start | bytes 49160 | tf_op jit(solution)/shard_map/ppermute | solution.py:484
  3.9 0.5 %collective-permute-start.1 = (bf16[1,4,2048]{2,1,0:T(4,128)(2,1)}, bf16[1,4,2048]{2,1,0:T(4,128)(2,1)S(1)}, u32[]{:S(2)}, u32[]{:S(2)}) collective-permute-start(bf16[1,4,2048]{2,1,0:T(4,128)(2,1)} %bitcast.3), channel_id=1, source_target_pairs={{0,16},{4,20},{8,24},{12,28},{16,0},{20,4},{24,8},{28,12},{1,17},{... | collective-permute-start | bytes 49160 | tf_op jit(solution)/shard_map/ppermute | solution.py:484
  4.4 0.1 collective-permute-start
  4.5 1.6 %shard_map.55 = (bf16[1,4,2048]{2,1,0:T(4,128)(2,1)S(1)}, bf16[4,8,2,64,256]{4,3,2,1,0:T(8,128)(2,1)S(1)}, s32[2,4,2,8,128]{4,3,2,1,0:T(8,128)S(1)}, bf16[2,16,256]{2,1,0:T(8,128)(2,1)S(1)}) custom-call(bf16[1,4,2048]{2,1,0:T(4,128)(2,1)} %bitcast.5, bf16[8,8,2,64,256]{4,3,2,1,0:T(8,128)(2,1)} %kv_in.1, s32[4,8,2,8]{3,2,1,0:T(2,128)} %selected_in.1, ...), custom_call_target="tpu_custom_call" | custom-call | flops 1048576 | bytes 4194304 | tf_op jit(solution)/shard_map/pallas_call | solution.py:119
  6.2 0.0 collective-permute-done.2.refs_3_
  6.2 1.7 %collective-permute-done.1.refs_2_ = bf16[1,4,2048]{2,1,0:T(4,128)(2,1)S(1)} collective-permute-done((bf16[1,4,2048]{2,1,0:T(4,128)(2,1)}, bf16[1,4,2048]{2,1,0:T(4,128)(2,1)S(1)}, u32[]{:S(2)}, u32[]{:S(2)}) %collective-permute-start.1) | collective-permute-done | bytes 16416 | tf_op jit(solution)/shard_map/ppermute | solution.py:484
  7.8 0.5 %collective-permute-done.refs_1_ = bf16[1,4,2048]{2,1,0:T(4,128)(2,1)S(1)} collective-permute-done((bf16[1,4,2048]{2,1,0:T(4,128)(2,1)}, bf16[1,4,2048]{2,1,0:T(4,128)(2,1)S(1)}, u32[]{:S(2)}, u32[]{:S(2)}) %collective-permute-start) | collective-permute-done | bytes 16416 | tf_op jit(solution)/shard_map/ppermute | solution.py:484
  8.4 0.9 %shard_map.56 = (bf16[4,64,256]{2,1,0:T(8,128)(2,1)S(1)}, f32[4,64,128]{2,1,0:T(8,128)S(1)}, f32[4,64,128]{2,1,0:T(8,128)S(1)}, f32[4,64,128]{2,1,0:T(8,128)S(1)}) custom-call(s32[2,4,2,8,128]{4,3,2,1,0:T(8,128)S(1)} %get-tuple-element.18.bits_ref, bf16[2,16,256]{2,1,0:T(8,128)(2,1)S(1)} %get-tuple-element.19.new_ref, ...), custom_call_target="tpu_custom_call" | custom-call | flops 134217728 | bytes 1048576 | tf_op jit(solution)/shard_map/pallas_call | solution.py:251
  9.3 0.0 collective-permute-done.3.other_ref
  9.3 0.8 %shard_map.57._ = bf16[272,128]{1,0:T(8,128)(2,1)S(1)} custom-call(s32[2,4,2,8,128]{4,3,2,1,0:T(8,128)S(1)} %get-tuple-element.18.bits_ref, bf16[4,64,256]{2,1,0:T(8,128)(2,1)S(1)} %get-tuple-element.22.spread_ref, f32[4,64,128]{2,1,0:T(8,128)S(1)} %get-tuple-element.23.sum_ref, f32[4,64,128]{2,1,0:T(8,128)S(1)} %get-tuple-element.24.top_ref, ...), custom_call_target="tpu_custom_call" | custom-call | flops 134217728 | bytes 1048576 | tf_op jit(solution)/shard_map/pallas_call | solution.py:264
  10.0 1.8 %collective-permute-start.7 = (bf16[272,128]{1,0:T(8,128)(2,1)S(1)}, bf16[272,128]{1,0:T(8,128)(2,1)S(1)}, u32[]{:S(2)}, u32[]{:S(2)}) collective-permute-start(bf16[272,128]{1,0:T(8,128)(2,1)S(1)} %shard_map.57._), channel_id=1, source_target_pairs={{0,28},{4,24},{8,20},{12,16},{16,12},{20,8},{24,4},{28,0},{1,29},{... | collective-permute-start | bytes 208904 | tf_op jit(solution)/shard_map/ppermute | solution.py:484
  11.8 0.5 %collective-permute-start.6 = (bf16[272,128]{1,0:T(8,128)(2,1)S(1)}, bf16[272,128]{1,0:T(8,128)(2,1)S(1)}, u32[]{:S(2)}, u32[]{:S(2)}) collective-permute-start(bf16[272,128]{1,0:T(8,128)(2,1)S(1)} %shard_map.57._), channel_id=1, source_target_pairs={{0,20},{4,16},{8,28},{12,24},{16,4},{20,0},{24,12},{28,8},{1,21},{... | collective-permute-start | bytes 208904 | tf_op jit(solution)/shard_map/ppermute | solution.py:484
  12.3 0.5 %collective-permute-start.5 = (bf16[272,128]{1,0:T(8,128)(2,1)S(1)}, bf16[272,128]{1,0:T(8,128)(2,1)S(1)}, u32[]{:S(2)}, u32[]{:S(2)}) collective-permute-start(bf16[272,128]{1,0:T(8,128)(2,1)S(1)} %shard_map.57._), channel_id=1, source_target_pairs={{0,12},{4,8},{8,4},{12,0},{16,28},{20,24},{24,20},{28,16},{1,13},{... | collective-permute-start | bytes 208904 | tf_op jit(solution)/shard_map/ppermute | solution.py:484
  12.8 0.6 %collective-permute-start.4 = (bf16[272,128]{1,0:T(8,128)(2,1)S(1)}, bf16[272,128]{1,0:T(8,128)(2,1)S(1)}, u32[]{:S(2)}, u32[]{:S(2)}) collective-permute-start(bf16[272,128]{1,0:T(8,128)(2,1)S(1)} %shard_map.57._), channel_id=1, source_target_pairs={{0,4},{4,0},{8,12},{12,8},{16,20},{20,16},{24,28},{28,24},{1,5},{5... | collective-permute-start | bytes 208904 | tf_op jit(solution)/shard_map/ppermute | solution.py:484
  13.4 2.2 %shard_map.58.refs_4_.weight_ref = bf16[2048,1024]{1,0:T(8,128)(2,1)S(1)} custom-call(bf16[2048,1024]{1,0:T(8,128)(2,1)} %weight_ref.1, bf16[272,128]{1,0:T(8,128)(2,1)S(1)} %shard_map.57._), custom_call_target="tpu_custom_call" | custom-call | bytes 8388608 | tf_op jit(solution)/shard_map/pallas_call | solution.py:345
  15.6 0.0 collective-permute-done.7.refs_3_
  15.6 0.7 %collective-permute-done.6.refs_2_ = bf16[272,128]{1,0:T(8,128)(2,1)S(1)} collective-permute-done((bf16[272,128]{1,0:T(8,128)(2,1)S(1)}, bf16[272,128]{1,0:T(8,128)(2,1)S(1)}, u32[]{:S(2)}, u32[]{:S(2)}) %collective-permute-start.6) | collective-permute-done | bytes 69664 | tf_op jit(solution)/shard_map/ppermute | solution.py:484
  16.3 0.3 %collective-permute-done.5.refs_1_ = bf16[272,128]{1,0:T(8,128)(2,1)S(1)} collective-permute-done((bf16[272,128]{1,0:T(8,128)(2,1)S(1)}, bf16[272,128]{1,0:T(8,128)(2,1)S(1)}, u32[]{:S(2)}, u32[]{:S(2)}) %collective-permute-start.5) | collective-permute-done | bytes 69664 | tf_op jit(solution)/shard_map/ppermute | solution.py:484
  16.7 0.3 %shard_map.59.att_ref = bf16[4,4,2048]{2,1,0:T(4,128)(2,1)S(1)} custom-call(bf16[272,128]{1,0:T(8,128)(2,1)S(1)} %collective-permute-done.4.refs_0_, bf16[272,128]{1,0:T(8,128)(2,1)S(1)} %collective-permute-done.5.refs_1_, bf16[272,128]{1,0:T(8,128)(2,1)S(1)} %collective-permute-done.6.refs_2_, bf16[272,128]{1,0:T(8,128)(2,1)S(1)} %collective-permute-done.7.refs_3_, ...), custom_call_target="tpu_custom_call" | custom-call | flops 262144 | bytes 262144 | tf_op jit(solution)/shard_map/pallas_call | solution.py:320
  17.0 0.2 collective-permute-start.8
  17.2 0.8 %shard_map.60.half_ref = f32[4,8,1024]{2,1,0:T(8,128)S(1)} custom-call(bf16[4,4,2048]{2,1,0:T(4,128)(2,1)S(1)} %shard_map.59.att_ref, bf16[2048,1024]{1,0:T(8,128)(2,1)S(1)} %shard_map.58.refs_4_.weight_ref), custom_call_target="tpu_custom_call" | custom-call | flops 134217728 | bytes 4194304 | tf_op jit(solution)/shard_map/pallas_call | solution.py:411
  18.0 0.3 %collective-permute-done.8.att_ref = bf16[4,4,2048]{2,1,0:T(4,128)(2,1)S(1)} collective-permute-done((bf16[4,4,2048]{2,1,0:T(4,128)(2,1)S(1)}, bf16[4,4,2048]{2,1,0:T(4,128)(2,1)S(1)}, u32[]{:S(2)}, u32[]{:S(2)}) %collective-permute-start.8) | collective-permute-done | bytes 65568 | tf_op jit(solution)/shard_map/ppermute | solution.py:484
  18.3 0.9 %shard_map.61 = (f32[2,4,1024]{2,1,0:T(4,128)S(1)}, bf16[2,4,1024]{2,1,0:T(4,128)(2,1)S(1)}, bf16[2,4,1024]{2,1,0:T(4,128)(2,1)S(1)}, bf16[2,4,1024]{2,1,0:T(4,128)(2,1)S(1)}, bf16[2,4,1024]{2,1,0:T(4,128)(2,1)S(1)}) custom-call(bf16[4,4,2048]{2,1,0:T(4,128)(2,1)S(1)} %collective-permute-done.8.att_ref, f32[4,8,1024]{2,1,0:T(8,128)S(1)} %shard_map.60.half_ref, ...), custom_call_target="tpu_custom_call" | custom-call | flops 134217728 | bytes 4194304 | tf_op jit(solution)/shard_map/pallas_call | solution.py:429
  19.2 1.8 %collective-permute-start.9 = (bf16[2,4,1024]{2,1,0:T(4,128)(2,1)S(1)}, bf16[2,4,1024]{2,1,0:T(4,128)(2,1)S(1)}, u32[]{:S(2)}, u32[]{:S(2)}) collective-permute-start(bf16[2,4,1024]{2,1,0:T(4,128)(2,1)S(1)} %get-tuple-element.27), channel_id=1, source_target_pairs={{0,1},{1,5},{2,3},{3,0},{4,6},{5,7},{6,2},{7,4},{8,9},{9,13},{10,1... | collective-permute-start | bytes 49160 | tf_op jit(solution)/shard_map/ppermute | solution.py:479
  20.9 0.9 %collective-permute-start.10 = (bf16[2,4,1024]{2,1,0:T(4,128)(2,1)S(1)}, bf16[2,4,1024]{2,1,0:T(4,128)(2,1)S(1)}, u32[]{:S(2)}, u32[]{:S(2)}) collective-permute-start(bf16[2,4,1024]{2,1,0:T(4,128)(2,1)S(1)} %get-tuple-element.28), channel_id=1, source_target_pairs={{0,4},{1,2},{2,0},{3,1},{4,5},{5,6},{6,7},{7,3},{8,12},{9,10},{10,... | collective-permute-start | bytes 49160 | tf_op jit(solution)/shard_map/ppermute | solution.py:479
  21.8 1.6 %collective-permute-start.11 = (bf16[2,4,1024]{2,1,0:T(4,128)(2,1)S(1)}, bf16[2,4,1024]{2,1,0:T(4,128)(2,1)S(1)}, u32[]{:S(2)}, u32[]{:S(2)}) collective-permute-start(bf16[2,4,1024]{2,1,0:T(4,128)(2,1)S(1)} %get-tuple-element.29), channel_id=1, source_target_pairs={{0,3},{1,0},{2,6},{3,2},{4,7},{5,1},{6,4},{7,5},{8,11},{9,8},{10,1... | collective-permute-start | bytes 49160 | tf_op jit(solution)/shard_map/ppermute | solution.py:479
  23.4 0.4 %collective-permute-start.12 = (bf16[2,4,1024]{2,1,0:T(4,128)(2,1)S(1)}, bf16[2,4,1024]{2,1,0:T(4,128)(2,1)S(1)}, u32[]{:S(2)}, u32[]{:S(2)}) collective-permute-start(bf16[2,4,1024]{2,1,0:T(4,128)(2,1)S(1)} %get-tuple-element.30), channel_id=1, source_target_pairs={{0,2},{1,3},{2,1},{3,7},{4,0},{5,4},{6,5},{7,6},{8,10},{9,11},{10,... | collective-permute-start | bytes 49160 | tf_op jit(solution)/shard_map/ppermute | solution.py:479
  23.8 0.9 %collective-permute-done.9 = bf16[2,4,1024]{2,1,0:T(4,128)(2,1)S(1)} collective-permute-done((bf16[2,4,1024]{2,1,0:T(4,128)(2,1)S(1)}, bf16[2,4,1024]{2,1,0:T(4,128)(2,1)S(1)}, u32[]{:S(2)}, u32[]{:S(2)}) %collective-permute-start.9) | collective-permute-done | bytes 16416 | tf_op jit(solution)/shard_map/ppermute | solution.py:479
  24.8 0.8 %collective-permute-done.10 = bf16[2,4,1024]{2,1,0:T(4,128)(2,1)S(1)} collective-permute-done((bf16[2,4,1024]{2,1,0:T(4,128)(2,1)S(1)}, bf16[2,4,1024]{2,1,0:T(4,128)(2,1)S(1)}, u32[]{:S(2)}, u32[]{:S(2)}) %collective-permute-start.10) | collective-permute-done | bytes 16416 | tf_op jit(solution)/shard_map/ppermute | solution.py:479
  25.5 0.2 collective-permute-done.11
  25.8 0.6 %add_convert_fusion = bf16[2,4,1024]{2,1,0:T(4,128)(2,1)} fusion(bf16[2,4,1024]{2,1,0:T(4,128)(2,1)S(1)} %collective-permute-done.12, bf16[2,4,1024]{2,1,0:T(4,128)(2,1)S(1)} %collective-permute-done.11, bf16[2,4,1024]{2,1,0:T(4,128)(2,1)S(1)} %collective-permute-done.10, f32[2,4,1024]{2,1,0:T(4,128)S(1)} %get-tuple-element.26, ...), kind=kLoop, calls=%fused_computation | loop fusion | flops 73728 | bytes 114688 | tf_op jit(solution)/shard_map/convert_element_type | solution.py:518
  (2 shorter events, 0.0 us)
Async XLA Ops:
  0.0 9.3 %collective-permute-start.3 = (bf16[8,8,2,64,256]{4,3,2,1,0:T(8,128)(2,1)}, bf16[8,8,2,64,256]{4,3,2,1,0:T(8,128)(2,1)S(1)}, u32[]{:S(2)}, u32[]{:S(2)}) collective-permute-start(bf16[8,8,2,64,256]{4,3,2,1,0:T(8,128)(2,1)} %kv_in.1), channel_id=1, source_target_pairs={{0,4},{4,0},{8,12},{12,8},{16,20},{20,16},{24,28},{28,24},{1,5},{5... | collective-permute-start | bytes 12582920 | tf_op jit(solution)/shard_map/ppermute | solution.py:484
  0.5 5.7 %collective-permute-start.2 = (bf16[1,4,2048]{2,1,0:T(4,128)(2,1)}, bf16[1,4,2048]{2,1,0:T(4,128)(2,1)S(1)}, u32[]{:S(2)}, u32[]{:S(2)}) collective-permute-start(bf16[1,4,2048]{2,1,0:T(4,128)(2,1)} %bitcast.2), channel_id=1, source_target_pairs={{0,24},{4,28},{8,16},{12,20},{16,8},{20,12},{24,0},{28,4},{1,25},{... | collective-permute-start | bytes 49160 | tf_op jit(solution)/shard_map/ppermute | solution.py:484
  3.9 3.9 %collective-permute-start.1 = (bf16[1,4,2048]{2,1,0:T(4,128)(2,1)}, bf16[1,4,2048]{2,1,0:T(4,128)(2,1)S(1)}, u32[]{:S(2)}, u32[]{:S(2)}) collective-permute-start(bf16[1,4,2048]{2,1,0:T(4,128)(2,1)} %bitcast.3), channel_id=1, source_target_pairs={{0,16},{4,20},{8,24},{12,28},{16,0},{20,4},{24,8},{28,12},{1,17},{... | collective-permute-start | bytes 49160 | tf_op jit(solution)/shard_map/ppermute | solution.py:484
  4.4 3.9 %collective-permute-start = (bf16[1,4,2048]{2,1,0:T(4,128)(2,1)}, bf16[1,4,2048]{2,1,0:T(4,128)(2,1)S(1)}, u32[]{:S(2)}, u32[]{:S(2)}) collective-permute-start(bf16[1,4,2048]{2,1,0:T(4,128)(2,1)} %bitcast.4), channel_id=1, source_target_pairs={{0,8},{4,12},{8,0},{12,4},{16,24},{20,28},{24,16},{28,20},{1,9},{5... | collective-permute-start | bytes 49160 | tf_op jit(solution)/shard_map/ppermute | solution.py:484
  10.0 5.6 %collective-permute-start.7 = (bf16[272,128]{1,0:T(8,128)(2,1)S(1)}, bf16[272,128]{1,0:T(8,128)(2,1)S(1)}, u32[]{:S(2)}, u32[]{:S(2)}) collective-permute-start(bf16[272,128]{1,0:T(8,128)(2,1)S(1)} %shard_map.57._), channel_id=1, source_target_pairs={{0,28},{4,24},{8,20},{12,16},{16,12},{20,8},{24,4},{28,0},{1,29},{... | collective-permute-start | bytes 208904 | tf_op jit(solution)/shard_map/ppermute | solution.py:484
  11.8 4.5 %collective-permute-start.6 = (bf16[272,128]{1,0:T(8,128)(2,1)S(1)}, bf16[272,128]{1,0:T(8,128)(2,1)S(1)}, u32[]{:S(2)}, u32[]{:S(2)}) collective-permute-start(bf16[272,128]{1,0:T(8,128)(2,1)S(1)} %shard_map.57._), channel_id=1, source_target_pairs={{0,20},{4,16},{8,28},{12,24},{16,4},{20,0},{24,12},{28,8},{1,21},{... | collective-permute-start | bytes 208904 | tf_op jit(solution)/shard_map/ppermute | solution.py:484
  12.3 4.4 %collective-permute-start.5 = (bf16[272,128]{1,0:T(8,128)(2,1)S(1)}, bf16[272,128]{1,0:T(8,128)(2,1)S(1)}, u32[]{:S(2)}, u32[]{:S(2)}) collective-permute-start(bf16[272,128]{1,0:T(8,128)(2,1)S(1)} %shard_map.57._), channel_id=1, source_target_pairs={{0,12},{4,8},{8,4},{12,0},{16,28},{20,24},{24,20},{28,16},{1,13},{... | collective-permute-start | bytes 208904 | tf_op jit(solution)/shard_map/ppermute | solution.py:484
  12.8 3.8 %collective-permute-start.4 = (bf16[272,128]{1,0:T(8,128)(2,1)S(1)}, bf16[272,128]{1,0:T(8,128)(2,1)S(1)}, u32[]{:S(2)}, u32[]{:S(2)}) collective-permute-start(bf16[272,128]{1,0:T(8,128)(2,1)S(1)} %shard_map.57._), channel_id=1, source_target_pairs={{0,4},{4,0},{8,12},{12,8},{16,20},{20,16},{24,28},{28,24},{1,5},{5... | collective-permute-start | bytes 208904 | tf_op jit(solution)/shard_map/ppermute | solution.py:484
  17.0 1.3 %collective-permute-start.8 = (bf16[4,4,2048]{2,1,0:T(4,128)(2,1)S(1)}, bf16[4,4,2048]{2,1,0:T(4,128)(2,1)S(1)}, u32[]{:S(2)}, u32[]{:S(2)}) collective-permute-start(bf16[4,4,2048]{2,1,0:T(4,128)(2,1)S(1)} %shard_map.59.att_ref), channel_id=1, source_target_pairs={{0,4},{4,0},{8,12},{12,8},{16,20},{20,16},{24,28},{28,24},{1,5},{5... | collective-permute-start | bytes 196616 | tf_op jit(solution)/shard_map/ppermute | solution.py:484
  19.2 5.6 %collective-permute-start.9 = (bf16[2,4,1024]{2,1,0:T(4,128)(2,1)S(1)}, bf16[2,4,1024]{2,1,0:T(4,128)(2,1)S(1)}, u32[]{:S(2)}, u32[]{:S(2)}) collective-permute-start(bf16[2,4,1024]{2,1,0:T(4,128)(2,1)S(1)} %get-tuple-element.27), channel_id=1, source_target_pairs={{0,1},{1,5},{2,3},{3,0},{4,6},{5,7},{6,2},{7,4},{8,9},{9,13},{10,1... | collective-permute-start | bytes 49160 | tf_op jit(solution)/shard_map/ppermute | solution.py:479
  20.9 4.6 %collective-permute-start.10 = (bf16[2,4,1024]{2,1,0:T(4,128)(2,1)S(1)}, bf16[2,4,1024]{2,1,0:T(4,128)(2,1)S(1)}, u32[]{:S(2)}, u32[]{:S(2)}) collective-permute-start(bf16[2,4,1024]{2,1,0:T(4,128)(2,1)S(1)} %get-tuple-element.28), channel_id=1, source_target_pairs={{0,4},{1,2},{2,0},{3,1},{4,5},{5,6},{6,7},{7,3},{8,12},{9,10},{10,... | collective-permute-start | bytes 49160 | tf_op jit(solution)/shard_map/ppermute | solution.py:479
  21.8 4.0 %collective-permute-start.11 = (bf16[2,4,1024]{2,1,0:T(4,128)(2,1)S(1)}, bf16[2,4,1024]{2,1,0:T(4,128)(2,1)S(1)}, u32[]{:S(2)}, u32[]{:S(2)}) collective-permute-start(bf16[2,4,1024]{2,1,0:T(4,128)(2,1)S(1)} %get-tuple-element.29), channel_id=1, source_target_pairs={{0,3},{1,0},{2,6},{3,2},{4,7},{5,1},{6,4},{7,5},{8,11},{9,8},{10,1... | collective-permute-start | bytes 49160 | tf_op jit(solution)/shard_map/ppermute | solution.py:479
  23.4 2.4 %collective-permute-start.12 = (bf16[2,4,1024]{2,1,0:T(4,128)(2,1)S(1)}, bf16[2,4,1024]{2,1,0:T(4,128)(2,1)S(1)}, u32[]{:S(2)}, u32[]{:S(2)}) collective-permute-start(bf16[2,4,1024]{2,1,0:T(4,128)(2,1)S(1)} %get-tuple-element.30), channel_id=1, source_target_pairs={{0,2},{1,3},{2,1},{3,7},{4,0},{5,4},{6,5},{7,6},{8,10},{9,11},{10,... | collective-permute-start | bytes 49160 | tf_op jit(solution)/shard_map/ppermute | solution.py:479

commit v4 on v3

--- a/solution.py
+++ b/solution.py
@@ -298,6 +298,7 @@
         packed.append(wide)
     on_row = lax.broadcasted_iota(jnp.int32, (rows, 128), 0)
     diagonal = lax.broadcasted_iota(jnp.int32, (rows, 128), 1) % rows == on_row
+    joined = []
     for i in range(m):
         weights = jnp.concatenate(
             [jnp.where(diagonal, wide[i : i + 1], 0.0) for wide in packed], axis=1
@@ -308,18 +309,19 @@
         )
         high = weights.astype(jnp.bfloat16)
         low = (weights - high.astype(jnp.float32)).astype(jnp.bfloat16)
-        joined = jnp.dot(high, parts, preferred_element_type=jnp.float32)
-        joined = joined + jnp.dot(low, parts, preferred_element_type=jnp.float32)
-        for j in range(rows // steps):
-            piece = joined[j * steps : (j + 1) * steps]
-            out_ref[i, :, j * HD : (j + 1) * HD] = piece.astype(jnp.bfloat16)
+        product = jnp.dot(high, parts, preferred_element_type=jnp.float32)
+        product = product + jnp.dot(low, parts, preferred_element_type=jnp.float32)
+        joined.append(product)
+    for j in range(rows // steps):
+        piece = jnp.concatenate([x[j * steps : (j + 1) * steps] for x in joined], axis=0)
+        out_ref[:, j * HD : (j + 1) * HD] = piece.astype(jnp.bfloat16)
 
 
 def last_merge(parts, weight, rows, steps):
     m = len(parts)
     return pl.pallas_call(
         functools.partial(last_merge_kernel, rows, steps),
-        out_shape=jax.ShapeDtypeStruct((m, steps, rows // steps * HD), jnp.bfloat16),
+        out_shape=jax.ShapeDtypeStruct((m * steps, rows // steps * HD), jnp.bfloat16),
         in_specs=[VMEM] * m + [ANY],
         out_specs=VMEM,
         compiler_params=pltpu.CompilerParams(vmem_limit_bytes=VMEM_LIMIT),
@@ -355,31 +357,19 @@
     )(pltpu.with_memory_space_constraint(out_weight, pltpu.HBM), after)
 
 
-def project_rows(att_ref, weight_ref, lhs):
-    count, _, width = lhs.shape
-    steps = att_ref.shape[1]
-    for i in range(count):
-        lhs[i, :steps, :] = att_ref[i].astype(jnp.float32)
-    left = lhs[...].reshape(count * 8, width).astype(jnp.bfloat16)
-    product = jnp.dot(left, weight_ref[...], preferred_element_type=jnp.float32)
-    return product.reshape(count, 8, weight_ref.shape[1])
-
-
-def half_kernel(att_ref, weight_ref, out_ref, lhs):
-    out_ref[...] = project_rows(att_ref, weight_ref, lhs)
+def half_kernel(att_ref, weight_ref, out_ref):
+    out_ref[...] = jnp.dot(att_ref[...], weight_ref[...], preferred_element_type=jnp.float32)
 
 
 def project_kernel(n_head, targets, att_ref, half_ref, weight_ref, *refs):
-    lhs, rows_all = refs[-2:]
-    out_refs = refs[:-2]
-    m, steps, _ = att_ref.shape
-    seqs = 2 * m // n_head
+    *out_refs, rows_all = refs
+    seqs, steps, _ = out_refs[0].shape
     me = lax.axis_index("ctx")
     mine = lax.axis_index("head")
-    product = project_rows(att_ref, weight_ref, lhs)
-    for i in range(m):
-        rows_all[2 * i] = product[i]
-        rows_all[2 * i + 1] = half_ref[i]
+    product = jnp.dot(att_ref[...], weight_ref[...], preferred_element_type=jnp.float32)
+    for i in range(rows_all.shape[0] // 2):
+        rows_all[2 * i, :steps, :] = product[i * steps : (i + 1) * steps]
+        rows_all[2 * i + 1, :steps, :] = half_ref[i * steps : (i + 1) * steps, :]
     for k, ref in enumerate(out_refs):
         target = mine
         if k > 0:
@@ -387,40 +377,34 @@
                 for z, t in enumerate(row):
                     target = jnp.where((me % 2 == core) & (mine == z), t, target)
         for j in range(seqs):
-            found = rows_all[(jnp.maximum(target, 0) * seqs + j) ^ me][:steps]
+            found = rows_all[(jnp.maximum(target, 0) * seqs + j) ^ me, :steps]
             if k > 0 and any(t < 0 for row in targets[k - 1] for t in row):
                 found = jnp.where(target < 0, 0.0, found)
             ref[j] = found.astype(ref.dtype)
 
 
 def project_options(att, weight):
-    m, _, width = att.shape
-    columns = weight.shape[1]
+    width, columns = weight.shape
     return dict(
         compiler_params=pltpu.CompilerParams(vmem_limit_bytes=VMEM_LIMIT),
         cost_estimate=pl.CostEstimate(
-            flops=2 * m * 8 * width * columns,
-            bytes_accessed=width * columns * 2,
-            transcendentals=0,
+            flops=2 * att.size * columns, bytes_accessed=width * columns * 2, transcendentals=0
         ),
     )
 
 
 def project_half(att, weight):
-    m, _, width = att.shape
     return pl.pallas_call(
         half_kernel,
-        out_shape=jax.ShapeDtypeStruct((m, 8, weight.shape[1]), jnp.float32),
+        out_shape=jax.ShapeDtypeStruct((att.shape[0], weight.shape[1]), jnp.float32),
         in_specs=[VMEM] * 2,
         out_specs=VMEM,
-        scratch_shapes=[pltpu.VMEM((m, 8, width), jnp.float32)],
         **project_options(att, weight),
     )(att, weight)
 
 
-def project(att, half, weight, n_head, targets):
-    m, steps, width = att.shape
-    n = 2 * m
+def project(att, half, weight, steps, n_head, targets):
+    n = 2 * att.shape[0] // steps
     columns = weight.shape[1]
     outs = [
         jax.ShapeDtypeStruct((n // n_head, steps, columns), jnp.bfloat16 if k else jnp.float32)
@@ -431,10 +415,7 @@
         out_shape=outs,
         in_specs=[VMEM] * 3,
         out_specs=[VMEM] * len(outs),
-        scratch_shapes=[
-            pltpu.VMEM((m, 8, width), jnp.float32),
-            pltpu.VMEM((n, 8, columns), jnp.float32),
-        ],
+        scratch_shapes=[pltpu.VMEM((n, 8, columns), jnp.float32)],
         **project_options(att, weight),
     )(att, half, weight)
 
@@ -512,7 +493,9 @@
     even_att = swap(odd_att, "ctx", 1)
     plan = head_plan(n_head)
     half = project_half(odd_att, weight)
-    total, *rows_out = project(even_att, half, weight, n_head, plan_targets(plan))
+    total, *rows_out = project(
+        even_att, half, weight, steps, n_head, plan_targets(plan)
+    )
     for chunk, permutation in zip(rows_out, plan):
         total = total + send_by(permutation, chunk).astype(jnp.float32)
     return total.astype(jnp.bfloat16)

time: 26.9 us -> 26.7 us (level)
  Pallas kernels: 7.5 us -> 7.15 us
where the time goes in v4:
time: 26.7 us; the launch traced here: 26.2 us
  starting transfers between devices  12.8 us (48%)
  Pallas kernels  7.15 us (27%)
  waiting for transfers between devices  5.62 us (21%)
  other arithmetic  0.63 us (2%)
    ppermute x9, starting transfers between devices, swap(): return lax.ppermute(x, axis, [(i, i ^ r) for i in range(size)])  8.09 us
    ppermute x4, starting transfers between devices, send_by(): return lax.ppermute(x, ('ctx', 'head'), pairs)  4.68 us
    ppermute x9, waiting for transfers between devices, swap(): return lax.ppermute(x, axis, [(i, i ^ r) for i in range(size)])  3.68 us
    pallas_call x1, Pallas kernels, load_weight(): pl.pallas_call(load_kernel, out_shape=jax.ShapeDtypeStruct(out_weight.sha...  2.2 us
    ppermute x4, waiting for transfers between devices, send_by(): return lax.ppermute(x, ('ctx', 'head'), pairs)  1.94 us
    pallas_call x1, Pallas kernels, own_side(): pl.pallas_call(own_kernel, out_shape=[jax.ShapeDtypeStruct(queries.shape,...  1.63 us
    pallas_call x1, Pallas kernels, partials(): pl.pallas_call(functools.partial(first_kernel, heads), out_shape=[jax.Sha...  0.91 us
    pallas_call x1, Pallas kernels, partials(): pl.pallas_call(functools.partial(second_kernel, steps, heads), out_shape=...  0.76 us
  transfers between devices with their start and end apart: 13, of which 8 were waited for; matrix products, arithmetic and copies ran while one was open for 0% of the time, Pallas kernels for 21%

profile of v4, /device:TPU:0, one launch (start us, length us, event | category | flops | bytes accessed | tf_op | source)
XLA Modules:
  0.0 26.2 jit_solution(10028243325340556443)
XLA Ops:
  0.0 0.5 %collective-permute-start.3 = (bf16[8,8,2,64,256]{4,3,2,1,0:T(8,128)(2,1)}, bf16[8,8,2,64,256]{4,3,2,1,0:T(8,128)(2,1)S(1)}, u32[]{:S(2)}, u32[]{:S(2)}) collective-permute-start(bf16[8,8,2,64,256]{4,3,2,1,0:T(8,128)(2,1)} %kv_in.1), channel_id=1, source_target_pairs={{0,4},{4,0},{8,12},{12,8},{16,20},{20,16},{24,28},{28,24},{1,5},{5... | collective-permute-start | bytes 12582920 | tf_op jit(solution)/shard_map/ppermute | solution.py:465
  0.5 3.4 %collective-permute-start.2 = (bf16[1,4,2048]{2,1,0:T(4,128)(2,1)}, bf16[1,4,2048]{2,1,0:T(4,128)(2,1)S(1)}, u32[]{:S(2)}, u32[]{:S(2)}) collective-permute-start(bf16[1,4,2048]{2,1,0:T(4,128)(2,1)} %bitcast.2), channel_id=1, source_target_pairs={{0,24},{4,28},{8,16},{12,20},{16,8},{20,12},{24,0},{28,4},{1,25},{... | collective-permute-start | bytes 49160 | tf_op jit(solution)/shard_map/ppermute | solution.py:465
  3.9 0.5 %collective-permute-start.1 = (bf16[1,4,2048]{2,1,0:T(4,128)(2,1)}, bf16[1,4,2048]{2,1,0:T(4,128)(2,1)S(1)}, u32[]{:S(2)}, u32[]{:S(2)}) collective-permute-start(bf16[1,4,2048]{2,1,0:T(4,128)(2,1)} %bitcast.3), channel_id=1, source_target_pairs={{0,16},{4,20},{8,24},{12,28},{16,0},{20,4},{24,8},{28,12},{1,17},{... | collective-permute-start | bytes 49160 | tf_op jit(solution)/shard_map/ppermute | solution.py:465
  4.4 0.1 collective-permute-start
  4.5 1.6 %shard_map.55 = (bf16[1,4,2048]{2,1,0:T(4,128)(2,1)S(1)}, bf16[4,8,2,64,256]{4,3,2,1,0:T(8,128)(2,1)S(1)}, s32[2,4,2,8,128]{4,3,2,1,0:T(8,128)S(1)}, bf16[2,16,256]{2,1,0:T(8,128)(2,1)S(1)}) custom-call(bf16[1,4,2048]{2,1,0:T(4,128)(2,1)} %bitcast.5, bf16[8,8,2,64,256]{4,3,2,1,0:T(8,128)(2,1)} %kv_in.1, s32[4,8,2,8]{3,2,1,0:T(2,128)} %selected_in.1, ...), custom_call_target="tpu_custom_call" | custom-call | flops 1048576 | bytes 4194304 | tf_op jit(solution)/shard_map/pallas_call | solution.py:119
  6.2 0.0 collective-permute-done.2.refs_3_
  6.2 1.7 %collective-permute-done.1.refs_2_ = bf16[1,4,2048]{2,1,0:T(4,128)(2,1)S(1)} collective-permute-done((bf16[1,4,2048]{2,1,0:T(4,128)(2,1)}, bf16[1,4,2048]{2,1,0:T(4,128)(2,1)S(1)}, u32[]{:S(2)}, u32[]{:S(2)}) %collective-permute-start.1) | collective-permute-done | bytes 16416 | tf_op jit(solution)/shard_map/ppermute | solution.py:465
  7.8 0.5 %collective-permute-done.refs_1_ = bf16[1,4,2048]{2,1,0:T(4,128)(2,1)S(1)} collective-permute-done((bf16[1,4,2048]{2,1,0:T(4,128)(2,1)}, bf16[1,4,2048]{2,1,0:T(4,128)(2,1)S(1)}, u32[]{:S(2)}, u32[]{:S(2)}) %collective-permute-start) | collective-permute-done | bytes 16416 | tf_op jit(solution)/shard_map/ppermute | solution.py:465
  8.4 0.9 %shard_map.56 = (bf16[4,64,256]{2,1,0:T(8,128)(2,1)S(1)}, f32[4,64,128]{2,1,0:T(8,128)S(1)}, f32[4,64,128]{2,1,0:T(8,128)S(1)}, f32[4,64,128]{2,1,0:T(8,128)S(1)}) custom-call(s32[2,4,2,8,128]{4,3,2,1,0:T(8,128)S(1)} %get-tuple-element.18.bits_ref, bf16[2,16,256]{2,1,0:T(8,128)(2,1)S(1)} %get-tuple-element.19.new_ref, ...), custom_call_target="tpu_custom_call" | custom-call | flops 134217728 | bytes 1048576 | tf_op jit(solution)/shard_map/pallas_call | solution.py:251
  9.3 0.8 %shard_map.57._ = bf16[272,128]{1,0:T(8,128)(2,1)S(1)} custom-call(s32[2,4,2,8,128]{4,3,2,1,0:T(8,128)S(1)} %get-tuple-element.18.bits_ref, bf16[4,64,256]{2,1,0:T(8,128)(2,1)S(1)} %get-tuple-element.22.spread_ref, f32[4,64,128]{2,1,0:T(8,128)S(1)} %get-tuple-element.23.sum_ref, f32[4,64,128]{2,1,0:T(8,128)S(1)} %get-tuple-element.24.top_ref, ...), custom_call_target="tpu_custom_call" | custom-call | flops 134217728 | bytes 1048576 | tf_op jit(solution)/shard_map/pallas_call | solution.py:264
  10.0 1.8 %collective-permute-start.7 = (bf16[272,128]{1,0:T(8,128)(2,1)S(1)}, bf16[272,128]{1,0:T(8,128)(2,1)S(1)}, u32[]{:S(2)}, u32[]{:S(2)}) collective-permute-start(bf16[272,128]{1,0:T(8,128)(2,1)S(1)} %shard_map.57._), channel_id=1, source_target_pairs={{0,28},{4,24},{8,20},{12,16},{16,12},{20,8},{24,4},{28,0},{1,29},{... | collective-permute-start | bytes 208904 | tf_op jit(solution)/shard_map/ppermute | solution.py:465
  11.8 0.5 %collective-permute-start.6 = (bf16[272,128]{1,0:T(8,128)(2,1)S(1)}, bf16[272,128]{1,0:T(8,128)(2,1)S(1)}, u32[]{:S(2)}, u32[]{:S(2)}) collective-permute-start(bf16[272,128]{1,0:T(8,128)(2,1)S(1)} %shard_map.57._), channel_id=1, source_target_pairs={{0,20},{4,16},{8,28},{12,24},{16,4},{20,0},{24,12},{28,8},{1,21},{... | collective-permute-start | bytes 208904 | tf_op jit(solution)/shard_map/ppermute | solution.py:465
  12.3 0.5 %collective-permute-start.5 = (bf16[272,128]{1,0:T(8,128)(2,1)S(1)}, bf16[272,128]{1,0:T(8,128)(2,1)S(1)}, u32[]{:S(2)}, u32[]{:S(2)}) collective-permute-start(bf16[272,128]{1,0:T(8,128)(2,1)S(1)} %shard_map.57._), channel_id=1, source_target_pairs={{0,12},{4,8},{8,4},{12,0},{16,28},{20,24},{24,20},{28,16},{1,13},{... | collective-permute-start | bytes 208904 | tf_op jit(solution)/shard_map/ppermute | solution.py:465
  12.8 0.6 %collective-permute-start.4 = (bf16[272,128]{1,0:T(8,128)(2,1)S(1)}, bf16[272,128]{1,0:T(8,128)(2,1)S(1)}, u32[]{:S(2)}, u32[]{:S(2)}) collective-permute-start(bf16[272,128]{1,0:T(8,128)(2,1)S(1)} %shard_map.57._), channel_id=1, source_target_pairs={{0,4},{4,0},{8,12},{12,8},{16,20},{20,16},{24,28},{28,24},{1,5},{5... | collective-permute-start | bytes 208904 | tf_op jit(solution)/shard_map/ppermute | solution.py:465
  13.4 2.2 %shard_map.58.refs_4_.weight_ref = bf16[2048,1024]{1,0:T(8,128)(2,1)S(1)} custom-call(bf16[2048,1024]{1,0:T(8,128)(2,1)} %weight_ref.1, bf16[272,128]{1,0:T(8,128)(2,1)S(1)} %shard_map.57._), custom_call_target="tpu_custom_call" | custom-call | bytes 8388608 | tf_op jit(solution)/shard_map/pallas_call | solution.py:347
  15.6 0.0 collective-permute-done.7.refs_3_
  15.6 0.7 %collective-permute-done.6.refs_2_ = bf16[272,128]{1,0:T(8,128)(2,1)S(1)} collective-permute-done((bf16[272,128]{1,0:T(8,128)(2,1)S(1)}, bf16[272,128]{1,0:T(8,128)(2,1)S(1)}, u32[]{:S(2)}, u32[]{:S(2)}) %collective-permute-start.6) | collective-permute-done | bytes 69664 | tf_op jit(solution)/shard_map/ppermute | solution.py:465
  16.3 0.3 %collective-permute-done.5.refs_1_ = bf16[272,128]{1,0:T(8,128)(2,1)S(1)} collective-permute-done((bf16[272,128]{1,0:T(8,128)(2,1)S(1)}, bf16[272,128]{1,0:T(8,128)(2,1)S(1)}, u32[]{:S(2)}, u32[]{:S(2)}) %collective-permute-start.5) | collective-permute-done | bytes 69664 | tf_op jit(solution)/shard_map/ppermute | solution.py:465
  16.6 0.0 collective-permute-done.4.refs_0_
  16.7 0.3 %shard_map.59.att_ref = bf16[16,2048]{1,0:T(8,128)(2,1)S(1)} custom-call(bf16[272,128]{1,0:T(8,128)(2,1)S(1)} %collective-permute-done.4.refs_0_, bf16[272,128]{1,0:T(8,128)(2,1)S(1)} %collective-permute-done.5.refs_1_, bf16[272,128]{1,0:T(8,128)(2,1)S(1)} %collective-permute-done.6.refs_2_, bf16[272,128]{1,0:T(8,128)(2,1)S(1)} %collective-permute-done.7.refs_3_, ...), custom_call_target="tpu_custom_call" | custom-call | flops 262144 | bytes 262144 | tf_op jit(solution)/shard_map/pallas_call | solution.py:322
  17.0 0.2 collective-permute-start.8
  17.2 0.6 %shard_map.60.half_ref = f32[16,1024]{1,0:T(8,128)S(1)} custom-call(bf16[16,2048]{1,0:T(8,128)(2,1)S(1)} %shard_map.59.att_ref, bf16[2048,1024]{1,0:T(8,128)(2,1)S(1)} %shard_map.58.refs_4_.weight_ref), custom_call_target="tpu_custom_call" | custom-call | flops 67108864 | bytes 4194304 | tf_op jit(solution)/shard_map/pallas_call | solution.py:397
  17.8 0.5 %collective-permute-done.8.att_ref = bf16[16,2048]{1,0:T(8,128)(2,1)S(1)} collective-permute-done((bf16[16,2048]{1,0:T(8,128)(2,1)S(1)}, bf16[16,2048]{1,0:T(8,128)(2,1)S(1)}, u32[]{:S(2)}, u32[]{:S(2)}) %collective-permute-start.8) | collective-permute-done | bytes 65568 | tf_op jit(solution)/shard_map/ppermute | solution.py:465
  18.3 0.7 %shard_map.61 = (f32[2,4,1024]{2,1,0:T(4,128)S(1)}, bf16[2,4,1024]{2,1,0:T(4,128)(2,1)S(1)}, bf16[2,4,1024]{2,1,0:T(4,128)(2,1)S(1)}, bf16[2,4,1024]{2,1,0:T(4,128)(2,1)S(1)}, bf16[2,4,1024]{2,1,0:T(4,128)(2,1)S(1)}) custom-call(bf16[16,2048]{1,0:T(8,128)(2,1)S(1)} %collective-permute-done.8.att_ref, f32[16,1024]{1,0:T(8,128)S(1)} %shard_map.60.half_ref, ...), custom_call_target="tpu_custom_call" | custom-call | flops 67108864 | bytes 4194304 | tf_op jit(solution)/shard_map/pallas_call | solution.py:413
  19.0 1.8 %collective-permute-start.9 = (bf16[2,4,1024]{2,1,0:T(4,128)(2,1)S(1)}, bf16[2,4,1024]{2,1,0:T(4,128)(2,1)S(1)}, u32[]{:S(2)}, u32[]{:S(2)}) collective-permute-start(bf16[2,4,1024]{2,1,0:T(4,128)(2,1)S(1)} %get-tuple-element.27), channel_id=1, source_target_pairs={{0,1},{1,5},{2,3},{3,0},{4,6},{5,7},{6,2},{7,4},{8,9},{9,13},{10,1... | collective-permute-start | bytes 49160 | tf_op jit(solution)/shard_map/ppermute | solution.py:460
  20.7 0.9 %collective-permute-start.10 = (bf16[2,4,1024]{2,1,0:T(4,128)(2,1)S(1)}, bf16[2,4,1024]{2,1,0:T(4,128)(2,1)S(1)}, u32[]{:S(2)}, u32[]{:S(2)}) collective-permute-start(bf16[2,4,1024]{2,1,0:T(4,128)(2,1)S(1)} %get-tuple-element.28), channel_id=1, source_target_pairs={{0,4},{1,2},{2,0},{3,1},{4,5},{5,6},{6,7},{7,3},{8,12},{9,10},{10,... | collective-permute-start | bytes 49160 | tf_op jit(solution)/shard_map/ppermute | solution.py:460
  21.6 1.6 %collective-permute-start.11 = (bf16[2,4,1024]{2,1,0:T(4,128)(2,1)S(1)}, bf16[2,4,1024]{2,1,0:T(4,128)(2,1)S(1)}, u32[]{:S(2)}, u32[]{:S(2)}) collective-permute-start(bf16[2,4,1024]{2,1,0:T(4,128)(2,1)S(1)} %get-tuple-element.29), channel_id=1, source_target_pairs={{0,3},{1,0},{2,6},{3,2},{4,7},{5,1},{6,4},{7,5},{8,11},{9,8},{10,1... | collective-permute-start | bytes 49160 | tf_op jit(solution)/shard_map/ppermute | solution.py:460
  23.3 0.4 %collective-permute-start.12 = (bf16[2,4,1024]{2,1,0:T(4,128)(2,1)S(1)}, bf16[2,4,1024]{2,1,0:T(4,128)(2,1)S(1)}, u32[]{:S(2)}, u32[]{:S(2)}) collective-permute-start(bf16[2,4,1024]{2,1,0:T(4,128)(2,1)S(1)} %get-tuple-element.30), channel_id=1, source_target_pairs={{0,2},{1,3},{2,1},{3,7},{4,0},{5,4},{6,5},{7,6},{8,10},{9,11},{10,... | collective-permute-start | bytes 49160 | tf_op jit(solution)/shard_map/ppermute | solution.py:460
  23.7 0.9 %collective-permute-done.9 = bf16[2,4,1024]{2,1,0:T(4,128)(2,1)S(1)} collective-permute-done((bf16[2,4,1024]{2,1,0:T(4,128)(2,1)S(1)}, bf16[2,4,1024]{2,1,0:T(4,128)(2,1)S(1)}, u32[]{:S(2)}, u32[]{:S(2)}) %collective-permute-start.9) | collective-permute-done | bytes 16416 | tf_op jit(solution)/shard_map/ppermute | solution.py:460
  24.6 0.8 %collective-permute-done.10 = bf16[2,4,1024]{2,1,0:T(4,128)(2,1)S(1)} collective-permute-done((bf16[2,4,1024]{2,1,0:T(4,128)(2,1)S(1)}, bf16[2,4,1024]{2,1,0:T(4,128)(2,1)S(1)}, u32[]{:S(2)}, u32[]{:S(2)}) %collective-permute-start.10) | collective-permute-done | bytes 16416 | tf_op jit(solution)/shard_map/ppermute | solution.py:460
  25.4 0.2 collective-permute-done.11
  25.6 0.6 %add_convert_fusion = bf16[2,4,1024]{2,1,0:T(4,128)(2,1)} fusion(bf16[2,4,1024]{2,1,0:T(4,128)(2,1)S(1)} %collective-permute-done.12, bf16[2,4,1024]{2,1,0:T(4,128)(2,1)S(1)} %collective-permute-done.11, bf16[2,4,1024]{2,1,0:T(4,128)(2,1)S(1)} %collective-permute-done.10, f32[2,4,1024]{2,1,0:T(4,128)S(1)} %get-tuple-element.26, ...), kind=kLoop, calls=%fused_computation | loop fusion | flops 73728 | bytes 114688 | tf_op jit(solution)/shard_map/convert_element_type | solution.py:501
  (2 shorter events, 0.0 us)
Async XLA Ops:
  0.0 9.3 %collective-permute-start.3 = (bf16[8,8,2,64,256]{4,3,2,1,0:T(8,128)(2,1)}, bf16[8,8,2,64,256]{4,3,2,1,0:T(8,128)(2,1)S(1)}, u32[]{:S(2)}, u32[]{:S(2)}) collective-permute-start(bf16[8,8,2,64,256]{4,3,2,1,0:T(8,128)(2,1)} %kv_in.1), channel_id=1, source_target_pairs={{0,4},{4,0},{8,12},{12,8},{16,20},{20,16},{24,28},{28,24},{1,5},{5... | collective-permute-start | bytes 12582920 | tf_op jit(solution)/shard_map/ppermute | solution.py:465
  0.5 5.7 %collective-permute-start.2 = (bf16[1,4,2048]{2,1,0:T(4,128)(2,1)}, bf16[1,4,2048]{2,1,0:T(4,128)(2,1)S(1)}, u32[]{:S(2)}, u32[]{:S(2)}) collective-permute-start(bf16[1,4,2048]{2,1,0:T(4,128)(2,1)} %bitcast.2), channel_id=1, source_target_pairs={{0,24},{4,28},{8,16},{12,20},{16,8},{20,12},{24,0},{28,4},{1,25},{... | collective-permute-start | bytes 49160 | tf_op jit(solution)/shard_map/ppermute | solution.py:465
  3.9 3.9 %collective-permute-start.1 = (bf16[1,4,2048]{2,1,0:T(4,128)(2,1)}, bf16[1,4,2048]{2,1,0:T(4,128)(2,1)S(1)}, u32[]{:S(2)}, u32[]{:S(2)}) collective-permute-start(bf16[1,4,2048]{2,1,0:T(4,128)(2,1)} %bitcast.3), channel_id=1, source_target_pairs={{0,16},{4,20},{8,24},{12,28},{16,0},{20,4},{24,8},{28,12},{1,17},{... | collective-permute-start | bytes 49160 | tf_op jit(solution)/shard_map/ppermute | solution.py:465
  4.4 3.9 %collective-permute-start = (bf16[1,4,2048]{2,1,0:T(4,128)(2,1)}, bf16[1,4,2048]{2,1,0:T(4,128)(2,1)S(1)}, u32[]{:S(2)}, u32[]{:S(2)}) collective-permute-start(bf16[1,4,2048]{2,1,0:T(4,128)(2,1)} %bitcast.4), channel_id=1, source_target_pairs={{0,8},{4,12},{8,0},{12,4},{16,24},{20,28},{24,16},{28,20},{1,9},{5... | collective-permute-start | bytes 49160 | tf_op jit(solution)/shard_map/ppermute | solution.py:465
  10.0 5.6 %collective-permute-start.7 = (bf16[272,128]{1,0:T(8,128)(2,1)S(1)}, bf16[272,128]{1,0:T(8,128)(2,1)S(1)}, u32[]{:S(2)}, u32[]{:S(2)}) collective-permute-start(bf16[272,128]{1,0:T(8,128)(2,1)S(1)} %shard_map.57._), channel_id=1, source_target_pairs={{0,28},{4,24},{8,20},{12,16},{16,12},{20,8},{24,4},{28,0},{1,29},{... | collective-permute-start | bytes 208904 | tf_op jit(solution)/shard_map/ppermute | solution.py:465
  11.8 4.5 %collective-permute-start.6 = (bf16[272,128]{1,0:T(8,128)(2,1)S(1)}, bf16[272,128]{1,0:T(8,128)(2,1)S(1)}, u32[]{:S(2)}, u32[]{:S(2)}) collective-permute-start(bf16[272,128]{1,0:T(8,128)(2,1)S(1)} %shard_map.57._), channel_id=1, source_target_pairs={{0,20},{4,16},{8,28},{12,24},{16,4},{20,0},{24,12},{28,8},{1,21},{... | collective-permute-start | bytes 208904 | tf_op jit(solution)/shard_map/ppermute | solution.py:465
  12.3 4.4 %collective-permute-start.5 = (bf16[272,128]{1,0:T(8,128)(2,1)S(1)}, bf16[272,128]{1,0:T(8,128)(2,1)S(1)}, u32[]{:S(2)}, u32[]{:S(2)}) collective-permute-start(bf16[272,128]{1,0:T(8,128)(2,1)S(1)} %shard_map.57._), channel_id=1, source_target_pairs={{0,12},{4,8},{8,4},{12,0},{16,28},{20,24},{24,20},{28,16},{1,13},{... | collective-permute-start | bytes 208904 | tf_op jit(solution)/shard_map/ppermute | solution.py:465
  12.8 3.8 %collective-permute-start.4 = (bf16[272,128]{1,0:T(8,128)(2,1)S(1)}, bf16[272,128]{1,0:T(8,128)(2,1)S(1)}, u32[]{:S(2)}, u32[]{:S(2)}) collective-permute-start(bf16[272,128]{1,0:T(8,128)(2,1)S(1)} %shard_map.57._), channel_id=1, source_target_pairs={{0,4},{4,0},{8,12},{12,8},{16,20},{20,16},{24,28},{28,24},{1,5},{5... | collective-permute-start | bytes 208904 | tf_op jit(solution)/shard_map/ppermute | solution.py:465
  17.0 1.3 %collective-permute-start.8 = (bf16[16,2048]{1,0:T(8,128)(2,1)S(1)}, bf16[16,2048]{1,0:T(8,128)(2,1)S(1)}, u32[]{:S(2)}, u32[]{:S(2)}) collective-permute-start(bf16[16,2048]{1,0:T(8,128)(2,1)S(1)} %shard_map.59.att_ref), channel_id=1, source_target_pairs={{0,4},{4,0},{8,12},{12,8},{16,20},{20,16},{24,28},{28,24},{1,5},{5... | collective-permute-start | bytes 196616 | tf_op jit(solution)/shard_map/ppermute | solution.py:465
  19.0 5.6 %collective-permute-start.9 = (bf16[2,4,1024]{2,1,0:T(4,128)(2,1)S(1)}, bf16[2,4,1024]{2,1,0:T(4,128)(2,1)S(1)}, u32[]{:S(2)}, u32[]{:S(2)}) collective-permute-start(bf16[2,4,1024]{2,1,0:T(4,128)(2,1)S(1)} %get-tuple-element.27), channel_id=1, source_target_pairs={{0,1},{1,5},{2,3},{3,0},{4,6},{5,7},{6,2},{7,4},{8,9},{9,13},{10,1... | collective-permute-start | bytes 49160 | tf_op jit(solution)/shard_map/ppermute | solution.py:460
  20.7 4.6 %collective-permute-start.10 = (bf16[2,4,1024]{2,1,0:T(4,128)(2,1)S(1)}, bf16[2,4,1024]{2,1,0:T(4,128)(2,1)S(1)}, u32[]{:S(2)}, u32[]{:S(2)}) collective-permute-start(bf16[2,4,1024]{2,1,0:T(4,128)(2,1)S(1)} %get-tuple-element.28), channel_id=1, source_target_pairs={{0,4},{1,2},{2,0},{3,1},{4,5},{5,6},{6,7},{7,3},{8,12},{9,10},{10,... | collective-permute-start | bytes 49160 | tf_op jit(solution)/shard_map/ppermute | solution.py:460
  21.6 4.0 %collective-permute-start.11 = (bf16[2,4,1024]{2,1,0:T(4,128)(2,1)S(1)}, bf16[2,4,1024]{2,1,0:T(4,128)(2,1)S(1)}, u32[]{:S(2)}, u32[]{:S(2)}) collective-permute-start(bf16[2,4,1024]{2,1,0:T(4,128)(2,1)S(1)} %get-tuple-element.29), channel_id=1, source_target_pairs={{0,3},{1,0},{2,6},{3,2},{4,7},{5,1},{6,4},{7,5},{8,11},{9,8},{10,1... | collective-permute-start | bytes 49160 | tf_op jit(solution)/shard_map/ppermute | solution.py:460
  23.3 2.4 %collective-permute-start.12 = (bf16[2,4,1024]{2,1,0:T(4,128)(2,1)S(1)}, bf16[2,4,1024]{2,1,0:T(4,128)(2,1)S(1)}, u32[]{:S(2)}, u32[]{:S(2)}) collective-permute-start(bf16[2,4,1024]{2,1,0:T(4,128)(2,1)S(1)} %get-tuple-element.30), channel_id=1, source_target_pairs={{0,2},{1,3},{2,1},{3,7},{4,0},{5,4},{6,5},{7,6},{8,10},{9,11},{10,... | collective-permute-start | bytes 49160 | tf_op jit(solution)/shard_map/ppermute | solution.py:460

commit v5 on v4

--- a/solution.py
+++ b/solution.py
@@ -30,21 +30,6 @@
         piece = q_ref[slot, :, j * HD : (j + 1) * HD]
         turned[j * steps : (j + 1) * steps, :] = piece.astype(jnp.float32)
     return turned[...].astype(jnp.bfloat16)
-
-
-def spread_heads(query, heads):
-    rows = query.shape[0]
-    row_head = lax.broadcasted_iota(jnp.int32, (rows, heads * HD), 0) // (rows // heads)
-    lane_head = lax.broadcasted_iota(jnp.int32, (rows, heads * HD), 1) // HD
-    wide = jnp.concatenate([query] * heads, axis=1)
-    return jnp.where(row_head == lane_head, wide, jnp.zeros_like(wide))
-
-
-def own_heads(weighted, heads):
-    span = weighted.shape[0] // heads
-    return jnp.concatenate(
-        [weighted[h * span : (h + 1) * span, h * HD : (h + 1) * HD] for h in range(heads)], axis=0
-    )
 
 
 def three_parts(x):
@@ -138,18 +123,15 @@
     )(*[pltpu.with_memory_space_constraint(x, pltpu.HBM) for x in operands])
 
 
-def page_masks(bits_ref, core, i, steps, page_bit):
-    masks = []
-    for h in range(bits_ref.shape[2]):
-        bits = jnp.concatenate([bits_ref[core, i, h]] * (page_bit.shape[1] // 128), axis=1)
-        masks += [(page_bit & bits) != 0] * steps
-    return jnp.concatenate(masks, axis=0)
-
-
-def attend(spread, pieces):
+def page_mask(bits_ref, core, i, h, steps, page_bit):
+    bits = jnp.concatenate([bits_ref[core, i, h]] * (page_bit.shape[1] // 128), axis=1)
+    return jnp.concatenate([(page_bit & bits) != 0] * steps, axis=0)
+
+
+def attend(query, pieces):
     found = []
     for keys, values, allowed in pieces:
-        scores = lax.dot_general(spread, keys, NT, preferred_element_type=jnp.float32)
+        scores = lax.dot_general(query, keys, NT, preferred_element_type=jnp.float32)
         found.append((jnp.where(allowed, scores * HD ** (-0.5), MASKED), values))
 
     def finish():
@@ -167,12 +149,13 @@
     return finish
 
 
-def page_pieces(kv_ref, where, bits_ref, core, i, steps, heads):
+def page_piece(kv_ref, where, bits_ref, core, i, h, steps):
     tokens = kv_ref.shape[1] * PAGE
     page_bit = jnp.left_shift(1, lax.broadcasted_iota(jnp.int32, (8, tokens), 1) // PAGE)
-    keys = kv_ref[where, :, 0].reshape(tokens, heads * HD)
-    values = kv_ref[where, :, 1].reshape(tokens, heads * HD)
-    return keys, values, page_masks(bits_ref, core, i, steps, page_bit)
+    lanes = slice(h * HD, (h + 1) * HD)
+    keys = kv_ref[where, :, 0, :, lanes].reshape(tokens, HD)
+    values = kv_ref[where, :, 1, :, lanes].reshape(tokens, HD)
+    return keys, values, page_mask(bits_ref, core, i, h, steps, page_bit)
 
 
 def staged(count, ahead, begin, end):
@@ -184,55 +167,67 @@
 
 
 def first_kernel(heads, bits_ref, new_ref, own_ref, *refs):
-    *q_refs, spread_ref, sum_ref, top_ref, total_ref, turned = refs
+    *q_refs, query_ref, sum_ref, top_ref, total_ref, turned = refs
     steps = q_refs[0].shape[1]
-    rows = turned.shape[1]
-
-    def begin(i):
-        spread = spread_heads(query_rows(q_refs[i], 0, turned.at[i]), heads)
-        spread_ref[i] = spread
-        pieces = [page_pieces(own_ref, i, bits_ref, 0, i, steps, heads)]
+    m, span = len(q_refs), steps * GROUPS
+
+    def begin(unit):
+        i, h = divmod(unit, heads)
+        rows = slice(h * span, (h + 1) * span)
+        if h == 0:
+            query_ref[i] = query_rows(q_refs[i], 0, turned.at[i])
+        query = turned[i, rows].astype(jnp.bfloat16)
+        pieces = [page_piece(own_ref, i, bits_ref, 0, i, h, steps)]
         if i == 0:
-            step_of = lax.broadcasted_iota(jnp.int32, (rows, 16), 0) % steps
-            causal = lax.broadcasted_iota(jnp.int32, (rows, 16), 1) <= step_of
-            pieces.append((new_ref[0], new_ref[1], causal))
-        return attend(spread, pieces)
-
-    def end(i, finish):
+            step_of = lax.broadcasted_iota(jnp.int32, (span, 16), 0) % steps
+            causal = lax.broadcasted_iota(jnp.int32, (span, 16), 1) <= step_of
+            lanes = slice(h * HD, (h + 1) * HD)
+            pieces.append((new_ref[0, :, lanes], new_ref[1, :, lanes], causal))
+        return attend(query, pieces)
+
+    def end(unit, finish):
+        i, h = divmod(unit, heads)
+        rows = slice(h * span, (h + 1) * span)
         top, total, weighted = finish()
-        top_ref[i] = jnp.broadcast_to(top, (rows, 128))
-        total_ref[i] = jnp.broadcast_to(total, (rows, 128))
-        sum_ref[i] = own_heads(weighted, heads)
-
-    staged(len(q_refs), 1, begin, end)
+        top_ref[i, rows] = jnp.broadcast_to(top, (span, 128))
+        total_ref[i, rows] = jnp.broadcast_to(total, (span, 128))
+        sum_ref[i, rows] = weighted
+
+    staged(m * heads, heads, begin, end)
 
 
 def second_kernel(
-    steps, heads, bits_ref, spread_ref, sum_ref, top_ref, total_ref, other_ref, out_ref
+    steps, heads, bits_ref, query_ref, sum_ref, top_ref, total_ref, other_ref, out_ref
 ):
-    m, rows = spread_ref.shape[:2]
+    m, rows = query_ref.shape[:2]
+    span = steps * GROUPS
     me = lax.axis_index("ctx")
-    columns = []
-
-    def begin(i):
-        pieces = [page_pieces(other_ref, me ^ (2 * i), bits_ref, 1, i, steps, heads)]
-        return attend(spread_ref[i], pieces)
-
-    def end(i, finish):
-        first_top, first_total = top_ref[i], total_ref[i]
+    logs = []
+
+    def begin(unit):
+        i, h = divmod(unit, heads)
+        piece = page_piece(other_ref, me ^ (2 * i), bits_ref, 1, i, h, steps)
+        return attend(query_ref[i, h * span : (h + 1) * span], [piece])
+
+    def end(unit, finish):
+        i, h = divmod(unit, heads)
+        own = slice(h * span, (h + 1) * span)
+        first_top, first_total = top_ref[i, own], total_ref[i, own]
         top, total, weighted = finish()
-        top = jnp.broadcast_to(top, (rows, 128))
+        top = jnp.broadcast_to(top, (span, 128))
         both = jnp.maximum(top, first_top)
         factor, first_factor = jnp.exp(top - both), jnp.exp(first_top - both)
-        total = jnp.broadcast_to(total, (rows, 128)) * factor + first_total * first_factor
+        total = jnp.broadcast_to(total, (span, 128)) * factor + first_total * first_factor
         total = jnp.where(total > 0.0, total, 1.0)
         share = 1.0 / total
-        joined = own_heads(weighted, heads) * (factor * share)
-        joined = joined + sum_ref[i] * (first_factor * share)
-        out_ref[i * rows : (i + 1) * rows, :] = joined.astype(jnp.bfloat16)
-        columns.append(both + jnp.log(total))
-
-    staged(m, m if m <= 4 else 2, begin, end)
+        joined = weighted * (factor * share) + sum_ref[i, own] * (first_factor * share)
+        first = i * rows + h * span
+        out_ref[first : first + span, :] = joined.astype(jnp.bfloat16)
+        logs.append(both + jnp.log(total))
+
+    count = m * heads
+    staged(count, count if count <= 8 else heads, begin, end)
+    columns = [jnp.concatenate(logs[i * heads : (i + 1) * heads], axis=0) for i in range(m)]
     out_ref[m * rows :, :] = stat_block(columns)
 
 
@@ -251,7 +246,7 @@
     state = pl.pallas_call(
         functools.partial(first_kernel, heads),
         out_shape=[
-            jax.ShapeDtypeStruct((m, rows, width), jnp.bfloat16),
+            jax.ShapeDtypeStruct((m, rows, HD), jnp.bfloat16),
             jax.ShapeDtypeStruct((m, rows, HD), jnp.float32),
             jax.ShapeDtypeStruct((m, rows, 128), jnp.float32),
             jax.ShapeDtypeStruct((m, rows, 128), jnp.float32),
@@ -309,9 +304,9 @@
         )
         high = weights.astype(jnp.bfloat16)
         low = (weights - high.astype(jnp.float32)).astype(jnp.bfloat16)
-        product = jnp.dot(high, parts, preferred_element_type=jnp.float32)
-        product = product + jnp.dot(low, parts, preferred_element_type=jnp.float32)
-        joined.append(product)
+        both = jnp.concatenate([high, low], axis=0)
+        product = jnp.dot(both, parts, preferred_element_type=jnp.float32)
+        joined.append(product[:rows] + product[rows:])
     for j in range(rows // steps):
         piece = jnp.concatenate([x[j * steps : (j + 1) * steps] for x in joined], axis=0)
         out_ref[:, j * HD : (j + 1) * HD] = piece.astype(jnp.bfloat16)

time: 26.7 us -> 26.7 us (level)
  no operation moved by 1% of the time
where the time goes in v5:
time: 26.7 us; the launch traced here: 26.2 us
  starting transfers between devices  12.8 us (48%)
  Pallas kernels  7.22 us (27%)
  waiting for transfers between devices  5.57 us (21%)
  other arithmetic  0.63 us (2%)
    ppermute x9, starting transfers between devices, swap(): return lax.ppermute(x, axis, [(i, i ^ r) for i in range(size)])  8.09 us
    ppermute x4, starting transfers between devices, send_by(): return lax.ppermute(x, ('ctx', 'head'), pairs)  4.68 us
    ppermute x9, waiting for transfers between devices, swap(): return lax.ppermute(x, axis, [(i, i ^ r) for i in range(size)])  3.62 us
    pallas_call x1, Pallas kernels, load_weight(): pl.pallas_call(load_kernel, out_shape=jax.ShapeDtypeStruct(out_weight.sha...  2.2 us
    ppermute x4, waiting for transfers between devices, send_by(): return lax.ppermute(x, ('ctx', 'head'), pairs)  1.94 us
    pallas_call x1, Pallas kernels, own_side(): pl.pallas_call(own_kernel, out_shape=[jax.ShapeDtypeStruct(queries.shape,...  1.63 us
    pallas_call x1, Pallas kernels, partials(): pl.pallas_call(functools.partial(first_kernel, heads), out_shape=[jax.Sha...  0.97 us
    pallas_call x1, Pallas kernels, partials(): pl.pallas_call(functools.partial(second_kernel, steps, heads), out_shape=...  0.78 us
  transfers between devices with their start and end apart: 13, of which 8 were waited for; matrix products, arithmetic and copies ran while one was open for 0% of the time, Pallas kernels for 21%

profile of v5, /device:TPU:0, one launch (start us, length us, event | category | flops | bytes accessed | tf_op | source)
XLA Modules:
  0.0 26.2 jit_solution(4470933057802973526)
XLA Ops:
  0.0 0.5 %collective-permute-start.3 = (bf16[8,8,2,64,256]{4,3,2,1,0:T(8,128)(2,1)}, bf16[8,8,2,64,256]{4,3,2,1,0:T(8,128)(2,1)S(1)}, u32[]{:S(2)}, u32[]{:S(2)}) collective-permute-start(bf16[8,8,2,64,256]{4,3,2,1,0:T(8,128)(2,1)} %kv_in.1), channel_id=1, source_target_pairs={{0,4},{4,0},{8,12},{12,8},{16,20},{20,16},{24,28},{28,24},{1,5},{5... | collective-permute-start | bytes 12582920 | tf_op jit(solution)/shard_map/ppermute | solution.py:460
  0.5 3.4 %collective-permute-start.2 = (bf16[1,4,2048]{2,1,0:T(4,128)(2,1)}, bf16[1,4,2048]{2,1,0:T(4,128)(2,1)S(1)}, u32[]{:S(2)}, u32[]{:S(2)}) collective-permute-start(bf16[1,4,2048]{2,1,0:T(4,128)(2,1)} %bitcast.2), channel_id=1, source_target_pairs={{0,24},{4,28},{8,16},{12,20},{16,8},{20,12},{24,0},{28,4},{1,25},{... | collective-permute-start | bytes 49160 | tf_op jit(solution)/shard_map/ppermute | solution.py:460
  3.9 0.5 %collective-permute-start.1 = (bf16[1,4,2048]{2,1,0:T(4,128)(2,1)}, bf16[1,4,2048]{2,1,0:T(4,128)(2,1)S(1)}, u32[]{:S(2)}, u32[]{:S(2)}) collective-permute-start(bf16[1,4,2048]{2,1,0:T(4,128)(2,1)} %bitcast.3), channel_id=1, source_target_pairs={{0,16},{4,20},{8,24},{12,28},{16,0},{20,4},{24,8},{28,12},{1,17},{... | collective-permute-start | bytes 49160 | tf_op jit(solution)/shard_map/ppermute | solution.py:460
  4.4 0.1 collective-permute-start
  4.5 1.6 %shard_map.55 = (bf16[1,4,2048]{2,1,0:T(4,128)(2,1)S(1)}, bf16[4,8,2,64,256]{4,3,2,1,0:T(8,128)(2,1)S(1)}, s32[2,4,2,8,128]{4,3,2,1,0:T(8,128)S(1)}, bf16[2,16,256]{2,1,0:T(8,128)(2,1)S(1)}) custom-call(bf16[1,4,2048]{2,1,0:T(4,128)(2,1)} %bitcast.5, bf16[8,8,2,64,256]{4,3,2,1,0:T(8,128)(2,1)} %kv_in.1, s32[4,8,2,8]{3,2,1,0:T(2,128)} %selected_in.1, ...), custom_call_target="tpu_custom_call" | custom-call | flops 1048576 | bytes 4194304 | tf_op jit(solution)/shard_map/pallas_call | solution.py:104
  6.2 0.0 collective-permute-done.2.refs_3_
  6.2 1.7 %collective-permute-done.1.refs_2_ = bf16[1,4,2048]{2,1,0:T(4,128)(2,1)S(1)} collective-permute-done((bf16[1,4,2048]{2,1,0:T(4,128)(2,1)}, bf16[1,4,2048]{2,1,0:T(4,128)(2,1)S(1)}, u32[]{:S(2)}, u32[]{:S(2)}) %collective-permute-start.1) | collective-permute-done | bytes 16416 | tf_op jit(solution)/shard_map/ppermute | solution.py:460
  7.8 0.5 %collective-permute-done.refs_1_ = bf16[1,4,2048]{2,1,0:T(4,128)(2,1)S(1)} collective-permute-done((bf16[1,4,2048]{2,1,0:T(4,128)(2,1)}, bf16[1,4,2048]{2,1,0:T(4,128)(2,1)S(1)}, u32[]{:S(2)}, u32[]{:S(2)}) %collective-permute-start) | collective-permute-done | bytes 16416 | tf_op jit(solution)/shard_map/ppermute | solution.py:460
  8.4 1.0 %shard_map.56 = (bf16[4,64,128]{2,1,0:T(8,128)(2,1)S(1)}, f32[4,64,128]{2,1,0:T(8,128)S(1)}, f32[4,64,128]{2,1,0:T(8,128)S(1)}, f32[4,64,128]{2,1,0:T(8,128)S(1)}) custom-call(s32[2,4,2,8,128]{4,3,2,1,0:T(8,128)S(1)} %get-tuple-element.18.bits_ref, bf16[2,16,256]{2,1,0:T(8,128)(2,1)S(1)} %get-tuple-element.19.new_ref, ...), custom_call_target="tpu_custom_call" | custom-call | flops 134217728 | bytes 1048576 | tf_op jit(solution)/shard_map/pallas_call | solution.py:246
  9.3 0.0 collective-permute-done.3.other_ref
  9.3 0.8 %shard_map.57._ = bf16[272,128]{1,0:T(8,128)(2,1)S(1)} custom-call(s32[2,4,2,8,128]{4,3,2,1,0:T(8,128)S(1)} %get-tuple-element.18.bits_ref, bf16[4,64,128]{2,1,0:T(8,128)(2,1)S(1)} %get-tuple-element.22.query_ref, f32[4,64,128]{2,1,0:T(8,128)S(1)} %get-tuple-element.23.sum_ref, f32[4,64,128]{2,1,0:T(8,128)S(1)} %get-tuple-element.24.top_ref, ...), custom_call_target="tpu_custom_call" | custom-call | flops 134217728 | bytes 1048576 | tf_op jit(solution)/shard_map/pallas_call | solution.py:259
  10.1 1.7 %collective-permute-start.7 = (bf16[272,128]{1,0:T(8,128)(2,1)S(1)}, bf16[272,128]{1,0:T(8,128)(2,1)S(1)}, u32[]{:S(2)}, u32[]{:S(2)}) collective-permute-start(bf16[272,128]{1,0:T(8,128)(2,1)S(1)} %shard_map.57._), channel_id=1, source_target_pairs={{0,28},{4,24},{8,20},{12,16},{16,12},{20,8},{24,4},{28,0},{1,29},{... | collective-permute-start | bytes 208904 | tf_op jit(solution)/shard_map/ppermute | solution.py:460
  11.8 0.5 %collective-permute-start.6 = (bf16[272,128]{1,0:T(8,128)(2,1)S(1)}, bf16[272,128]{1,0:T(8,128)(2,1)S(1)}, u32[]{:S(2)}, u32[]{:S(2)}) collective-permute-start(bf16[272,128]{1,0:T(8,128)(2,1)S(1)} %shard_map.57._), channel_id=1, source_target_pairs={{0,20},{4,16},{8,28},{12,24},{16,4},{20,0},{24,12},{28,8},{1,21},{... | collective-permute-start | bytes 208904 | tf_op jit(solution)/shard_map/ppermute | solution.py:460
  12.3 0.6 %collective-permute-start.5 = (bf16[272,128]{1,0:T(8,128)(2,1)S(1)}, bf16[272,128]{1,0:T(8,128)(2,1)S(1)}, u32[]{:S(2)}, u32[]{:S(2)}) collective-permute-start(bf16[272,128]{1,0:T(8,128)(2,1)S(1)} %shard_map.57._), channel_id=1, source_target_pairs={{0,12},{4,8},{8,4},{12,0},{16,28},{20,24},{24,20},{28,16},{1,13},{... | collective-permute-start | bytes 208904 | tf_op jit(solution)/shard_map/ppermute | solution.py:460
  12.9 0.6 %collective-permute-start.4 = (bf16[272,128]{1,0:T(8,128)(2,1)S(1)}, bf16[272,128]{1,0:T(8,128)(2,1)S(1)}, u32[]{:S(2)}, u32[]{:S(2)}) collective-permute-start(bf16[272,128]{1,0:T(8,128)(2,1)S(1)} %shard_map.57._), channel_id=1, source_target_pairs={{0,4},{4,0},{8,12},{12,8},{16,20},{20,16},{24,28},{28,24},{1,5},{5... | collective-permute-start | bytes 208904 | tf_op jit(solution)/shard_map/ppermute | solution.py:460
  13.5 2.2 %shard_map.58.refs_4_.weight_ref = bf16[2048,1024]{1,0:T(8,128)(2,1)S(1)} custom-call(bf16[2048,1024]{1,0:T(8,128)(2,1)} %weight_ref.1, bf16[272,128]{1,0:T(8,128)(2,1)S(1)} %shard_map.57._), custom_call_target="tpu_custom_call" | custom-call | bytes 8388608 | tf_op jit(solution)/shard_map/pallas_call | solution.py:342
  15.7 0.6 %collective-permute-done.6.refs_2_ = bf16[272,128]{1,0:T(8,128)(2,1)S(1)} collective-permute-done((bf16[272,128]{1,0:T(8,128)(2,1)S(1)}, bf16[272,128]{1,0:T(8,128)(2,1)S(1)}, u32[]{:S(2)}, u32[]{:S(2)}) %collective-permute-start.6) | collective-permute-done | bytes 69664 | tf_op jit(solution)/shard_map/ppermute | solution.py:460
  16.4 0.3 %collective-permute-done.5.refs_1_ = bf16[272,128]{1,0:T(8,128)(2,1)S(1)} collective-permute-done((bf16[272,128]{1,0:T(8,128)(2,1)S(1)}, bf16[272,128]{1,0:T(8,128)(2,1)S(1)}, u32[]{:S(2)}, u32[]{:S(2)}) %collective-permute-start.5) | collective-permute-done | bytes 69664 | tf_op jit(solution)/shard_map/ppermute | solution.py:460
  16.7 0.3 %shard_map.59.att_ref = bf16[16,2048]{1,0:T(8,128)(2,1)S(1)} custom-call(bf16[272,128]{1,0:T(8,128)(2,1)S(1)} %collective-permute-done.4.refs_0_, bf16[272,128]{1,0:T(8,128)(2,1)S(1)} %collective-permute-done.5.refs_1_, bf16[272,128]{1,0:T(8,128)(2,1)S(1)} %collective-permute-done.6.refs_2_, bf16[272,128]{1,0:T(8,128)(2,1)S(1)} %collective-permute-done.7.refs_3_, ...), custom_call_target="tpu_custom_call" | custom-call | flops 262144 | bytes 262144 | tf_op jit(solution)/shard_map/pallas_call | solution.py:317
  17.0 0.2 collective-permute-start.8
  17.2 0.6 %shard_map.60.half_ref = f32[16,1024]{1,0:T(8,128)S(1)} custom-call(bf16[16,2048]{1,0:T(8,128)(2,1)S(1)} %shard_map.59.att_ref, bf16[2048,1024]{1,0:T(8,128)(2,1)S(1)} %shard_map.58.refs_4_.weight_ref), custom_call_target="tpu_custom_call" | custom-call | flops 67108864 | bytes 4194304 | tf_op jit(solution)/shard_map/pallas_call | solution.py:392
  17.8 0.5 %collective-permute-done.8.att_ref = bf16[16,2048]{1,0:T(8,128)(2,1)S(1)} collective-permute-done((bf16[16,2048]{1,0:T(8,128)(2,1)S(1)}, bf16[16,2048]{1,0:T(8,128)(2,1)S(1)}, u32[]{:S(2)}, u32[]{:S(2)}) %collective-permute-start.8) | collective-permute-done | bytes 65568 | tf_op jit(solution)/shard_map/ppermute | solution.py:460
  18.3 0.7 %shard_map.61 = (f32[2,4,1024]{2,1,0:T(4,128)S(1)}, bf16[2,4,1024]{2,1,0:T(4,128)(2,1)S(1)}, bf16[2,4,1024]{2,1,0:T(4,128)(2,1)S(1)}, bf16[2,4,1024]{2,1,0:T(4,128)(2,1)S(1)}, bf16[2,4,1024]{2,1,0:T(4,128)(2,1)S(1)}) custom-call(bf16[16,2048]{1,0:T(8,128)(2,1)S(1)} %collective-permute-done.8.att_ref, f32[16,1024]{1,0:T(8,128)S(1)} %shard_map.60.half_ref, ...), custom_call_target="tpu_custom_call" | custom-call | flops 67108864 | bytes 4194304 | tf_op jit(solution)/shard_map/pallas_call | solution.py:408
  19.0 1.8 %collective-permute-start.9 = (bf16[2,4,1024]{2,1,0:T(4,128)(2,1)S(1)}, bf16[2,4,1024]{2,1,0:T(4,128)(2,1)S(1)}, u32[]{:S(2)}, u32[]{:S(2)}) collective-permute-start(bf16[2,4,1024]{2,1,0:T(4,128)(2,1)S(1)} %get-tuple-element.27), channel_id=1, source_target_pairs={{0,1},{1,5},{2,3},{3,0},{4,6},{5,7},{6,2},{7,4},{8,9},{9,13},{10,1... | collective-permute-start | bytes 49160 | tf_op jit(solution)/shard_map/ppermute | solution.py:455
  20.7 0.9 %collective-permute-start.10 = (bf16[2,4,1024]{2,1,0:T(4,128)(2,1)S(1)}, bf16[2,4,1024]{2,1,0:T(4,128)(2,1)S(1)}, u32[]{:S(2)}, u32[]{:S(2)}) collective-permute-start(bf16[2,4,1024]{2,1,0:T(4,128)(2,1)S(1)} %get-tuple-element.28), channel_id=1, source_target_pairs={{0,4},{1,2},{2,0},{3,1},{4,5},{5,6},{6,7},{7,3},{8,12},{9,10},{10,... | collective-permute-start | bytes 49160 | tf_op jit(solution)/shard_map/ppermute | solution.py:455
  21.6 1.6 %collective-permute-start.11 = (bf16[2,4,1024]{2,1,0:T(4,128)(2,1)S(1)}, bf16[2,4,1024]{2,1,0:T(4,128)(2,1)S(1)}, u32[]{:S(2)}, u32[]{:S(2)}) collective-permute-start(bf16[2,4,1024]{2,1,0:T(4,128)(2,1)S(1)} %get-tuple-element.29), channel_id=1, source_target_pairs={{0,3},{1,0},{2,6},{3,2},{4,7},{5,1},{6,4},{7,5},{8,11},{9,8},{10,1... | collective-permute-start | bytes 49160 | tf_op jit(solution)/shard_map/ppermute | solution.py:455
  23.3 0.4 %collective-permute-start.12 = (bf16[2,4,1024]{2,1,0:T(4,128)(2,1)S(1)}, bf16[2,4,1024]{2,1,0:T(4,128)(2,1)S(1)}, u32[]{:S(2)}, u32[]{:S(2)}) collective-permute-start(bf16[2,4,1024]{2,1,0:T(4,128)(2,1)S(1)} %get-tuple-element.30), channel_id=1, source_target_pairs={{0,2},{1,3},{2,1},{3,7},{4,0},{5,4},{6,5},{7,6},{8,10},{9,11},{10,... | collective-permute-start | bytes 49160 | tf_op jit(solution)/shard_map/ppermute | solution.py:455
  23.7 0.9 %collective-permute-done.9 = bf16[2,4,1024]{2,1,0:T(4,128)(2,1)S(1)} collective-permute-done((bf16[2,4,1024]{2,1,0:T(4,128)(2,1)S(1)}, bf16[2,4,1024]{2,1,0:T(4,128)(2,1)S(1)}, u32[]{:S(2)}, u32[]{:S(2)}) %collective-permute-start.9) | collective-permute-done | bytes 16416 | tf_op jit(solution)/shard_map/ppermute | solution.py:455
  24.6 0.8 %collective-permute-done.10 = bf16[2,4,1024]{2,1,0:T(4,128)(2,1)S(1)} collective-permute-done((bf16[2,4,1024]{2,1,0:T(4,128)(2,1)S(1)}, bf16[2,4,1024]{2,1,0:T(4,128)(2,1)S(1)}, u32[]{:S(2)}, u32[]{:S(2)}) %collective-permute-start.10) | collective-permute-done | bytes 16416 | tf_op jit(solution)/shard_map/ppermute | solution.py:455
  25.4 0.2 collective-permute-done.11
  25.6 0.0 collective-permute-done.12
  25.6 0.6 %add_convert_fusion = bf16[2,4,1024]{2,1,0:T(4,128)(2,1)} fusion(bf16[2,4,1024]{2,1,0:T(4,128)(2,1)S(1)} %collective-permute-done.12, bf16[2,4,1024]{2,1,0:T(4,128)(2,1)S(1)} %collective-permute-done.11, bf16[2,4,1024]{2,1,0:T(4,128)(2,1)S(1)} %collective-permute-done.10, f32[2,4,1024]{2,1,0:T(4,128)S(1)} %get-tuple-element.26, ...), kind=kLoop, calls=%fused_computation | loop fusion | flops 73728 | bytes 114688 | tf_op jit(solution)/shard_map/convert_element_type | solution.py:496
  (2 shorter events, 0.0 us)
Async XLA Ops:
  0.0 9.3 %collective-permute-start.3 = (bf16[8,8,2,64,256]{4,3,2,1,0:T(8,128)(2,1)}, bf16[8,8,2,64,256]{4,3,2,1,0:T(8,128)(2,1)S(1)}, u32[]{:S(2)}, u32[]{:S(2)}) collective-permute-start(bf16[8,8,2,64,256]{4,3,2,1,0:T(8,128)(2,1)} %kv_in.1), channel_id=1, source_target_pairs={{0,4},{4,0},{8,12},{12,8},{16,20},{20,16},{24,28},{28,24},{1,5},{5... | collective-permute-start | bytes 12582920 | tf_op jit(solution)/shard_map/ppermute | solution.py:460
  0.5 5.7 %collective-permute-start.2 = (bf16[1,4,2048]{2,1,0:T(4,128)(2,1)}, bf16[1,4,2048]{2,1,0:T(4,128)(2,1)S(1)}, u32[]{:S(2)}, u32[]{:S(2)}) collective-permute-start(bf16[1,4,2048]{2,1,0:T(4,128)(2,1)} %bitcast.2), channel_id=1, source_target_pairs={{0,24},{4,28},{8,16},{12,20},{16,8},{20,12},{24,0},{28,4},{1,25},{... | collective-permute-start | bytes 49160 | tf_op jit(solution)/shard_map/ppermute | solution.py:460
  3.9 3.9 %collective-permute-start.1 = (bf16[1,4,2048]{2,1,0:T(4,128)(2,1)}, bf16[1,4,2048]{2,1,0:T(4,128)(2,1)S(1)}, u32[]{:S(2)}, u32[]{:S(2)}) collective-permute-start(bf16[1,4,2048]{2,1,0:T(4,128)(2,1)} %bitcast.3), channel_id=1, source_target_pairs={{0,16},{4,20},{8,24},{12,28},{16,0},{20,4},{24,8},{28,12},{1,17},{... | collective-permute-start | bytes 49160 | tf_op jit(solution)/shard_map/ppermute | solution.py:460
  4.4 3.9 %collective-permute-start = (bf16[1,4,2048]{2,1,0:T(4,128)(2,1)}, bf16[1,4,2048]{2,1,0:T(4,128)(2,1)S(1)}, u32[]{:S(2)}, u32[]{:S(2)}) collective-permute-start(bf16[1,4,2048]{2,1,0:T(4,128)(2,1)} %bitcast.4), channel_id=1, source_target_pairs={{0,8},{4,12},{8,0},{12,4},{16,24},{20,28},{24,16},{28,20},{1,9},{5... | collective-permute-start | bytes 49160 | tf_op jit(solution)/shard_map/ppermute | solution.py:460
  10.1 5.6 %collective-permute-start.7 = (bf16[272,128]{1,0:T(8,128)(2,1)S(1)}, bf16[272,128]{1,0:T(8,128)(2,1)S(1)}, u32[]{:S(2)}, u32[]{:S(2)}) collective-permute-start(bf16[272,128]{1,0:T(8,128)(2,1)S(1)} %shard_map.57._), channel_id=1, source_target_pairs={{0,28},{4,24},{8,20},{12,16},{16,12},{20,8},{24,4},{28,0},{1,29},{... | collective-permute-start | bytes 208904 | tf_op jit(solution)/shard_map/ppermute | solution.py:460
  11.8 4.5 %collective-permute-start.6 = (bf16[272,128]{1,0:T(8,128)(2,1)S(1)}, bf16[272,128]{1,0:T(8,128)(2,1)S(1)}, u32[]{:S(2)}, u32[]{:S(2)}) collective-permute-start(bf16[272,128]{1,0:T(8,128)(2,1)S(1)} %shard_map.57._), channel_id=1, source_target_pairs={{0,20},{4,16},{8,28},{12,24},{16,4},{20,0},{24,12},{28,8},{1,21},{... | collective-permute-start | bytes 208904 | tf_op jit(solution)/shard_map/ppermute | solution.py:460
  12.3 4.4 %collective-permute-start.5 = (bf16[272,128]{1,0:T(8,128)(2,1)S(1)}, bf16[272,128]{1,0:T(8,128)(2,1)S(1)}, u32[]{:S(2)}, u32[]{:S(2)}) collective-permute-start(bf16[272,128]{1,0:T(8,128)(2,1)S(1)} %shard_map.57._), channel_id=1, source_target_pairs={{0,12},{4,8},{8,4},{12,0},{16,28},{20,24},{24,20},{28,16},{1,13},{... | collective-permute-start | bytes 208904 | tf_op jit(solution)/shard_map/ppermute | solution.py:460
  12.9 3.8 %collective-permute-start.4 = (bf16[272,128]{1,0:T(8,128)(2,1)S(1)}, bf16[272,128]{1,0:T(8,128)(2,1)S(1)}, u32[]{:S(2)}, u32[]{:S(2)}) collective-permute-start(bf16[272,128]{1,0:T(8,128)(2,1)S(1)} %shard_map.57._), channel_id=1, source_target_pairs={{0,4},{4,0},{8,12},{12,8},{16,20},{20,16},{24,28},{28,24},{1,5},{5... | collective-permute-start | bytes 208904 | tf_op jit(solution)/shard_map/ppermute | solution.py:460
  17.0 1.3 %collective-permute-start.8 = (bf16[16,2048]{1,0:T(8,128)(2,1)S(1)}, bf16[16,2048]{1,0:T(8,128)(2,1)S(1)}, u32[]{:S(2)}, u32[]{:S(2)}) collective-permute-start(bf16[16,2048]{1,0:T(8,128)(2,1)S(1)} %shard_map.59.att_ref), channel_id=1, source_target_pairs={{0,4},{4,0},{8,12},{12,8},{16,20},{20,16},{24,28},{28,24},{1,5},{5... | collective-permute-start | bytes 196616 | tf_op jit(solution)/shard_map/ppermute | solution.py:460
  19.0 5.6 %collective-permute-start.9 = (bf16[2,4,1024]{2,1,0:T(4,128)(2,1)S(1)}, bf16[2,4,1024]{2,1,0:T(4,128)(2,1)S(1)}, u32[]{:S(2)}, u32[]{:S(2)}) collective-permute-start(bf16[2,4,1024]{2,1,0:T(4,128)(2,1)S(1)} %get-tuple-element.27), channel_id=1, source_target_pairs={{0,1},{1,5},{2,3},{3,0},{4,6},{5,7},{6,2},{7,4},{8,9},{9,13},{10,1... | collective-permute-start | bytes 49160 | tf_op jit(solution)/shard_map/ppermute | solution.py:455
  20.7 4.6 %collective-permute-start.10 = (bf16[2,4,1024]{2,1,0:T(4,128)(2,1)S(1)}, bf16[2,4,1024]{2,1,0:T(4,128)(2,1)S(1)}, u32[]{:S(2)}, u32[]{:S(2)}) collective-permute-start(bf16[2,4,1024]{2,1,0:T(4,128)(2,1)S(1)} %get-tuple-element.28), channel_id=1, source_target_pairs={{0,4},{1,2},{2,0},{3,1},{4,5},{5,6},{6,7},{7,3},{8,12},{9,10},{10,... | collective-permute-start | bytes 49160 | tf_op jit(solution)/shard_map/ppermute | solution.py:455
  21.6 4.0 %collective-permute-start.11 = (bf16[2,4,1024]{2,1,0:T(4,128)(2,1)S(1)}, bf16[2,4,1024]{2,1,0:T(4,128)(2,1)S(1)}, u32[]{:S(2)}, u32[]{:S(2)}) collective-permute-start(bf16[2,4,1024]{2,1,0:T(4,128)(2,1)S(1)} %get-tuple-element.29), channel_id=1, source_target_pairs={{0,3},{1,0},{2,6},{3,2},{4,7},{5,1},{6,4},{7,5},{8,11},{9,8},{10,1... | collective-permute-start | bytes 49160 | tf_op jit(solution)/shard_map/ppermute | solution.py:455
  23.3 2.4 %collective-permute-start.12 = (bf16[2,4,1024]{2,1,0:T(4,128)(2,1)S(1)}, bf16[2,4,1024]{2,1,0:T(4,128)(2,1)S(1)}, u32[]{:S(2)}, u32[]{:S(2)}) collective-permute-start(bf16[2,4,1024]{2,1,0:T(4,128)(2,1)S(1)} %get-tuple-element.30), channel_id=1, source_target_pairs={{0,2},{1,3},{2,1},{3,7},{4,0},{5,4},{6,5},{7,6},{8,10},{9,11},{10,... | collective-permute-start | bytes 49160 | tf_op jit(solution)/shard_map/ppermute | solution.py:455

commit v6 on v4

--- a/solution.py
+++ b/solution.py
@@ -309,9 +309,9 @@
         )
         high = weights.astype(jnp.bfloat16)
         low = (weights - high.astype(jnp.float32)).astype(jnp.bfloat16)
-        product = jnp.dot(high, parts, preferred_element_type=jnp.float32)
-        product = product + jnp.dot(low, parts, preferred_element_type=jnp.float32)
-        joined.append(product)
+        both = jnp.concatenate([high, low], axis=0)
+        product = jnp.dot(both, parts, preferred_element_type=jnp.float32)
+        joined.append(product[:rows] + product[rows:])
     for j in range(rows // steps):
         piece = jnp.concatenate([x[j * steps : (j + 1) * steps] for x in joined], axis=0)
         out_ref[:, j * HD : (j + 1) * HD] = piece.astype(jnp.bfloat16)
@@ -423,10 +423,10 @@
 def head_plan(n_head):
     if n_head == 4:
         return [
-            (((0, 1), (1, 1), (0, 3), (0, 0)), ((1, 2), (1, 3), (0, 2), (1, 0))),
-            (((1, 0), (0, 2), (0, 0), (0, 1)), ((1, 1), (1, 2), (1, 3), (0, 3))),
-            (((0, 3), (0, 0), (1, 2), (0, 2)), ((1, 3), (0, 1), (1, 0), (1, 1))),
-            (((0, 2), (0, 3), (0, 1), (1, 3)), ((0, 0), (1, 0), (1, 1), (1, 2))),
+            (((1, 0), (1, 1), (0, 0), (1, 3)), ((1, 2), (0, 1), (0, 2), (0, 3))),
+            (((0, 1), (0, 2), (0, 3), (0, 0)), ((1, 1), (1, 3), (1, 0), (1, 2))),
+            (((0, 3), (0, 0), (0, 1), (0, 2)), ((1, 3), (1, 2), (1, 1), (1, 0))),
+            (((0, 2), (0, 3), (1, 2), (0, 1)), ((0, 0), (1, 0), (1, 3), (1, 1))),
         ]
     return [
         tuple(tuple((core, (z + t) % n_head) for z in range(n_head)) for core in range(2))

time: 26.7 us -> 26.3 us (0.985)
  waiting for transfers between devices: 5.62 us -> 5.12 us
  starting transfers between devices: 12.8 us -> 13.1 us
    ppermute x4, waiting for transfers between devices: 1.94 us -> 1.44 us  [send_by(): return lax.ppermute(x, ('ctx', 'head'), pairs)]
    ppermute x4, starting transfers between devices: 4.68 us -> 5 us  [send_by(): return lax.ppermute(x, ('ctx', 'head'), pairs)]
  transfers between devices with their start and end apart: 13 -> 13, of which waited for: 8 -> 7; matrix products, arithmetic and copies ran while one was open for 0% -> 0% of each run, Pallas kernels for 21% -> 21%
where the time goes in v6:
time: 26.3 us; the launch traced here: 26.1 us
  starting transfers between devices  13.1 us (50%)
  Pallas kernels  7.14 us (27%)
  waiting for transfers between devices  5.12 us (19%)
  other arithmetic  0.63 us (2%)
    ppermute x9, starting transfers between devices, swap(): return lax.ppermute(x, axis, [(i, i ^ r) for i in range(size)])  8.09 us
    ppermute x4, starting transfers between devices, send_by(): return lax.ppermute(x, ('ctx', 'head'), pairs)  5 us
    ppermute x9, waiting for transfers between devices, swap(): return lax.ppermute(x, axis, [(i, i ^ r) for i in range(size)])  3.68 us
    pallas_call x1, Pallas kernels, load_weight(): pl.pallas_call(load_kernel, out_shape=jax.ShapeDtypeStruct(out_weight.sha...  2.2 us
    pallas_call x1, Pallas kernels, own_side(): pl.pallas_call(own_kernel, out_shape=[jax.ShapeDtypeStruct(queries.shape,...  1.63 us
    ppermute x4, waiting for transfers between devices, send_by(): return lax.ppermute(x, ('ctx', 'head'), pairs)  1.44 us
    pallas_call x1, Pallas kernels, partials(): pl.pallas_call(functools.partial(first_kernel, heads), out_shape=[jax.Sha...  0.91 us
    pallas_call x1, Pallas kernels, partials(): pl.pallas_call(functools.partial(second_kernel, steps, heads), out_shape=...  0.76 us
  transfers between devices with their start and end apart: 13, of which 7 were waited for; matrix products, arithmetic and copies ran while one was open for 0% of the time, Pallas kernels for 21%

profile of v6, /device:TPU:0, one launch (start us, length us, event | category | flops | bytes accessed | tf_op | source)
XLA Modules:
  0.0 26.1 jit_solution(8386749940290660475)
XLA Ops:
  0.0 0.5 %collective-permute-start.3 = (bf16[8,8,2,64,256]{4,3,2,1,0:T(8,128)(2,1)}, bf16[8,8,2,64,256]{4,3,2,1,0:T(8,128)(2,1)S(1)}, u32[]{:S(2)}, u32[]{:S(2)}) collective-permute-start(bf16[8,8,2,64,256]{4,3,2,1,0:T(8,128)(2,1)} %kv_in.1), channel_id=1, source_target_pairs={{0,4},{4,0},{8,12},{12,8},{16,20},{20,16},{24,28},{28,24},{1,5},{5... | collective-permute-start | bytes 12582920 | tf_op jit(solution)/shard_map/ppermute | solution.py:465
  0.5 3.4 %collective-permute-start.2 = (bf16[1,4,2048]{2,1,0:T(4,128)(2,1)}, bf16[1,4,2048]{2,1,0:T(4,128)(2,1)S(1)}, u32[]{:S(2)}, u32[]{:S(2)}) collective-permute-start(bf16[1,4,2048]{2,1,0:T(4,128)(2,1)} %bitcast.2), channel_id=1, source_target_pairs={{0,24},{4,28},{8,16},{12,20},{16,8},{20,12},{24,0},{28,4},{1,25},{... | collective-permute-start | bytes 49160 | tf_op jit(solution)/shard_map/ppermute | solution.py:465
  3.9 0.5 %collective-permute-start.1 = (bf16[1,4,2048]{2,1,0:T(4,128)(2,1)}, bf16[1,4,2048]{2,1,0:T(4,128)(2,1)S(1)}, u32[]{:S(2)}, u32[]{:S(2)}) collective-permute-start(bf16[1,4,2048]{2,1,0:T(4,128)(2,1)} %bitcast.3), channel_id=1, source_target_pairs={{0,16},{4,20},{8,24},{12,28},{16,0},{20,4},{24,8},{28,12},{1,17},{... | collective-permute-start | bytes 49160 | tf_op jit(solution)/shard_map/ppermute | solution.py:465
  4.4 0.1 collective-permute-start
  4.5 1.6 %shard_map.55 = (bf16[1,4,2048]{2,1,0:T(4,128)(2,1)S(1)}, bf16[4,8,2,64,256]{4,3,2,1,0:T(8,128)(2,1)S(1)}, s32[2,4,2,8,128]{4,3,2,1,0:T(8,128)S(1)}, bf16[2,16,256]{2,1,0:T(8,128)(2,1)S(1)}) custom-call(bf16[1,4,2048]{2,1,0:T(4,128)(2,1)} %bitcast.5, bf16[8,8,2,64,256]{4,3,2,1,0:T(8,128)(2,1)} %kv_in.1, s32[4,8,2,8]{3,2,1,0:T(2,128)} %selected_in.1, ...), custom_call_target="tpu_custom_call" | custom-call | flops 1048576 | bytes 4194304 | tf_op jit(solution)/shard_map/pallas_call | solution.py:119
  6.2 0.0 collective-permute-done.2.refs_3_
  6.2 1.7 %collective-permute-done.1.refs_2_ = bf16[1,4,2048]{2,1,0:T(4,128)(2,1)S(1)} collective-permute-done((bf16[1,4,2048]{2,1,0:T(4,128)(2,1)}, bf16[1,4,2048]{2,1,0:T(4,128)(2,1)S(1)}, u32[]{:S(2)}, u32[]{:S(2)}) %collective-permute-start.1) | collective-permute-done | bytes 16416 | tf_op jit(solution)/shard_map/ppermute | solution.py:465
  7.8 0.5 %collective-permute-done.refs_1_ = bf16[1,4,2048]{2,1,0:T(4,128)(2,1)S(1)} collective-permute-done((bf16[1,4,2048]{2,1,0:T(4,128)(2,1)}, bf16[1,4,2048]{2,1,0:T(4,128)(2,1)S(1)}, u32[]{:S(2)}, u32[]{:S(2)}) %collective-permute-start) | collective-permute-done | bytes 16416 | tf_op jit(solution)/shard_map/ppermute | solution.py:465
  8.4 0.9 %shard_map.56 = (bf16[4,64,256]{2,1,0:T(8,128)(2,1)S(1)}, f32[4,64,128]{2,1,0:T(8,128)S(1)}, f32[4,64,128]{2,1,0:T(8,128)S(1)}, f32[4,64,128]{2,1,0:T(8,128)S(1)}) custom-call(s32[2,4,2,8,128]{4,3,2,1,0:T(8,128)S(1)} %get-tuple-element.18.bits_ref, bf16[2,16,256]{2,1,0:T(8,128)(2,1)S(1)} %get-tuple-element.19.new_ref, ...), custom_call_target="tpu_custom_call" | custom-call | flops 134217728 | bytes 1048576 | tf_op jit(solution)/shard_map/pallas_call | solution.py:251
  9.3 0.0 collective-permute-done.3.other_ref
  9.3 0.8 %shard_map.57._ = bf16[272,128]{1,0:T(8,128)(2,1)S(1)} custom-call(s32[2,4,2,8,128]{4,3,2,1,0:T(8,128)S(1)} %get-tuple-element.18.bits_ref, bf16[4,64,256]{2,1,0:T(8,128)(2,1)S(1)} %get-tuple-element.22.spread_ref, f32[4,64,128]{2,1,0:T(8,128)S(1)} %get-tuple-element.23.sum_ref, f32[4,64,128]{2,1,0:T(8,128)S(1)} %get-tuple-element.24.top_ref, ...), custom_call_target="tpu_custom_call" | custom-call | flops 134217728 | bytes 1048576 | tf_op jit(solution)/shard_map/pallas_call | solution.py:264
  10.0 1.8 %collective-permute-start.7 = (bf16[272,128]{1,0:T(8,128)(2,1)S(1)}, bf16[272,128]{1,0:T(8,128)(2,1)S(1)}, u32[]{:S(2)}, u32[]{:S(2)}) collective-permute-start(bf16[272,128]{1,0:T(8,128)(2,1)S(1)} %shard_map.57._), channel_id=1, source_target_pairs={{0,28},{4,24},{8,20},{12,16},{16,12},{20,8},{24,4},{28,0},{1,29},{... | collective-permute-start | bytes 208904 | tf_op jit(solution)/shard_map/ppermute | solution.py:465
  11.8 0.5 %collective-permute-start.6 = (bf16[272,128]{1,0:T(8,128)(2,1)S(1)}, bf16[272,128]{1,0:T(8,128)(2,1)S(1)}, u32[]{:S(2)}, u32[]{:S(2)}) collective-permute-start(bf16[272,128]{1,0:T(8,128)(2,1)S(1)} %shard_map.57._), channel_id=1, source_target_pairs={{0,20},{4,16},{8,28},{12,24},{16,4},{20,0},{24,12},{28,8},{1,21},{... | collective-permute-start | bytes 208904 | tf_op jit(solution)/shard_map/ppermute | solution.py:465
  12.3 0.5 %collective-permute-start.5 = (bf16[272,128]{1,0:T(8,128)(2,1)S(1)}, bf16[272,128]{1,0:T(8,128)(2,1)S(1)}, u32[]{:S(2)}, u32[]{:S(2)}) collective-permute-start(bf16[272,128]{1,0:T(8,128)(2,1)S(1)} %shard_map.57._), channel_id=1, source_target_pairs={{0,12},{4,8},{8,4},{12,0},{16,28},{20,24},{24,20},{28,16},{1,13},{... | collective-permute-start | bytes 208904 | tf_op jit(solution)/shard_map/ppermute | solution.py:465
  12.8 0.6 %collective-permute-start.4 = (bf16[272,128]{1,0:T(8,128)(2,1)S(1)}, bf16[272,128]{1,0:T(8,128)(2,1)S(1)}, u32[]{:S(2)}, u32[]{:S(2)}) collective-permute-start(bf16[272,128]{1,0:T(8,128)(2,1)S(1)} %shard_map.57._), channel_id=1, source_target_pairs={{0,4},{4,0},{8,12},{12,8},{16,20},{20,16},{24,28},{28,24},{1,5},{5... | collective-permute-start | bytes 208904 | tf_op jit(solution)/shard_map/ppermute | solution.py:465
  13.4 2.2 %shard_map.58.refs_4_.weight_ref = bf16[2048,1024]{1,0:T(8,128)(2,1)S(1)} custom-call(bf16[2048,1024]{1,0:T(8,128)(2,1)} %weight_ref.1, bf16[272,128]{1,0:T(8,128)(2,1)S(1)} %shard_map.57._), custom_call_target="tpu_custom_call" | custom-call | bytes 8388608 | tf_op jit(solution)/shard_map/pallas_call | solution.py:347
  15.6 0.0 collective-permute-done.7.refs_3_
  15.6 0.7 %collective-permute-done.6.refs_2_ = bf16[272,128]{1,0:T(8,128)(2,1)S(1)} collective-permute-done((bf16[272,128]{1,0:T(8,128)(2,1)S(1)}, bf16[272,128]{1,0:T(8,128)(2,1)S(1)}, u32[]{:S(2)}, u32[]{:S(2)}) %collective-permute-start.6) | collective-permute-done | bytes 69664 | tf_op jit(solution)/shard_map/ppermute | solution.py:465
  16.3 0.3 %collective-permute-done.5.refs_1_ = bf16[272,128]{1,0:T(8,128)(2,1)S(1)} collective-permute-done((bf16[272,128]{1,0:T(8,128)(2,1)S(1)}, bf16[272,128]{1,0:T(8,128)(2,1)S(1)}, u32[]{:S(2)}, u32[]{:S(2)}) %collective-permute-start.5) | collective-permute-done | bytes 69664 | tf_op jit(solution)/shard_map/ppermute | solution.py:465
  16.6 0.0 collective-permute-done.4.refs_0_
  16.7 0.3 %shard_map.59.att_ref = bf16[16,2048]{1,0:T(8,128)(2,1)S(1)} custom-call(bf16[272,128]{1,0:T(8,128)(2,1)S(1)} %collective-permute-done.4.refs_0_, bf16[272,128]{1,0:T(8,128)(2,1)S(1)} %collective-permute-done.5.refs_1_, bf16[272,128]{1,0:T(8,128)(2,1)S(1)} %collective-permute-done.6.refs_2_, bf16[272,128]{1,0:T(8,128)(2,1)S(1)} %collective-permute-done.7.refs_3_, ...), custom_call_target="tpu_custom_call" | custom-call | flops 262144 | bytes 262144 | tf_op jit(solution)/shard_map/pallas_call | solution.py:322
  17.0 0.2 collective-permute-start.8
  17.1 0.6 %shard_map.60.half_ref = f32[16,1024]{1,0:T(8,128)S(1)} custom-call(bf16[16,2048]{1,0:T(8,128)(2,1)S(1)} %shard_map.59.att_ref, bf16[2048,1024]{1,0:T(8,128)(2,1)S(1)} %shard_map.58.refs_4_.weight_ref), custom_call_target="tpu_custom_call" | custom-call | flops 67108864 | bytes 4194304 | tf_op jit(solution)/shard_map/pallas_call | solution.py:397
  17.8 0.5 %collective-permute-done.8.att_ref = bf16[16,2048]{1,0:T(8,128)(2,1)S(1)} collective-permute-done((bf16[16,2048]{1,0:T(8,128)(2,1)S(1)}, bf16[16,2048]{1,0:T(8,128)(2,1)S(1)}, u32[]{:S(2)}, u32[]{:S(2)}) %collective-permute-start.8) | collective-permute-done | bytes 65568 | tf_op jit(solution)/shard_map/ppermute | solution.py:465
  18.3 0.7 %shard_map.61 = (f32[2,4,1024]{2,1,0:T(4,128)S(1)}, bf16[2,4,1024]{2,1,0:T(4,128)(2,1)S(1)}, bf16[2,4,1024]{2,1,0:T(4,128)(2,1)S(1)}, bf16[2,4,1024]{2,1,0:T(4,128)(2,1)S(1)}, bf16[2,4,1024]{2,1,0:T(4,128)(2,1)S(1)}) custom-call(bf16[16,2048]{1,0:T(8,128)(2,1)S(1)} %collective-permute-done.8.att_ref, f32[16,1024]{1,0:T(8,128)S(1)} %shard_map.60.half_ref, ...), custom_call_target="tpu_custom_call" | custom-call | flops 67108864 | bytes 4194304 | tf_op jit(solution)/shard_map/pallas_call | solution.py:413
  19.0 0.2 collective-permute-start.9
  19.2 1.7 %collective-permute-start.10 = (bf16[2,4,1024]{2,1,0:T(4,128)(2,1)S(1)}, bf16[2,4,1024]{2,1,0:T(4,128)(2,1)S(1)}, u32[]{:S(2)}, u32[]{:S(2)}) collective-permute-start(bf16[2,4,1024]{2,1,0:T(4,128)(2,1)S(1)} %get-tuple-element.28), channel_id=1, source_target_pairs={{0,1},{1,2},{2,3},{3,0},{4,5},{5,7},{6,4},{7,6},{8,9},{9,10},{10,1... | collective-permute-start | bytes 49160 | tf_op jit(solution)/shard_map/ppermute | solution.py:460
  20.9 2.1 %collective-permute-start.11 = (bf16[2,4,1024]{2,1,0:T(4,128)(2,1)S(1)}, bf16[2,4,1024]{2,1,0:T(4,128)(2,1)S(1)}, u32[]{:S(2)}, u32[]{:S(2)}) collective-permute-start(bf16[2,4,1024]{2,1,0:T(4,128)(2,1)S(1)} %get-tuple-element.29), channel_id=1, source_target_pairs={{0,3},{1,0},{2,1},{3,2},{4,7},{5,6},{6,5},{7,4},{8,11},{9,8},{10,9... | collective-permute-start | bytes 49160 | tf_op jit(solution)/shard_map/ppermute | solution.py:460
  23.0 1.0 %collective-permute-start.12 = (bf16[2,4,1024]{2,1,0:T(4,128)(2,1)S(1)}, bf16[2,4,1024]{2,1,0:T(4,128)(2,1)S(1)}, u32[]{:S(2)}, u32[]{:S(2)}) collective-permute-start(bf16[2,4,1024]{2,1,0:T(4,128)(2,1)S(1)} %get-tuple-element.30), channel_id=1, source_target_pairs={{0,2},{1,3},{2,6},{3,1},{4,0},{5,4},{6,7},{7,5},{8,10},{9,11},{10,... | collective-permute-start | bytes 49160 | tf_op jit(solution)/shard_map/ppermute | solution.py:460
  24.0 0.8 %collective-permute-done.10 = bf16[2,4,1024]{2,1,0:T(4,128)(2,1)S(1)} collective-permute-done((bf16[2,4,1024]{2,1,0:T(4,128)(2,1)S(1)}, bf16[2,4,1024]{2,1,0:T(4,128)(2,1)S(1)}, u32[]{:S(2)}, u32[]{:S(2)}) %collective-permute-start.10) | collective-permute-done | bytes 16416 | tf_op jit(solution)/shard_map/ppermute | solution.py:460
  24.8 0.6 %collective-permute-done.12 = bf16[2,4,1024]{2,1,0:T(4,128)(2,1)S(1)} collective-permute-done((bf16[2,4,1024]{2,1,0:T(4,128)(2,1)S(1)}, bf16[2,4,1024]{2,1,0:T(4,128)(2,1)S(1)}, u32[]{:S(2)}, u32[]{:S(2)}) %collective-permute-start.12) | collective-permute-done | bytes 16416 | tf_op jit(solution)/shard_map/ppermute | solution.py:460
  25.4 0.6 %add_convert_fusion = bf16[2,4,1024]{2,1,0:T(4,128)(2,1)} fusion(bf16[2,4,1024]{2,1,0:T(4,128)(2,1)S(1)} %collective-permute-done.12, bf16[2,4,1024]{2,1,0:T(4,128)(2,1)S(1)} %collective-permute-done.11, bf16[2,4,1024]{2,1,0:T(4,128)(2,1)S(1)} %collective-permute-done.10, f32[2,4,1024]{2,1,0:T(4,128)S(1)} %get-tuple-element.26, ...), kind=kLoop, calls=%fused_computation | loop fusion | flops 73728 | bytes 114688 | tf_op jit(solution)/shard_map/convert_element_type | solution.py:501
  (2 shorter events, 0.0 us)
Async XLA Ops:
  0.0 9.3 %collective-permute-start.3 = (bf16[8,8,2,64,256]{4,3,2,1,0:T(8,128)(2,1)}, bf16[8,8,2,64,256]{4,3,2,1,0:T(8,128)(2,1)S(1)}, u32[]{:S(2)}, u32[]{:S(2)}) collective-permute-start(bf16[8,8,2,64,256]{4,3,2,1,0:T(8,128)(2,1)} %kv_in.1), channel_id=1, source_target_pairs={{0,4},{4,0},{8,12},{12,8},{16,20},{20,16},{24,28},{28,24},{1,5},{5... | collective-permute-start | bytes 12582920 | tf_op jit(solution)/shard_map/ppermute | solution.py:465
  0.5 5.7 %collective-permute-start.2 = (bf16[1,4,2048]{2,1,0:T(4,128)(2,1)}, bf16[1,4,2048]{2,1,0:T(4,128)(2,1)S(1)}, u32[]{:S(2)}, u32[]{:S(2)}) collective-permute-start(bf16[1,4,2048]{2,1,0:T(4,128)(2,1)} %bitcast.2), channel_id=1, source_target_pairs={{0,24},{4,28},{8,16},{12,20},{16,8},{20,12},{24,0},{28,4},{1,25},{... | collective-permute-start | bytes 49160 | tf_op jit(solution)/shard_map/ppermute | solution.py:465
  3.9 3.9 %collective-permute-start.1 = (bf16[1,4,2048]{2,1,0:T(4,128)(2,1)}, bf16[1,4,2048]{2,1,0:T(4,128)(2,1)S(1)}, u32[]{:S(2)}, u32[]{:S(2)}) collective-permute-start(bf16[1,4,2048]{2,1,0:T(4,128)(2,1)} %bitcast.3), channel_id=1, source_target_pairs={{0,16},{4,20},{8,24},{12,28},{16,0},{20,4},{24,8},{28,12},{1,17},{... | collective-permute-start | bytes 49160 | tf_op jit(solution)/shard_map/ppermute | solution.py:465
  4.4 3.9 %collective-permute-start = (bf16[1,4,2048]{2,1,0:T(4,128)(2,1)}, bf16[1,4,2048]{2,1,0:T(4,128)(2,1)S(1)}, u32[]{:S(2)}, u32[]{:S(2)}) collective-permute-start(bf16[1,4,2048]{2,1,0:T(4,128)(2,1)} %bitcast.4), channel_id=1, source_target_pairs={{0,8},{4,12},{8,0},{12,4},{16,24},{20,28},{24,16},{28,20},{1,9},{5... | collective-permute-start | bytes 49160 | tf_op jit(solution)/shard_map/ppermute | solution.py:465
  10.0 5.6 %collective-permute-start.7 = (bf16[272,128]{1,0:T(8,128)(2,1)S(1)}, bf16[272,128]{1,0:T(8,128)(2,1)S(1)}, u32[]{:S(2)}, u32[]{:S(2)}) collective-permute-start(bf16[272,128]{1,0:T(8,128)(2,1)S(1)} %shard_map.57._), channel_id=1, source_target_pairs={{0,28},{4,24},{8,20},{12,16},{16,12},{20,8},{24,4},{28,0},{1,29},{... | collective-permute-start | bytes 208904 | tf_op jit(solution)/shard_map/ppermute | solution.py:465
  11.8 4.5 %collective-permute-start.6 = (bf16[272,128]{1,0:T(8,128)(2,1)S(1)}, bf16[272,128]{1,0:T(8,128)(2,1)S(1)}, u32[]{:S(2)}, u32[]{:S(2)}) collective-permute-start(bf16[272,128]{1,0:T(8,128)(2,1)S(1)} %shard_map.57._), channel_id=1, source_target_pairs={{0,20},{4,16},{8,28},{12,24},{16,4},{20,0},{24,12},{28,8},{1,21},{... | collective-permute-start | bytes 208904 | tf_op jit(solution)/shard_map/ppermute | solution.py:465
  12.3 4.4 %collective-permute-start.5 = (bf16[272,128]{1,0:T(8,128)(2,1)S(1)}, bf16[272,128]{1,0:T(8,128)(2,1)S(1)}, u32[]{:S(2)}, u32[]{:S(2)}) collective-permute-start(bf16[272,128]{1,0:T(8,128)(2,1)S(1)} %shard_map.57._), channel_id=1, source_target_pairs={{0,12},{4,8},{8,4},{12,0},{16,28},{20,24},{24,20},{28,16},{1,13},{... | collective-permute-start | bytes 208904 | tf_op jit(solution)/shard_map/ppermute | solution.py:465
  12.8 3.8 %collective-permute-start.4 = (bf16[272,128]{1,0:T(8,128)(2,1)S(1)}, bf16[272,128]{1,0:T(8,128)(2,1)S(1)}, u32[]{:S(2)}, u32[]{:S(2)}) collective-permute-start(bf16[272,128]{1,0:T(8,128)(2,1)S(1)} %shard_map.57._), channel_id=1, source_target_pairs={{0,4},{4,0},{8,12},{12,8},{16,20},{20,16},{24,28},{28,24},{1,5},{5... | collective-permute-start | bytes 208904 | tf_op jit(solution)/shard_map/ppermute | solution.py:465
  17.0 1.3 %collective-permute-start.8 = (bf16[16,2048]{1,0:T(8,128)(2,1)S(1)}, bf16[16,2048]{1,0:T(8,128)(2,1)S(1)}, u32[]{:S(2)}, u32[]{:S(2)}) collective-permute-start(bf16[16,2048]{1,0:T(8,128)(2,1)S(1)} %shard_map.59.att_ref), channel_id=1, source_target_pairs={{0,4},{4,0},{8,12},{12,8},{16,20},{20,16},{24,28},{28,24},{1,5},{5... | collective-permute-start | bytes 196616 | tf_op jit(solution)/shard_map/ppermute | solution.py:465
  19.0 5.0 %collective-permute-start.9 = (bf16[2,4,1024]{2,1,0:T(4,128)(2,1)S(1)}, bf16[2,4,1024]{2,1,0:T(4,128)(2,1)S(1)}, u32[]{:S(2)}, u32[]{:S(2)}) collective-permute-start(bf16[2,4,1024]{2,1,0:T(4,128)(2,1)S(1)} %get-tuple-element.27), channel_id=1, source_target_pairs={{0,4},{1,5},{2,0},{3,7},{4,6},{5,1},{6,2},{7,3},{8,12},{9,13},{10,... | collective-permute-start | bytes 49160 | tf_op jit(solution)/shard_map/ppermute | solution.py:460
  19.2 5.6 %collective-permute-start.10 = (bf16[2,4,1024]{2,1,0:T(4,128)(2,1)S(1)}, bf16[2,4,1024]{2,1,0:T(4,128)(2,1)S(1)}, u32[]{:S(2)}, u32[]{:S(2)}) collective-permute-start(bf16[2,4,1024]{2,1,0:T(4,128)(2,1)S(1)} %get-tuple-element.28), channel_id=1, source_target_pairs={{0,1},{1,2},{2,3},{3,0},{4,5},{5,7},{6,4},{7,6},{8,9},{9,10},{10,1... | collective-permute-start | bytes 49160 | tf_op jit(solution)/shard_map/ppermute | solution.py:460
  20.9 3.9 %collective-permute-start.11 = (bf16[2,4,1024]{2,1,0:T(4,128)(2,1)S(1)}, bf16[2,4,1024]{2,1,0:T(4,128)(2,1)S(1)}, u32[]{:S(2)}, u32[]{:S(2)}) collective-permute-start(bf16[2,4,1024]{2,1,0:T(4,128)(2,1)S(1)} %get-tuple-element.29), channel_id=1, source_target_pairs={{0,3},{1,0},{2,1},{3,2},{4,7},{5,6},{6,5},{7,4},{8,11},{9,8},{10,9... | collective-permute-start | bytes 49160 | tf_op jit(solution)/shard_map/ppermute | solution.py:460
  23.0 2.4 %collective-permute-start.12 = (bf16[2,4,1024]{2,1,0:T(4,128)(2,1)S(1)}, bf16[2,4,1024]{2,1,0:T(4,128)(2,1)S(1)}, u32[]{:S(2)}, u32[]{:S(2)}) collective-permute-start(bf16[2,4,1024]{2,1,0:T(4,128)(2,1)S(1)} %get-tuple-element.30), channel_id=1, source_target_pairs={{0,2},{1,3},{2,6},{3,1},{4,0},{5,4},{6,7},{7,5},{8,10},{9,11},{10,... | collective-permute-start | bytes 49160 | tf_op jit(solution)/shard_map/ppermute | solution.py:460

commit v7 on v6

--- a/solution.py
+++ b/solution.py
@@ -420,6 +420,38 @@
     )(att, half, weight)
 
 
+def sum_kernel(own_ref, *refs):
+    *part_refs, out_ref, held, sems = refs
+    copies = []
+    for j in range(own_ref.shape[0]):
+        total = own_ref[j]
+        for ref in part_refs:
+            total = total + ref[j].astype(jnp.float32)
+        held[j] = total.astype(jnp.bfloat16)
+        copy = pltpu.make_async_copy(held.at[j], out_ref.at[j], sems.at[j])
+        copy.start()
+        copies.append(copy)
+    for copy in copies:
+        copy.wait()
+
+
+def sum_parts(own, parts):
+    return pl.pallas_call(
+        sum_kernel,
+        out_shape=jax.ShapeDtypeStruct(own.shape, jnp.bfloat16),
+        in_specs=[VMEM] * (1 + len(parts)),
+        out_specs=HBM,
+        scratch_shapes=[
+            pltpu.VMEM(own.shape, jnp.bfloat16),
+            pltpu.SemaphoreType.DMA((own.shape[0],)),
+        ],
+        compiler_params=pltpu.CompilerParams(vmem_limit_bytes=VMEM_LIMIT),
+        cost_estimate=pl.CostEstimate(
+            flops=own.size * len(parts), bytes_accessed=own.size * 8, transcendentals=0
+        ),
+    )(own, *parts)
+
+
 def head_plan(n_head):
     if n_head == 4:
         return [
@@ -493,12 +525,11 @@
     even_att = swap(odd_att, "ctx", 1)
     plan = head_plan(n_head)
     half = project_half(odd_att, weight)
-    total, *rows_out = project(
+    own_rows, *rows_out = project(
         even_att, half, weight, steps, n_head, plan_targets(plan)
     )
-    for chunk, permutation in zip(rows_out, plan):
-        total = total + send_by(permutation, chunk).astype(jnp.float32)
-    return total.astype(jnp.bfloat16)
+    got = [send_by(permutation, chunk) for chunk, permutation in zip(rows_out, plan)]
+    return sum_parts(own_rows, got)
 
 
 def solution(mesh):

time: 26.3 us -> 26.3 us (level)
  other arithmetic: 0.63 us -> 0 us
  Pallas kernels: 7.14 us -> 7.77 us
    pallas_call x0 -> x1, Pallas kernels: none -> 0.63 us  [sum_parts(): pl.pallas_call(sum_kernel, out_shape=jax.ShapeDtypeStruct(own.shape, jnp....]
    convert_element_type x1 -> x0, other arithmetic: 0.63 us -> none  [local(): return total.astype(jnp.bfloat16)]
where the time goes in v7:
time: 26.3 us; the launch traced here: 26.1 us
  starting transfers between devices  13.1 us (50%)
  Pallas kernels  7.77 us (30%)
  waiting for transfers between devices  5.12 us (19%)
    ppermute x9, starting transfers between devices, swap(): return lax.ppermute(x, axis, [(i, i ^ r) for i in range(size)])  8.09 us
    ppermute x4, starting transfers between devices, send_by(): return lax.ppermute(x, ('ctx', 'head'), pairs)  5 us
    ppermute x9, waiting for transfers between devices, swap(): return lax.ppermute(x, axis, [(i, i ^ r) for i in range(size)])  3.68 us
    pallas_call x1, Pallas kernels, load_weight(): pl.pallas_call(load_kernel, out_shape=jax.ShapeDtypeStruct(out_weight.sha...  2.2 us
    pallas_call x1, Pallas kernels, own_side(): pl.pallas_call(own_kernel, out_shape=[jax.ShapeDtypeStruct(queries.shape,...  1.63 us
    ppermute x4, waiting for transfers between devices, send_by(): return lax.ppermute(x, ('ctx', 'head'), pairs)  1.44 us
    pallas_call x1, Pallas kernels, partials(): pl.pallas_call(functools.partial(first_kernel, heads), out_shape=[jax.Sha...  0.91 us
    pallas_call x1, Pallas kernels, partials(): pl.pallas_call(functools.partial(second_kernel, steps, heads), out_shape=...  0.76 us
  transfers between devices with their start and end apart: 13, of which 7 were waited for; matrix products, arithmetic and copies ran while one was open for 0% of the time, Pallas kernels for 21%

profile of v7, /device:TPU:0, one launch (start us, length us, event | category | flops | bytes accessed | tf_op | source)
XLA Modules:
  0.0 26.1 jit_solution(1502809706977978412)
XLA Ops:
  0.0 0.5 %collective-permute-start.3 = (bf16[8,8,2,64,256]{4,3,2,1,0:T(8,128)(2,1)}, bf16[8,8,2,64,256]{4,3,2,1,0:T(8,128)(2,1)S(1)}, u32[]{:S(2)}, u32[]{:S(2)}) collective-permute-start(bf16[8,8,2,64,256]{4,3,2,1,0:T(8,128)(2,1)} %kv_in.1), channel_id=1, source_target_pairs={{0,4},{4,0},{8,12},{12,8},{16,20},{20,16},{24,28},{28,24},{1,5},{5... | collective-permute-start | bytes 12582920 | tf_op jit(solution)/shard_map/ppermute | solution.py:497
  0.5 3.4 %collective-permute-start.2 = (bf16[1,4,2048]{2,1,0:T(4,128)(2,1)}, bf16[1,4,2048]{2,1,0:T(4,128)(2,1)S(1)}, u32[]{:S(2)}, u32[]{:S(2)}) collective-permute-start(bf16[1,4,2048]{2,1,0:T(4,128)(2,1)} %bitcast.2), channel_id=1, source_target_pairs={{0,24},{4,28},{8,16},{12,20},{16,8},{20,12},{24,0},{28,4},{1,25},{... | collective-permute-start | bytes 49160 | tf_op jit(solution)/shard_map/ppermute | solution.py:497
  3.9 0.5 %collective-permute-start.1 = (bf16[1,4,2048]{2,1,0:T(4,128)(2,1)}, bf16[1,4,2048]{2,1,0:T(4,128)(2,1)S(1)}, u32[]{:S(2)}, u32[]{:S(2)}) collective-permute-start(bf16[1,4,2048]{2,1,0:T(4,128)(2,1)} %bitcast.3), channel_id=1, source_target_pairs={{0,16},{4,20},{8,24},{12,28},{16,0},{20,4},{24,8},{28,12},{1,17},{... | collective-permute-start | bytes 49160 | tf_op jit(solution)/shard_map/ppermute | solution.py:497
  4.4 0.1 collective-permute-start
  4.5 1.6 %shard_map.55 = (bf16[1,4,2048]{2,1,0:T(4,128)(2,1)S(1)}, bf16[4,8,2,64,256]{4,3,2,1,0:T(8,128)(2,1)S(1)}, s32[2,4,2,8,128]{4,3,2,1,0:T(8,128)S(1)}, bf16[2,16,256]{2,1,0:T(8,128)(2,1)S(1)}) custom-call(bf16[1,4,2048]{2,1,0:T(4,128)(2,1)} %bitcast.5, bf16[8,8,2,64,256]{4,3,2,1,0:T(8,128)(2,1)} %kv_in.1, s32[4,8,2,8]{3,2,1,0:T(2,128)} %selected_in.1, ...), custom_call_target="tpu_custom_call" | custom-call | flops 1048576 | bytes 4194304 | tf_op jit(solution)/shard_map/pallas_call | solution.py:119
  6.2 0.0 collective-permute-done.2.refs_3_
  6.2 1.7 %collective-permute-done.1.refs_2_ = bf16[1,4,2048]{2,1,0:T(4,128)(2,1)S(1)} collective-permute-done((bf16[1,4,2048]{2,1,0:T(4,128)(2,1)}, bf16[1,4,2048]{2,1,0:T(4,128)(2,1)S(1)}, u32[]{:S(2)}, u32[]{:S(2)}) %collective-permute-start.1) | collective-permute-done | bytes 16416 | tf_op jit(solution)/shard_map/ppermute | solution.py:497
  7.8 0.5 %collective-permute-done.refs_1_ = bf16[1,4,2048]{2,1,0:T(4,128)(2,1)S(1)} collective-permute-done((bf16[1,4,2048]{2,1,0:T(4,128)(2,1)}, bf16[1,4,2048]{2,1,0:T(4,128)(2,1)S(1)}, u32[]{:S(2)}, u32[]{:S(2)}) %collective-permute-start) | collective-permute-done | bytes 16416 | tf_op jit(solution)/shard_map/ppermute | solution.py:497
  8.4 0.9 %shard_map.56 = (bf16[4,64,256]{2,1,0:T(8,128)(2,1)S(1)}, f32[4,64,128]{2,1,0:T(8,128)S(1)}, f32[4,64,128]{2,1,0:T(8,128)S(1)}, f32[4,64,128]{2,1,0:T(8,128)S(1)}) custom-call(s32[2,4,2,8,128]{4,3,2,1,0:T(8,128)S(1)} %get-tuple-element.18.bits_ref, bf16[2,16,256]{2,1,0:T(8,128)(2,1)S(1)} %get-tuple-element.19.new_ref, ...), custom_call_target="tpu_custom_call" | custom-call | flops 134217728 | bytes 1048576 | tf_op jit(solution)/shard_map/pallas_call | solution.py:251
  9.3 0.0 collective-permute-done.3.other_ref
  9.3 0.8 %shard_map.57._ = bf16[272,128]{1,0:T(8,128)(2,1)S(1)} custom-call(s32[2,4,2,8,128]{4,3,2,1,0:T(8,128)S(1)} %get-tuple-element.18.bits_ref, bf16[4,64,256]{2,1,0:T(8,128)(2,1)S(1)} %get-tuple-element.22.spread_ref, f32[4,64,128]{2,1,0:T(8,128)S(1)} %get-tuple-element.23.sum_ref, f32[4,64,128]{2,1,0:T(8,128)S(1)} %get-tuple-element.24.top_ref, ...), custom_call_target="tpu_custom_call" | custom-call | flops 134217728 | bytes 1048576 | tf_op jit(solution)/shard_map/pallas_call | solution.py:264
  10.0 1.8 %collective-permute-start.7 = (bf16[272,128]{1,0:T(8,128)(2,1)S(1)}, bf16[272,128]{1,0:T(8,128)(2,1)S(1)}, u32[]{:S(2)}, u32[]{:S(2)}) collective-permute-start(bf16[272,128]{1,0:T(8,128)(2,1)S(1)} %shard_map.57._), channel_id=1, source_target_pairs={{0,28},{4,24},{8,20},{12,16},{16,12},{20,8},{24,4},{28,0},{1,29},{... | collective-permute-start | bytes 208904 | tf_op jit(solution)/shard_map/ppermute | solution.py:497
  11.8 0.5 %collective-permute-start.6 = (bf16[272,128]{1,0:T(8,128)(2,1)S(1)}, bf16[272,128]{1,0:T(8,128)(2,1)S(1)}, u32[]{:S(2)}, u32[]{:S(2)}) collective-permute-start(bf16[272,128]{1,0:T(8,128)(2,1)S(1)} %shard_map.57._), channel_id=1, source_target_pairs={{0,20},{4,16},{8,28},{12,24},{16,4},{20,0},{24,12},{28,8},{1,21},{... | collective-permute-start | bytes 208904 | tf_op jit(solution)/shard_map/ppermute | solution.py:497
  12.3 0.5 %collective-permute-start.5 = (bf16[272,128]{1,0:T(8,128)(2,1)S(1)}, bf16[272,128]{1,0:T(8,128)(2,1)S(1)}, u32[]{:S(2)}, u32[]{:S(2)}) collective-permute-start(bf16[272,128]{1,0:T(8,128)(2,1)S(1)} %shard_map.57._), channel_id=1, source_target_pairs={{0,12},{4,8},{8,4},{12,0},{16,28},{20,24},{24,20},{28,16},{1,13},{... | collective-permute-start | bytes 208904 | tf_op jit(solution)/shard_map/ppermute | solution.py:497
  12.8 0.6 %collective-permute-start.4 = (bf16[272,128]{1,0:T(8,128)(2,1)S(1)}, bf16[272,128]{1,0:T(8,128)(2,1)S(1)}, u32[]{:S(2)}, u32[]{:S(2)}) collective-permute-start(bf16[272,128]{1,0:T(8,128)(2,1)S(1)} %shard_map.57._), channel_id=1, source_target_pairs={{0,4},{4,0},{8,12},{12,8},{16,20},{20,16},{24,28},{28,24},{1,5},{5... | collective-permute-start | bytes 208904 | tf_op jit(solution)/shard_map/ppermute | solution.py:497
  13.4 2.2 %shard_map.58.refs_4_.weight_ref = bf16[2048,1024]{1,0:T(8,128)(2,1)S(1)} custom-call(bf16[2048,1024]{1,0:T(8,128)(2,1)} %weight_ref.1, bf16[272,128]{1,0:T(8,128)(2,1)S(1)} %shard_map.57._), custom_call_target="tpu_custom_call" | custom-call | bytes 8388608 | tf_op jit(solution)/shard_map/pallas_call | solution.py:347
  15.6 0.0 collective-permute-done.7.refs_3_
  15.6 0.7 %collective-permute-done.6.refs_2_ = bf16[272,128]{1,0:T(8,128)(2,1)S(1)} collective-permute-done((bf16[272,128]{1,0:T(8,128)(2,1)S(1)}, bf16[272,128]{1,0:T(8,128)(2,1)S(1)}, u32[]{:S(2)}, u32[]{:S(2)}) %collective-permute-start.6) | collective-permute-done | bytes 69664 | tf_op jit(solution)/shard_map/ppermute | solution.py:497
  16.3 0.3 %collective-permute-done.5.refs_1_ = bf16[272,128]{1,0:T(8,128)(2,1)S(1)} collective-permute-done((bf16[272,128]{1,0:T(8,128)(2,1)S(1)}, bf16[272,128]{1,0:T(8,128)(2,1)S(1)}, u32[]{:S(2)}, u32[]{:S(2)}) %collective-permute-start.5) | collective-permute-done | bytes 69664 | tf_op jit(solution)/shard_map/ppermute | solution.py:497
  16.7 0.3 %shard_map.59.att_ref = bf16[16,2048]{1,0:T(8,128)(2,1)S(1)} custom-call(bf16[272,128]{1,0:T(8,128)(2,1)S(1)} %collective-permute-done.4.refs_0_, bf16[272,128]{1,0:T(8,128)(2,1)S(1)} %collective-permute-done.5.refs_1_, bf16[272,128]{1,0:T(8,128)(2,1)S(1)} %collective-permute-done.6.refs_2_, bf16[272,128]{1,0:T(8,128)(2,1)S(1)} %collective-permute-done.7.refs_3_, ...), custom_call_target="tpu_custom_call" | custom-call | flops 262144 | bytes 262144 | tf_op jit(solution)/shard_map/pallas_call | solution.py:322
  17.0 0.2 collective-permute-start.8
  17.1 0.6 %shard_map.60.half_ref = f32[16,1024]{1,0:T(8,128)S(1)} custom-call(bf16[16,2048]{1,0:T(8,128)(2,1)S(1)} %shard_map.59.att_ref, bf16[2048,1024]{1,0:T(8,128)(2,1)S(1)} %shard_map.58.refs_4_.weight_ref), custom_call_target="tpu_custom_call" | custom-call | flops 67108864 | bytes 4194304 | tf_op jit(solution)/shard_map/pallas_call | solution.py:397
  17.8 0.5 %collective-permute-done.8.att_ref = bf16[16,2048]{1,0:T(8,128)(2,1)S(1)} collective-permute-done((bf16[16,2048]{1,0:T(8,128)(2,1)S(1)}, bf16[16,2048]{1,0:T(8,128)(2,1)S(1)}, u32[]{:S(2)}, u32[]{:S(2)}) %collective-permute-start.8) | collective-permute-done | bytes 65568 | tf_op jit(solution)/shard_map/ppermute | solution.py:497
  18.3 0.7 %shard_map.61 = (f32[2,4,1024]{2,1,0:T(4,128)S(1)}, bf16[2,4,1024]{2,1,0:T(4,128)(2,1)S(1)}, bf16[2,4,1024]{2,1,0:T(4,128)(2,1)S(1)}, bf16[2,4,1024]{2,1,0:T(4,128)(2,1)S(1)}, bf16[2,4,1024]{2,1,0:T(4,128)(2,1)S(1)}) custom-call(bf16[16,2048]{1,0:T(8,128)(2,1)S(1)} %collective-permute-done.8.att_ref, f32[16,1024]{1,0:T(8,128)S(1)} %shard_map.60.half_ref, ...), custom_call_target="tpu_custom_call" | custom-call | flops 67108864 | bytes 4194304 | tf_op jit(solution)/shard_map/pallas_call | solution.py:413
  19.0 0.2 collective-permute-start.9
  19.2 1.7 %collective-permute-start.10 = (bf16[2,4,1024]{2,1,0:T(4,128)(2,1)S(1)}, bf16[2,4,1024]{2,1,0:T(4,128)(2,1)S(1)}, u32[]{:S(2)}, u32[]{:S(2)}) collective-permute-start(bf16[2,4,1024]{2,1,0:T(4,128)(2,1)S(1)} %get-tuple-element.28), channel_id=1, source_target_pairs={{0,1},{1,2},{2,3},{3,0},{4,5},{5,7},{6,4},{7,6},{8,9},{9,10},{10,1... | collective-permute-start | bytes 49160 | tf_op jit(solution)/shard_map/ppermute | solution.py:492
  20.9 2.1 %collective-permute-start.11 = (bf16[2,4,1024]{2,1,0:T(4,128)(2,1)S(1)}, bf16[2,4,1024]{2,1,0:T(4,128)(2,1)S(1)}, u32[]{:S(2)}, u32[]{:S(2)}) collective-permute-start(bf16[2,4,1024]{2,1,0:T(4,128)(2,1)S(1)} %get-tuple-element.29), channel_id=1, source_target_pairs={{0,3},{1,0},{2,1},{3,2},{4,7},{5,6},{6,5},{7,4},{8,11},{9,8},{10,9... | collective-permute-start | bytes 49160 | tf_op jit(solution)/shard_map/ppermute | solution.py:492
  23.0 1.0 %collective-permute-start.12 = (bf16[2,4,1024]{2,1,0:T(4,128)(2,1)S(1)}, bf16[2,4,1024]{2,1,0:T(4,128)(2,1)S(1)}, u32[]{:S(2)}, u32[]{:S(2)}) collective-permute-start(bf16[2,4,1024]{2,1,0:T(4,128)(2,1)S(1)} %get-tuple-element.30), channel_id=1, source_target_pairs={{0,2},{1,3},{2,6},{3,1},{4,0},{5,4},{6,7},{7,5},{8,10},{9,11},{10,... | collective-permute-start | bytes 49160 | tf_op jit(solution)/shard_map/ppermute | solution.py:492
  24.0 0.0 collective-permute-done.9.refs_0_
  24.0 0.8 %collective-permute-done.10.refs_1_ = bf16[2,4,1024]{2,1,0:T(4,128)(2,1)S(1)} collective-permute-done((bf16[2,4,1024]{2,1,0:T(4,128)(2,1)S(1)}, bf16[2,4,1024]{2,1,0:T(4,128)(2,1)S(1)}, u32[]{:S(2)}, u32[]{:S(2)}) %collective-permute-start.10) | collective-permute-done | bytes 16416 | tf_op jit(solution)/shard_map/ppermute | solution.py:492
  24.8 0.6 %collective-permute-done.12.refs_3_ = bf16[2,4,1024]{2,1,0:T(4,128)(2,1)S(1)} collective-permute-done((bf16[2,4,1024]{2,1,0:T(4,128)(2,1)S(1)}, bf16[2,4,1024]{2,1,0:T(4,128)(2,1)S(1)}, u32[]{:S(2)}, u32[]{:S(2)}) %collective-permute-start.12) | collective-permute-done | bytes 16416 | tf_op jit(solution)/shard_map/ppermute | solution.py:492
  25.4 0.6 %shard_map.62 = bf16[2,4,1024]{2,1,0:T(4,128)(2,1)} custom-call(f32[2,4,1024]{2,1,0:T(4,128)S(1)} %get-tuple-element.26.own_ref, bf16[2,4,1024]{2,1,0:T(4,128)(2,1)S(1)} %collective-permute-done.9.refs_0_, bf16[2,4,1024]{2,1,0:T(4,128)(2,1)S(1)} %collective-permute-done.10.refs_1_, bf16[2,4,1024]{2,1,0:T(4,128)(2,1)S(1)} %collective-permute-done.11.refs_2_, ...), custom_call_target="tpu_custom_call" | custom-call | flops 32768 | bytes 65536 | tf_op jit(solution)/shard_map/pallas_call | solution.py:439
  (2 shorter events, 0.0 us)
Async XLA Ops:
  0.0 9.3 %collective-permute-start.3 = (bf16[8,8,2,64,256]{4,3,2,1,0:T(8,128)(2,1)}, bf16[8,8,2,64,256]{4,3,2,1,0:T(8,128)(2,1)S(1)}, u32[]{:S(2)}, u32[]{:S(2)}) collective-permute-start(bf16[8,8,2,64,256]{4,3,2,1,0:T(8,128)(2,1)} %kv_in.1), channel_id=1, source_target_pairs={{0,4},{4,0},{8,12},{12,8},{16,20},{20,16},{24,28},{28,24},{1,5},{5... | collective-permute-start | bytes 12582920 | tf_op jit(solution)/shard_map/ppermute | solution.py:497
  0.5 5.7 %collective-permute-start.2 = (bf16[1,4,2048]{2,1,0:T(4,128)(2,1)}, bf16[1,4,2048]{2,1,0:T(4,128)(2,1)S(1)}, u32[]{:S(2)}, u32[]{:S(2)}) collective-permute-start(bf16[1,4,2048]{2,1,0:T(4,128)(2,1)} %bitcast.2), channel_id=1, source_target_pairs={{0,24},{4,28},{8,16},{12,20},{16,8},{20,12},{24,0},{28,4},{1,25},{... | collective-permute-start | bytes 49160 | tf_op jit(solution)/shard_map/ppermute | solution.py:497
  3.9 3.9 %collective-permute-start.1 = (bf16[1,4,2048]{2,1,0:T(4,128)(2,1)}, bf16[1,4,2048]{2,1,0:T(4,128)(2,1)S(1)}, u32[]{:S(2)}, u32[]{:S(2)}) collective-permute-start(bf16[1,4,2048]{2,1,0:T(4,128)(2,1)} %bitcast.3), channel_id=1, source_target_pairs={{0,16},{4,20},{8,24},{12,28},{16,0},{20,4},{24,8},{28,12},{1,17},{... | collective-permute-start | bytes 49160 | tf_op jit(solution)/shard_map/ppermute | solution.py:497
  4.4 3.9 %collective-permute-start = (bf16[1,4,2048]{2,1,0:T(4,128)(2,1)}, bf16[1,4,2048]{2,1,0:T(4,128)(2,1)S(1)}, u32[]{:S(2)}, u32[]{:S(2)}) collective-permute-start(bf16[1,4,2048]{2,1,0:T(4,128)(2,1)} %bitcast.4), channel_id=1, source_target_pairs={{0,8},{4,12},{8,0},{12,4},{16,24},{20,28},{24,16},{28,20},{1,9},{5... | collective-permute-start | bytes 49160 | tf_op jit(solution)/shard_map/ppermute | solution.py:497
  10.0 5.6 %collective-permute-start.7 = (bf16[272,128]{1,0:T(8,128)(2,1)S(1)}, bf16[272,128]{1,0:T(8,128)(2,1)S(1)}, u32[]{:S(2)}, u32[]{:S(2)}) collective-permute-start(bf16[272,128]{1,0:T(8,128)(2,1)S(1)} %shard_map.57._), channel_id=1, source_target_pairs={{0,28},{4,24},{8,20},{12,16},{16,12},{20,8},{24,4},{28,0},{1,29},{... | collective-permute-start | bytes 208904 | tf_op jit(solution)/shard_map/ppermute | solution.py:497
  11.8 4.5 %collective-permute-start.6 = (bf16[272,128]{1,0:T(8,128)(2,1)S(1)}, bf16[272,128]{1,0:T(8,128)(2,1)S(1)}, u32[]{:S(2)}, u32[]{:S(2)}) collective-permute-start(bf16[272,128]{1,0:T(8,128)(2,1)S(1)} %shard_map.57._), channel_id=1, source_target_pairs={{0,20},{4,16},{8,28},{12,24},{16,4},{20,0},{24,12},{28,8},{1,21},{... | collective-permute-start | bytes 208904 | tf_op jit(solution)/shard_map/ppermute | solution.py:497
  12.3 4.4 %collective-permute-start.5 = (bf16[272,128]{1,0:T(8,128)(2,1)S(1)}, bf16[272,128]{1,0:T(8,128)(2,1)S(1)}, u32[]{:S(2)}, u32[]{:S(2)}) collective-permute-start(bf16[272,128]{1,0:T(8,128)(2,1)S(1)} %shard_map.57._), channel_id=1, source_target_pairs={{0,12},{4,8},{8,4},{12,0},{16,28},{20,24},{24,20},{28,16},{1,13},{... | collective-permute-start | bytes 208904 | tf_op jit(solution)/shard_map/ppermute | solution.py:497
  12.8 3.8 %collective-permute-start.4 = (bf16[272,128]{1,0:T(8,128)(2,1)S(1)}, bf16[272,128]{1,0:T(8,128)(2,1)S(1)}, u32[]{:S(2)}, u32[]{:S(2)}) collective-permute-start(bf16[272,128]{1,0:T(8,128)(2,1)S(1)} %shard_map.57._), channel_id=1, source_target_pairs={{0,4},{4,0},{8,12},{12,8},{16,20},{20,16},{24,28},{28,24},{1,5},{5... | collective-permute-start | bytes 208904 | tf_op jit(solution)/shard_map/ppermute | solution.py:497
  17.0 1.3 %collective-permute-start.8 = (bf16[16,2048]{1,0:T(8,128)(2,1)S(1)}, bf16[16,2048]{1,0:T(8,128)(2,1)S(1)}, u32[]{:S(2)}, u32[]{:S(2)}) collective-permute-start(bf16[16,2048]{1,0:T(8,128)(2,1)S(1)} %shard_map.59.att_ref), channel_id=1, source_target_pairs={{0,4},{4,0},{8,12},{12,8},{16,20},{20,16},{24,28},{28,24},{1,5},{5... | collective-permute-start | bytes 196616 | tf_op jit(solution)/shard_map/ppermute | solution.py:497
  19.0 5.0 %collective-permute-start.9 = (bf16[2,4,1024]{2,1,0:T(4,128)(2,1)S(1)}, bf16[2,4,1024]{2,1,0:T(4,128)(2,1)S(1)}, u32[]{:S(2)}, u32[]{:S(2)}) collective-permute-start(bf16[2,4,1024]{2,1,0:T(4,128)(2,1)S(1)} %get-tuple-element.27), channel_id=1, source_target_pairs={{0,4},{1,5},{2,0},{3,7},{4,6},{5,1},{6,2},{7,3},{8,12},{9,13},{10,... | collective-permute-start | bytes 49160 | tf_op jit(solution)/shard_map/ppermute | solution.py:492
  19.2 5.6 %collective-permute-start.10 = (bf16[2,4,1024]{2,1,0:T(4,128)(2,1)S(1)}, bf16[2,4,1024]{2,1,0:T(4,128)(2,1)S(1)}, u32[]{:S(2)}, u32[]{:S(2)}) collective-permute-start(bf16[2,4,1024]{2,1,0:T(4,128)(2,1)S(1)} %get-tuple-element.28), channel_id=1, source_target_pairs={{0,1},{1,2},{2,3},{3,0},{4,5},{5,7},{6,4},{7,6},{8,9},{9,10},{10,1... | collective-permute-start | bytes 49160 | tf_op jit(solution)/shard_map/ppermute | solution.py:492
  20.9 3.9 %collective-permute-start.11 = (bf16[2,4,1024]{2,1,0:T(4,128)(2,1)S(1)}, bf16[2,4,1024]{2,1,0:T(4,128)(2,1)S(1)}, u32[]{:S(2)}, u32[]{:S(2)}) collective-permute-start(bf16[2,4,1024]{2,1,0:T(4,128)(2,1)S(1)} %get-tuple-element.29), channel_id=1, source_target_pairs={{0,3},{1,0},{2,1},{3,2},{4,7},{5,6},{6,5},{7,4},{8,11},{9,8},{10,9... | collective-permute-start | bytes 49160 | tf_op jit(solution)/shard_map/ppermute | solution.py:492
  23.0 2.4 %collective-permute-start.12 = (bf16[2,4,1024]{2,1,0:T(4,128)(2,1)S(1)}, bf16[2,4,1024]{2,1,0:T(4,128)(2,1)S(1)}, u32[]{:S(2)}, u32[]{:S(2)}) collective-permute-start(bf16[2,4,1024]{2,1,0:T(4,128)(2,1)S(1)} %get-tuple-element.30), channel_id=1, source_target_pairs={{0,2},{1,3},{2,6},{3,1},{4,0},{5,4},{6,7},{7,5},{8,10},{9,11},{10,... | collective-permute-start | bytes 49160 | tf_op jit(solution)/shard_map/ppermute | solution.py:492

commit v8 on v6

--- a/solution.py
+++ b/solution.py
@@ -74,18 +74,17 @@
 
 
 def own_kernel(
-    q_in, kv_in, selected_in, new_in, q_out, kv_out, bits_out, new_out, selected_ref, new_ref, sems
+    kv_in, selected_in, new_ref, kv_out, bits_out, new_out, selected_ref, sems
 ):
     steps, _, heads, _ = selected_ref.shape
     m, pages = kv_out.shape[:2]
     me = lax.axis_index("ctx")
-    pairs = [(selected_in, selected_ref), (new_in, new_ref), (q_in, q_out)]
+    pairs = [(selected_in, selected_ref)]
     pairs += [(kv_in.at[me ^ (2 * i)], kv_out.at[i]) for i in range(m)]
     copies = [pltpu.make_async_copy(*pair, sems.at[i]) for i, pair in enumerate(pairs)]
     for copy in copies:
         copy.start()
-    for copy in copies[:2]:
-        copy.wait()
+    copies[0].wait()
     by_step = []
     for s in range(steps):
         lists = jnp.concatenate([selected_ref[s, me ^ (2 * i)] for i in range(m)], axis=0)
@@ -108,34 +107,32 @@
         tokens = [new_ref[s, part : part + 1].astype(jnp.float32) for s in range(steps)]
         blank = jnp.zeros((16 - steps, new_ref.shape[2]), jnp.float32)
         new_out[part] = jnp.concatenate(tokens + [blank], axis=0).astype(jnp.bfloat16)
-    for copy in copies[2:]:
+    for copy in copies[1:]:
         copy.wait()
 
 
-def own_side(queries, kv_cache, selected, new_kv):
+def own_side(kv_cache, selected, new_kv):
     batch, heads = selected.shape[1:3]
     m = batch // 2
-    operands = (queries, kv_cache, selected, new_kv)
+    operands = (kv_cache, selected)
     return pl.pallas_call(
         own_kernel,
         out_shape=[
-            jax.ShapeDtypeStruct(queries.shape, queries.dtype),
             jax.ShapeDtypeStruct((m,) + kv_cache.shape[1:], kv_cache.dtype),
             jax.ShapeDtypeStruct((2, m, heads, 8, 128), jnp.int32),
             jax.ShapeDtypeStruct((2, 16, new_kv.shape[2]), jnp.bfloat16),
         ],
-        in_specs=[HBM] * 4,
-        out_specs=[VMEM] * 4,
+        in_specs=[HBM, HBM, VMEM],
+        out_specs=[VMEM] * 3,
         scratch_shapes=[
             pltpu.VMEM(selected.shape, selected.dtype),
-            pltpu.VMEM(new_kv.shape, new_kv.dtype),
-            pltpu.SemaphoreType.DMA((3 + m,)),
+            pltpu.SemaphoreType.DMA((1 + m,)),
         ],
         compiler_params=pltpu.CompilerParams(vmem_limit_bytes=VMEM_LIMIT),
         cost_estimate=pl.CostEstimate(
             flops=2**20, bytes_accessed=kv_cache.size * 2, transcendentals=0
         ),
-    )(*[pltpu.with_memory_space_constraint(x, pltpu.HBM) for x in operands])
+    )(*[pltpu.with_memory_space_constraint(x, pltpu.HBM) for x in operands], new_kv)
 
 
 def page_masks(bits_ref, core, i, steps, page_bit):
@@ -484,8 +481,8 @@
     other_kv = swap(kv_cache, "ctx", 1)
     far_q = swap_chips(first_q, n)
     new_pairs = new_kv.reshape(steps, 2, heads * HD)
-    own_q, own_kv, bits, new_pairs = own_side(first_q, kv_cache, selected, new_pairs)
-    all_q = [own_q] + far_q
+    own_kv, bits, new_pairs = own_side(kv_cache, selected, new_pairs)
+    all_q = [first_q] + far_q
     sent = partials(bits, new_pairs, own_kv, other_kv, all_q, rows, heads)
     parts = swap_other_cores(sent, n)
     weight = load_weight(out_weight, sent)

time: 26.3 us -> 26.4 us (level)
  waiting for transfers between devices: 5.12 us -> 4.39 us
  local copies, waits for them, and re-layouts: 0 us -> 0.69 us
    ppermute x9, waiting for transfers between devices: 3.68 us -> 2.95 us  [swap(): return lax.ppermute(x, axis, [(i, i ^ r) for i in range(size)])]
    unnamed x0 -> x4, local copies, waits for them, and re-layouts: none -> 0.69 us
  transfers between devices with their start and end apart: 13 -> 13, of which waited for: 7 -> 7; matrix products, arithmetic and copies ran while one was open for 0% -> 0% of each run, Pallas kernels for 21% -> 20%
where the time goes in v8:
time: 26.4 us; the launch traced here: 26.1 us
  starting transfers between devices  13.2 us (50%)
  Pallas kernels  7.09 us (27%)
  waiting for transfers between devices  4.39 us (17%)
  local copies, waits for them, and re-layouts  0.69 us (3%)
  other arithmetic  0.63 us (2%)
    ppermute x9, starting transfers between devices, swap(): return lax.ppermute(x, axis, [(i, i ^ r) for i in range(size)])  8.17 us
    ppermute x4, starting transfers between devices, send_by(): return lax.ppermute(x, ('ctx', 'head'), pairs)  5 us
    ppermute x9, waiting for transfers between devices, swap(): return lax.ppermute(x, axis, [(i, i ^ r) for i in range(size)])  2.95 us
    pallas_call x1, Pallas kernels, load_weight(): pl.pallas_call(load_kernel, out_shape=jax.ShapeDtypeStruct(out_weight.sha...  2.2 us
    pallas_call x1, Pallas kernels, own_side(): pl.pallas_call(own_kernel, out_shape=[jax.ShapeDtypeStruct((m,) + kv_cach...  1.58 us
    ppermute x4, waiting for transfers between devices, send_by(): return lax.ppermute(x, ('ctx', 'head'), pairs)  1.44 us
    pallas_call x1, Pallas kernels, partials(): pl.pallas_call(functools.partial(first_kernel, heads), out_shape=[jax.Sha...  0.92 us
    pallas_call x1, Pallas kernels, partials(): pl.pallas_call(functools.partial(second_kernel, steps, heads), out_shape=...  0.76 us
  transfers between devices with their start and end apart: 13, of which 7 were waited for; matrix products, arithmetic and copies ran while one was open for 0% of the time, Pallas kernels for 20%

profile of v8, /device:TPU:0, one launch (start us, length us, event | category | flops | bytes accessed | tf_op | source)
XLA Modules:
  0.0 26.1 jit_solution(15430462675848819094)
XLA Ops:
  0.0 0.5 %collective-permute-start.3 = (bf16[8,8,2,64,256]{4,3,2,1,0:T(8,128)(2,1)}, bf16[8,8,2,64,256]{4,3,2,1,0:T(8,128)(2,1)S(1)}, u32[]{:S(2)}, u32[]{:S(2)}) collective-permute-start(bf16[8,8,2,64,256]{4,3,2,1,0:T(8,128)(2,1)} %kv_in.1), channel_id=1, source_target_pairs={{0,4},{4,0},{8,12},{12,8},{16,20},{20,16},{24,28},{28,24},{1,5},{5... | collective-permute-start | bytes 12582920 | tf_op jit(solution)/shard_map/ppermute | solution.py:462
  0.5 3.5 %collective-permute-start.2 = (bf16[1,4,2048]{2,1,0:T(4,128)(2,1)}, bf16[1,4,2048]{2,1,0:T(4,128)(2,1)S(1)}, u32[]{:S(2)}, u32[]{:S(2)}) collective-permute-start(bf16[1,4,2048]{2,1,0:T(4,128)(2,1)} %bitcast.2), channel_id=1, source_target_pairs={{0,24},{4,28},{8,16},{12,20},{16,8},{20,12},{24,0},{28,4},{1,25},{... | collective-permute-start | bytes 49160 | tf_op jit(solution)/shard_map/ppermute | solution.py:462
  4.0 0.5 %collective-permute-start.1 = (bf16[1,4,2048]{2,1,0:T(4,128)(2,1)}, bf16[1,4,2048]{2,1,0:T(4,128)(2,1)S(1)}, u32[]{:S(2)}, u32[]{:S(2)}) collective-permute-start(bf16[1,4,2048]{2,1,0:T(4,128)(2,1)} %bitcast.3), channel_id=1, source_target_pairs={{0,16},{4,20},{8,24},{12,28},{16,0},{20,4},{24,8},{28,12},{1,17},{... | collective-permute-start | bytes 49160 | tf_op jit(solution)/shard_map/ppermute | solution.py:462
  4.5 0.1 collective-permute-start
  4.6 0.7 %copy-done.1 = bf16[4,1,2,256]{3,2,1,0:T(2,128)(2,1)S(1)} copy-done((bf16[4,1,2,256]{3,2,1,0:T(2,128)(2,1)S(1)}, bf16[4,1,2,256]{3,2,1,0:T(2,128)(2,1)}, u32[]{:S(2)}) %copy-start.1) | copy-done | bytes 4120
  5.3 1.6 %shard_map.55 = (bf16[4,8,2,64,256]{4,3,2,1,0:T(8,128)(2,1)S(1)}, s32[2,4,2,8,128]{4,3,2,1,0:T(8,128)S(1)}, bf16[2,16,256]{2,1,0:T(8,128)(2,1)S(1)}) custom-call(bf16[8,8,2,64,256]{4,3,2,1,0:T(8,128)(2,1)} %kv_in.1, s32[4,8,2,8]{3,2,1,0:T(2,128)} %selected_in.1, bf16[4,2,256]{2,1,0:T(2,128)(2,1)S(1)} %bitcast.6), custom_call_target="tpu_custom_call" | custom-call | flops 1048576 | bytes 4194304 | tf_op jit(solution)/shard_map/pallas_call | solution.py:118
  6.9 0.0 collective-permute-done.2.refs_3_
  6.9 1.0 %collective-permute-done.1.refs_2_ = bf16[1,4,2048]{2,1,0:T(4,128)(2,1)S(1)} collective-permute-done((bf16[1,4,2048]{2,1,0:T(4,128)(2,1)}, bf16[1,4,2048]{2,1,0:T(4,128)(2,1)S(1)}, u32[]{:S(2)}, u32[]{:S(2)}) %collective-permute-start.1) | collective-permute-done | bytes 16416 | tf_op jit(solution)/shard_map/ppermute | solution.py:462
  7.9 0.5 %collective-permute-done.refs_1_ = bf16[1,4,2048]{2,1,0:T(4,128)(2,1)S(1)} collective-permute-done((bf16[1,4,2048]{2,1,0:T(4,128)(2,1)}, bf16[1,4,2048]{2,1,0:T(4,128)(2,1)S(1)}, u32[]{:S(2)}, u32[]{:S(2)}) %collective-permute-start) | collective-permute-done | bytes 16416 | tf_op jit(solution)/shard_map/ppermute | solution.py:462
  8.4 0.9 %shard_map.56 = (bf16[4,64,256]{2,1,0:T(8,128)(2,1)S(1)}, f32[4,64,128]{2,1,0:T(8,128)S(1)}, f32[4,64,128]{2,1,0:T(8,128)S(1)}, f32[4,64,128]{2,1,0:T(8,128)S(1)}) custom-call(s32[2,4,2,8,128]{4,3,2,1,0:T(8,128)S(1)} %get-tuple-element.17.bits_ref, bf16[2,16,256]{2,1,0:T(8,128)(2,1)S(1)} %get-tuple-element.18.new_ref, ...), custom_call_target="tpu_custom_call" | custom-call | flops 134217728 | bytes 1048576 | tf_op jit(solution)/shard_map/pallas_call | solution.py:248
  9.4 0.8 %shard_map.57._ = bf16[272,128]{1,0:T(8,128)(2,1)S(1)} custom-call(s32[2,4,2,8,128]{4,3,2,1,0:T(8,128)S(1)} %get-tuple-element.17.bits_ref, bf16[4,64,256]{2,1,0:T(8,128)(2,1)S(1)} %get-tuple-element.20.spread_ref, f32[4,64,128]{2,1,0:T(8,128)S(1)} %get-tuple-element.21.sum_ref, f32[4,64,128]{2,1,0:T(8,128)S(1)} %get-tuple-element.22.top_ref, ...), custom_call_target="tpu_custom_call" | custom-call | flops 134217728 | bytes 1048576 | tf_op jit(solution)/shard_map/pallas_call | solution.py:261
  10.1 1.7 %collective-permute-start.7 = (bf16[272,128]{1,0:T(8,128)(2,1)S(1)}, bf16[272,128]{1,0:T(8,128)(2,1)S(1)}, u32[]{:S(2)}, u32[]{:S(2)}) collective-permute-start(bf16[272,128]{1,0:T(8,128)(2,1)S(1)} %shard_map.57._), channel_id=1, source_target_pairs={{0,28},{4,24},{8,20},{12,16},{16,12},{20,8},{24,4},{28,0},{1,29},{... | collective-permute-start | bytes 208904 | tf_op jit(solution)/shard_map/ppermute | solution.py:462
  11.8 0.5 %collective-permute-start.6 = (bf16[272,128]{1,0:T(8,128)(2,1)S(1)}, bf16[272,128]{1,0:T(8,128)(2,1)S(1)}, u32[]{:S(2)}, u32[]{:S(2)}) collective-permute-start(bf16[272,128]{1,0:T(8,128)(2,1)S(1)} %shard_map.57._), channel_id=1, source_target_pairs={{0,20},{4,16},{8,28},{12,24},{16,4},{20,0},{24,12},{28,8},{1,21},{... | collective-permute-start | bytes 208904 | tf_op jit(solution)/shard_map/ppermute | solution.py:462
  12.3 0.6 %collective-permute-start.5 = (bf16[272,128]{1,0:T(8,128)(2,1)S(1)}, bf16[272,128]{1,0:T(8,128)(2,1)S(1)}, u32[]{:S(2)}, u32[]{:S(2)}) collective-permute-start(bf16[272,128]{1,0:T(8,128)(2,1)S(1)} %shard_map.57._), channel_id=1, source_target_pairs={{0,12},{4,8},{8,4},{12,0},{16,28},{20,24},{24,20},{28,16},{1,13},{... | collective-permute-start | bytes 208904 | tf_op jit(solution)/shard_map/ppermute | solution.py:462
  12.9 0.6 %collective-permute-start.4 = (bf16[272,128]{1,0:T(8,128)(2,1)S(1)}, bf16[272,128]{1,0:T(8,128)(2,1)S(1)}, u32[]{:S(2)}, u32[]{:S(2)}) collective-permute-start(bf16[272,128]{1,0:T(8,128)(2,1)S(1)} %shard_map.57._), channel_id=1, source_target_pairs={{0,4},{4,0},{8,12},{12,8},{16,20},{20,16},{24,28},{28,24},{1,5},{5... | collective-permute-start | bytes 208904 | tf_op jit(solution)/shard_map/ppermute | solution.py:462
  13.5 2.2 %shard_map.58.refs_4_.weight_ref = bf16[2048,1024]{1,0:T(8,128)(2,1)S(1)} custom-call(bf16[2048,1024]{1,0:T(8,128)(2,1)} %weight_ref.1, bf16[272,128]{1,0:T(8,128)(2,1)S(1)} %shard_map.57._), custom_call_target="tpu_custom_call" | custom-call | bytes 8388608 | tf_op jit(solution)/shard_map/pallas_call | solution.py:344
  15.7 0.6 %collective-permute-done.6.refs_2_ = bf16[272,128]{1,0:T(8,128)(2,1)S(1)} collective-permute-done((bf16[272,128]{1,0:T(8,128)(2,1)S(1)}, bf16[272,128]{1,0:T(8,128)(2,1)S(1)}, u32[]{:S(2)}, u32[]{:S(2)}) %collective-permute-start.6) | collective-permute-done | bytes 69664 | tf_op jit(solution)/shard_map/ppermute | solution.py:462
  16.3 0.3 %collective-permute-done.5.refs_1_ = bf16[272,128]{1,0:T(8,128)(2,1)S(1)} collective-permute-done((bf16[272,128]{1,0:T(8,128)(2,1)S(1)}, bf16[272,128]{1,0:T(8,128)(2,1)S(1)}, u32[]{:S(2)}, u32[]{:S(2)}) %collective-permute-start.5) | collective-permute-done | bytes 69664 | tf_op jit(solution)/shard_map/ppermute | solution.py:462
  16.7 0.0 collective-permute-done.4.refs_0_
  16.7 0.3 %shard_map.59.att_ref = bf16[16,2048]{1,0:T(8,128)(2,1)S(1)} custom-call(bf16[272,128]{1,0:T(8,128)(2,1)S(1)} %collective-permute-done.4.refs_0_, bf16[272,128]{1,0:T(8,128)(2,1)S(1)} %collective-permute-done.5.refs_1_, bf16[272,128]{1,0:T(8,128)(2,1)S(1)} %collective-permute-done.6.refs_2_, bf16[272,128]{1,0:T(8,128)(2,1)S(1)} %collective-permute-done.7.refs_3_, ...), custom_call_target="tpu_custom_call" | custom-call | flops 262144 | bytes 262144 | tf_op jit(solution)/shard_map/pallas_call | solution.py:319
  17.0 0.2 collective-permute-start.8
  17.1 0.6 %shard_map.60.half_ref = f32[16,1024]{1,0:T(8,128)S(1)} custom-call(bf16[16,2048]{1,0:T(8,128)(2,1)S(1)} %shard_map.59.att_ref, bf16[2048,1024]{1,0:T(8,128)(2,1)S(1)} %shard_map.58.refs_4_.weight_ref), custom_call_target="tpu_custom_call" | custom-call | flops 67108864 | bytes 4194304 | tf_op jit(solution)/shard_map/pallas_call | solution.py:394
  17.8 0.5 %collective-permute-done.8.att_ref = bf16[16,2048]{1,0:T(8,128)(2,1)S(1)} collective-permute-done((bf16[16,2048]{1,0:T(8,128)(2,1)S(1)}, bf16[16,2048]{1,0:T(8,128)(2,1)S(1)}, u32[]{:S(2)}, u32[]{:S(2)}) %collective-permute-start.8) | collective-permute-done | bytes 65568 | tf_op jit(solution)/shard_map/ppermute | solution.py:462
  18.3 0.7 %shard_map.61 = (f32[2,4,1024]{2,1,0:T(4,128)S(1)}, bf16[2,4,1024]{2,1,0:T(4,128)(2,1)S(1)}, bf16[2,4,1024]{2,1,0:T(4,128)(2,1)S(1)}, bf16[2,4,1024]{2,1,0:T(4,128)(2,1)S(1)}, bf16[2,4,1024]{2,1,0:T(4,128)(2,1)S(1)}) custom-call(bf16[16,2048]{1,0:T(8,128)(2,1)S(1)} %collective-permute-done.8.att_ref, f32[16,1024]{1,0:T(8,128)S(1)} %shard_map.60.half_ref, ...), custom_call_target="tpu_custom_call" | custom-call | flops 67108864 | bytes 4194304 | tf_op jit(solution)/shard_map/pallas_call | solution.py:410
  19.0 0.2 collective-permute-start.9
  19.2 1.7 %collective-permute-start.10 = (bf16[2,4,1024]{2,1,0:T(4,128)(2,1)S(1)}, bf16[2,4,1024]{2,1,0:T(4,128)(2,1)S(1)}, u32[]{:S(2)}, u32[]{:S(2)}) collective-permute-start(bf16[2,4,1024]{2,1,0:T(4,128)(2,1)S(1)} %get-tuple-element.26), channel_id=1, source_target_pairs={{0,1},{1,2},{2,3},{3,0},{4,5},{5,7},{6,4},{7,6},{8,9},{9,10},{10,1... | collective-permute-start | bytes 49160 | tf_op jit(solution)/shard_map/ppermute | solution.py:457
  20.9 2.1 %collective-permute-start.11 = (bf16[2,4,1024]{2,1,0:T(4,128)(2,1)S(1)}, bf16[2,4,1024]{2,1,0:T(4,128)(2,1)S(1)}, u32[]{:S(2)}, u32[]{:S(2)}) collective-permute-start(bf16[2,4,1024]{2,1,0:T(4,128)(2,1)S(1)} %get-tuple-element.27), channel_id=1, source_target_pairs={{0,3},{1,0},{2,1},{3,2},{4,7},{5,6},{6,5},{7,4},{8,11},{9,8},{10,9... | collective-permute-start | bytes 49160 | tf_op jit(solution)/shard_map/ppermute | solution.py:457
  23.0 1.0 %collective-permute-start.12 = (bf16[2,4,1024]{2,1,0:T(4,128)(2,1)S(1)}, bf16[2,4,1024]{2,1,0:T(4,128)(2,1)S(1)}, u32[]{:S(2)}, u32[]{:S(2)}) collective-permute-start(bf16[2,4,1024]{2,1,0:T(4,128)(2,1)S(1)} %get-tuple-element.28), channel_id=1, source_target_pairs={{0,2},{1,3},{2,6},{3,1},{4,0},{5,4},{6,7},{7,5},{8,10},{9,11},{10,... | collective-permute-start | bytes 49160 | tf_op jit(solution)/shard_map/ppermute | solution.py:457
  24.0 0.0 collective-permute-done.9
  24.0 0.8 %collective-permute-done.10 = bf16[2,4,1024]{2,1,0:T(4,128)(2,1)S(1)} collective-permute-done((bf16[2,4,1024]{2,1,0:T(4,128)(2,1)S(1)}, bf16[2,4,1024]{2,1,0:T(4,128)(2,1)S(1)}, u32[]{:S(2)}, u32[]{:S(2)}) %collective-permute-start.10) | collective-permute-done | bytes 16416 | tf_op jit(solution)/shard_map/ppermute | solution.py:457
  24.8 0.6 %collective-permute-done.12 = bf16[2,4,1024]{2,1,0:T(4,128)(2,1)S(1)} collective-permute-done((bf16[2,4,1024]{2,1,0:T(4,128)(2,1)S(1)}, bf16[2,4,1024]{2,1,0:T(4,128)(2,1)S(1)}, u32[]{:S(2)}, u32[]{:S(2)}) %collective-permute-start.12) | collective-permute-done | bytes 16416 | tf_op jit(solution)/shard_map/ppermute | solution.py:457
  25.4 0.6 %add_convert_fusion = bf16[2,4,1024]{2,1,0:T(4,128)(2,1)} fusion(bf16[2,4,1024]{2,1,0:T(4,128)(2,1)S(1)} %collective-permute-done.12, bf16[2,4,1024]{2,1,0:T(4,128)(2,1)S(1)} %collective-permute-done.11, bf16[2,4,1024]{2,1,0:T(4,128)(2,1)S(1)} %collective-permute-done.10, f32[2,4,1024]{2,1,0:T(4,128)S(1)} %get-tuple-element.24, ...), kind=kLoop, calls=%fused_computation | loop fusion | flops 73728 | bytes 114688 | tf_op jit(solution)/shard_map/convert_element_type | solution.py:498
  (6 shorter events, 0.0 us)
Async XLA Ops:
  0.0 8.4 %copy-start = (bf16[4,1,2048]{2,0,1:T(4,128)(2,1)S(1)}, bf16[4,1,2048]{2,0,1:T(4,128)(2,1)}, u32[]{:S(2)}) copy-start(bf16[4,1,2048]{2,0,1:T(4,128)(2,1)} %param.5) | copy-start | bytes 49156
  0.0 9.3 %collective-permute-start.3 = (bf16[8,8,2,64,256]{4,3,2,1,0:T(8,128)(2,1)}, bf16[8,8,2,64,256]{4,3,2,1,0:T(8,128)(2,1)S(1)}, u32[]{:S(2)}, u32[]{:S(2)}) collective-permute-start(bf16[8,8,2,64,256]{4,3,2,1,0:T(8,128)(2,1)} %kv_in.1), channel_id=1, source_target_pairs={{0,4},{4,0},{8,12},{12,8},{16,20},{20,16},{24,28},{28,24},{1,5},{5... | collective-permute-start | bytes 12582920 | tf_op jit(solution)/shard_map/ppermute | solution.py:462
  0.5 6.4 %collective-permute-start.2 = (bf16[1,4,2048]{2,1,0:T(4,128)(2,1)}, bf16[1,4,2048]{2,1,0:T(4,128)(2,1)S(1)}, u32[]{:S(2)}, u32[]{:S(2)}) collective-permute-start(bf16[1,4,2048]{2,1,0:T(4,128)(2,1)} %bitcast.2), channel_id=1, source_target_pairs={{0,24},{4,28},{8,16},{12,20},{16,8},{20,12},{24,0},{28,4},{1,25},{... | collective-permute-start | bytes 49160 | tf_op jit(solution)/shard_map/ppermute | solution.py:462
  4.0 3.9 %collective-permute-start.1 = (bf16[1,4,2048]{2,1,0:T(4,128)(2,1)}, bf16[1,4,2048]{2,1,0:T(4,128)(2,1)S(1)}, u32[]{:S(2)}, u32[]{:S(2)}) collective-permute-start(bf16[1,4,2048]{2,1,0:T(4,128)(2,1)} %bitcast.3), channel_id=1, source_target_pairs={{0,16},{4,20},{8,24},{12,28},{16,0},{20,4},{24,8},{28,12},{1,17},{... | collective-permute-start | bytes 49160 | tf_op jit(solution)/shard_map/ppermute | solution.py:462
  4.5 3.9 %collective-permute-start = (bf16[1,4,2048]{2,1,0:T(4,128)(2,1)}, bf16[1,4,2048]{2,1,0:T(4,128)(2,1)S(1)}, u32[]{:S(2)}, u32[]{:S(2)}) collective-permute-start(bf16[1,4,2048]{2,1,0:T(4,128)(2,1)} %bitcast.4), channel_id=1, source_target_pairs={{0,8},{4,12},{8,0},{12,4},{16,24},{20,28},{24,16},{28,20},{1,9},{5... | collective-permute-start | bytes 49160 | tf_op jit(solution)/shard_map/ppermute | solution.py:462
  4.6 0.7 %copy-start.1 = (bf16[4,1,2,256]{3,2,1,0:T(2,128)(2,1)S(1)}, bf16[4,1,2,256]{3,2,1,0:T(2,128)(2,1)}, u32[]{:S(2)}) copy-start(bf16[4,1,2,256]{3,2,1,0:T(2,128)(2,1)} %param.7) | copy-start | bytes 12292
  10.1 5.6 %collective-permute-start.7 = (bf16[272,128]{1,0:T(8,128)(2,1)S(1)}, bf16[272,128]{1,0:T(8,128)(2,1)S(1)}, u32[]{:S(2)}, u32[]{:S(2)}) collective-permute-start(bf16[272,128]{1,0:T(8,128)(2,1)S(1)} %shard_map.57._), channel_id=1, source_target_pairs={{0,28},{4,24},{8,20},{12,16},{16,12},{20,8},{24,4},{28,0},{1,29},{... | collective-permute-start | bytes 208904 | tf_op jit(solution)/shard_map/ppermute | solution.py:462
  11.8 4.5 %collective-permute-start.6 = (bf16[272,128]{1,0:T(8,128)(2,1)S(1)}, bf16[272,128]{1,0:T(8,128)(2,1)S(1)}, u32[]{:S(2)}, u32[]{:S(2)}) collective-permute-start(bf16[272,128]{1,0:T(8,128)(2,1)S(1)} %shard_map.57._), channel_id=1, source_target_pairs={{0,20},{4,16},{8,28},{12,24},{16,4},{20,0},{24,12},{28,8},{1,21},{... | collective-permute-start | bytes 208904 | tf_op jit(solution)/shard_map/ppermute | solution.py:462
  12.3 4.4 %collective-permute-start.5 = (bf16[272,128]{1,0:T(8,128)(2,1)S(1)}, bf16[272,128]{1,0:T(8,128)(2,1)S(1)}, u32[]{:S(2)}, u32[]{:S(2)}) collective-permute-start(bf16[272,128]{1,0:T(8,128)(2,1)S(1)} %shard_map.57._), channel_id=1, source_target_pairs={{0,12},{4,8},{8,4},{12,0},{16,28},{20,24},{24,20},{28,16},{1,13},{... | collective-permute-start | bytes 208904 | tf_op jit(solution)/shard_map/ppermute | solution.py:462
  12.9 3.8 %collective-permute-start.4 = (bf16[272,128]{1,0:T(8,128)(2,1)S(1)}, bf16[272,128]{1,0:T(8,128)(2,1)S(1)}, u32[]{:S(2)}, u32[]{:S(2)}) collective-permute-start(bf16[272,128]{1,0:T(8,128)(2,1)S(1)} %shard_map.57._), channel_id=1, source_target_pairs={{0,4},{4,0},{8,12},{12,8},{16,20},{20,16},{24,28},{28,24},{1,5},{5... | collective-permute-start | bytes 208904 | tf_op jit(solution)/shard_map/ppermute | solution.py:462
  17.0 1.3 %collective-permute-start.8 = (bf16[16,2048]{1,0:T(8,128)(2,1)S(1)}, bf16[16,2048]{1,0:T(8,128)(2,1)S(1)}, u32[]{:S(2)}, u32[]{:S(2)}) collective-permute-start(bf16[16,2048]{1,0:T(8,128)(2,1)S(1)} %shard_map.59.att_ref), channel_id=1, source_target_pairs={{0,4},{4,0},{8,12},{12,8},{16,20},{20,16},{24,28},{28,24},{1,5},{5... | collective-permute-start | bytes 196616 | tf_op jit(solution)/shard_map/ppermute | solution.py:462
  19.0 5.0 %collective-permute-start.9 = (bf16[2,4,1024]{2,1,0:T(4,128)(2,1)S(1)}, bf16[2,4,1024]{2,1,0:T(4,128)(2,1)S(1)}, u32[]{:S(2)}, u32[]{:S(2)}) collective-permute-start(bf16[2,4,1024]{2,1,0:T(4,128)(2,1)S(1)} %get-tuple-element.25), channel_id=1, source_target_pairs={{0,4},{1,5},{2,0},{3,7},{4,6},{5,1},{6,2},{7,3},{8,12},{9,13},{10,... | collective-permute-start | bytes 49160 | tf_op jit(solution)/shard_map/ppermute | solution.py:457
  19.2 5.6 %collective-permute-start.10 = (bf16[2,4,1024]{2,1,0:T(4,128)(2,1)S(1)}, bf16[2,4,1024]{2,1,0:T(4,128)(2,1)S(1)}, u32[]{:S(2)}, u32[]{:S(2)}) collective-permute-start(bf16[2,4,1024]{2,1,0:T(4,128)(2,1)S(1)} %get-tuple-element.26), channel_id=1, source_target_pairs={{0,1},{1,2},{2,3},{3,0},{4,5},{5,7},{6,4},{7,6},{8,9},{9,10},{10,1... | collective-permute-start | bytes 49160 | tf_op jit(solution)/shard_map/ppermute | solution.py:457
  20.9 3.9 %collective-permute-start.11 = (bf16[2,4,1024]{2,1,0:T(4,128)(2,1)S(1)}, bf16[2,4,1024]{2,1,0:T(4,128)(2,1)S(1)}, u32[]{:S(2)}, u32[]{:S(2)}) collective-permute-start(bf16[2,4,1024]{2,1,0:T(4,128)(2,1)S(1)} %get-tuple-element.27), channel_id=1, source_target_pairs={{0,3},{1,0},{2,1},{3,2},{4,7},{5,6},{6,5},{7,4},{8,11},{9,8},{10,9... | collective-permute-start | bytes 49160 | tf_op jit(solution)/shard_map/ppermute | solution.py:457
  23.0 2.4 %collective-permute-start.12 = (bf16[2,4,1024]{2,1,0:T(4,128)(2,1)S(1)}, bf16[2,4,1024]{2,1,0:T(4,128)(2,1)S(1)}, u32[]{:S(2)}, u32[]{:S(2)}) collective-permute-start(bf16[2,4,1024]{2,1,0:T(4,128)(2,1)S(1)} %get-tuple-element.28), channel_id=1, source_target_pairs={{0,2},{1,3},{2,6},{3,1},{4,0},{5,4},{6,7},{7,5},{8,10},{9,11},{10,... | collective-permute-start | bytes 49160 | tf_op jit(solution)/shard_map/ppermute | solution.py:457

commit v9 on v8

--- a/solution.py
+++ b/solution.py
@@ -104,7 +104,7 @@
                     bits = jnp.where(step_of == s, by_step[2 * s + core][row : row + 1], bits)
                 bits_out[core, i, h] = bits
     for part in range(2):
-        tokens = [new_ref[s, part : part + 1].astype(jnp.float32) for s in range(steps)]
+        tokens = [new_ref[s].astype(jnp.float32)[part : part + 1] for s in range(steps)]
         blank = jnp.zeros((16 - steps, new_ref.shape[2]), jnp.float32)
         new_out[part] = jnp.concatenate(tokens + [blank], axis=0).astype(jnp.bfloat16)
     for copy in copies[1:]:

time: 26.4 us -> 26.4 us (level)
  no operation moved by 1% of the time
where the time goes in v9:
time: 26.4 us; the launch traced here: 26.1 us
  starting transfers between devices  13.2 us (50%)
  Pallas kernels  7.09 us (27%)
  waiting for transfers between devices  4.39 us (17%)
  local copies, waits for them, and re-layouts  0.69 us (3%)
  other arithmetic  0.63 us (2%)
    ppermute x9, starting transfers between devices, swap(): return lax.ppermute(x, axis, [(i, i ^ r) for i in range(size)])  8.17 us
    ppermute x4, starting transfers between devices, send_by(): return lax.ppermute(x, ('ctx', 'head'), pairs)  5 us
    ppermute x9, waiting for transfers between devices, swap(): return lax.ppermute(x, axis, [(i, i ^ r) for i in range(size)])  2.95 us
    pallas_call x1, Pallas kernels, load_weight(): pl.pallas_call(load_kernel, out_shape=jax.ShapeDtypeStruct(out_weight.sha...  2.2 us
    pallas_call x1, Pallas kernels, own_side(): pl.pallas_call(own_kernel, out_shape=[jax.ShapeDtypeStruct((m,) + kv_cach...  1.58 us
    ppermute x4, waiting for transfers between devices, send_by(): return lax.ppermute(x, ('ctx', 'head'), pairs)  1.44 us
    pallas_call x1, Pallas kernels, partials(): pl.pallas_call(functools.partial(first_kernel, heads), out_shape=[jax.Sha...  0.92 us
    pallas_call x1, Pallas kernels, partials(): pl.pallas_call(functools.partial(second_kernel, steps, heads), out_shape=...  0.76 us
  transfers between devices with their start and end apart: 13, of which 7 were waited for; matrix products, arithmetic and copies ran while one was open for 0% of the time, Pallas kernels for 20%

profile of v9, /device:TPU:0, one launch (start us, length us, event | category | flops | bytes accessed | tf_op | source)
XLA Modules:
  0.0 26.1 jit_solution(15430462675848819094)
XLA Ops:
  0.0 0.5 %collective-permute-start.3 = (bf16[8,8,2,64,256]{4,3,2,1,0:T(8,128)(2,1)}, bf16[8,8,2,64,256]{4,3,2,1,0:T(8,128)(2,1)S(1)}, u32[]{:S(2)}, u32[]{:S(2)}) collective-permute-start(bf16[8,8,2,64,256]{4,3,2,1,0:T(8,128)(2,1)} %kv_in.1), channel_id=1, source_target_pairs={{0,4},{4,0},{8,12},{12,8},{16,20},{20,16},{24,28},{28,24},{1,5},{5... | collective-permute-start | bytes 12582920 | tf_op jit(solution)/shard_map/ppermute | solution.py:462
  0.5 3.5 %collective-permute-start.2 = (bf16[1,4,2048]{2,1,0:T(4,128)(2,1)}, bf16[1,4,2048]{2,1,0:T(4,128)(2,1)S(1)}, u32[]{:S(2)}, u32[]{:S(2)}) collective-permute-start(bf16[1,4,2048]{2,1,0:T(4,128)(2,1)} %bitcast.2), channel_id=1, source_target_pairs={{0,24},{4,28},{8,16},{12,20},{16,8},{20,12},{24,0},{28,4},{1,25},{... | collective-permute-start | bytes 49160 | tf_op jit(solution)/shard_map/ppermute | solution.py:462
  4.0 0.5 %collective-permute-start.1 = (bf16[1,4,2048]{2,1,0:T(4,128)(2,1)}, bf16[1,4,2048]{2,1,0:T(4,128)(2,1)S(1)}, u32[]{:S(2)}, u32[]{:S(2)}) collective-permute-start(bf16[1,4,2048]{2,1,0:T(4,128)(2,1)} %bitcast.3), channel_id=1, source_target_pairs={{0,16},{4,20},{8,24},{12,28},{16,0},{20,4},{24,8},{28,12},{1,17},{... | collective-permute-start | bytes 49160 | tf_op jit(solution)/shard_map/ppermute | solution.py:462
  4.5 0.1 collective-permute-start
  4.6 0.7 %copy-done.1 = bf16[4,1,2,256]{3,2,1,0:T(2,128)(2,1)S(1)} copy-done((bf16[4,1,2,256]{3,2,1,0:T(2,128)(2,1)S(1)}, bf16[4,1,2,256]{3,2,1,0:T(2,128)(2,1)}, u32[]{:S(2)}) %copy-start.1) | copy-done | bytes 4120
  5.3 1.6 %shard_map.55 = (bf16[4,8,2,64,256]{4,3,2,1,0:T(8,128)(2,1)S(1)}, s32[2,4,2,8,128]{4,3,2,1,0:T(8,128)S(1)}, bf16[2,16,256]{2,1,0:T(8,128)(2,1)S(1)}) custom-call(bf16[8,8,2,64,256]{4,3,2,1,0:T(8,128)(2,1)} %kv_in.1, s32[4,8,2,8]{3,2,1,0:T(2,128)} %selected_in.1, bf16[4,2,256]{2,1,0:T(2,128)(2,1)S(1)} %bitcast.6), custom_call_target="tpu_custom_call" | custom-call | flops 1048576 | bytes 4194304 | tf_op jit(solution)/shard_map/pallas_call | solution.py:118
  6.9 0.0 collective-permute-done.2.refs_3_
  6.9 1.0 %collective-permute-done.1.refs_2_ = bf16[1,4,2048]{2,1,0:T(4,128)(2,1)S(1)} collective-permute-done((bf16[1,4,2048]{2,1,0:T(4,128)(2,1)}, bf16[1,4,2048]{2,1,0:T(4,128)(2,1)S(1)}, u32[]{:S(2)}, u32[]{:S(2)}) %collective-permute-start.1) | collective-permute-done | bytes 16416 | tf_op jit(solution)/shard_map/ppermute | solution.py:462
  7.9 0.5 %collective-permute-done.refs_1_ = bf16[1,4,2048]{2,1,0:T(4,128)(2,1)S(1)} collective-permute-done((bf16[1,4,2048]{2,1,0:T(4,128)(2,1)}, bf16[1,4,2048]{2,1,0:T(4,128)(2,1)S(1)}, u32[]{:S(2)}, u32[]{:S(2)}) %collective-permute-start) | collective-permute-done | bytes 16416 | tf_op jit(solution)/shard_map/ppermute | solution.py:462
  8.4 0.9 %shard_map.56 = (bf16[4,64,256]{2,1,0:T(8,128)(2,1)S(1)}, f32[4,64,128]{2,1,0:T(8,128)S(1)}, f32[4,64,128]{2,1,0:T(8,128)S(1)}, f32[4,64,128]{2,1,0:T(8,128)S(1)}) custom-call(s32[2,4,2,8,128]{4,3,2,1,0:T(8,128)S(1)} %get-tuple-element.17.bits_ref, bf16[2,16,256]{2,1,0:T(8,128)(2,1)S(1)} %get-tuple-element.18.new_ref, ...), custom_call_target="tpu_custom_call" | custom-call | flops 134217728 | bytes 1048576 | tf_op jit(solution)/shard_map/pallas_call | solution.py:248
  9.4 0.8 %shard_map.57._ = bf16[272,128]{1,0:T(8,128)(2,1)S(1)} custom-call(s32[2,4,2,8,128]{4,3,2,1,0:T(8,128)S(1)} %get-tuple-element.17.bits_ref, bf16[4,64,256]{2,1,0:T(8,128)(2,1)S(1)} %get-tuple-element.20.spread_ref, f32[4,64,128]{2,1,0:T(8,128)S(1)} %get-tuple-element.21.sum_ref, f32[4,64,128]{2,1,0:T(8,128)S(1)} %get-tuple-element.22.top_ref, ...), custom_call_target="tpu_custom_call" | custom-call | flops 134217728 | bytes 1048576 | tf_op jit(solution)/shard_map/pallas_call | solution.py:261
  10.1 1.7 %collective-permute-start.7 = (bf16[272,128]{1,0:T(8,128)(2,1)S(1)}, bf16[272,128]{1,0:T(8,128)(2,1)S(1)}, u32[]{:S(2)}, u32[]{:S(2)}) collective-permute-start(bf16[272,128]{1,0:T(8,128)(2,1)S(1)} %shard_map.57._), channel_id=1, source_target_pairs={{0,28},{4,24},{8,20},{12,16},{16,12},{20,8},{24,4},{28,0},{1,29},{... | collective-permute-start | bytes 208904 | tf_op jit(solution)/shard_map/ppermute | solution.py:462
  11.8 0.5 %collective-permute-start.6 = (bf16[272,128]{1,0:T(8,128)(2,1)S(1)}, bf16[272,128]{1,0:T(8,128)(2,1)S(1)}, u32[]{:S(2)}, u32[]{:S(2)}) collective-permute-start(bf16[272,128]{1,0:T(8,128)(2,1)S(1)} %shard_map.57._), channel_id=1, source_target_pairs={{0,20},{4,16},{8,28},{12,24},{16,4},{20,0},{24,12},{28,8},{1,21},{... | collective-permute-start | bytes 208904 | tf_op jit(solution)/shard_map/ppermute | solution.py:462
  12.3 0.6 %collective-permute-start.5 = (bf16[272,128]{1,0:T(8,128)(2,1)S(1)}, bf16[272,128]{1,0:T(8,128)(2,1)S(1)}, u32[]{:S(2)}, u32[]{:S(2)}) collective-permute-start(bf16[272,128]{1,0:T(8,128)(2,1)S(1)} %shard_map.57._), channel_id=1, source_target_pairs={{0,12},{4,8},{8,4},{12,0},{16,28},{20,24},{24,20},{28,16},{1,13},{... | collective-permute-start | bytes 208904 | tf_op jit(solution)/shard_map/ppermute | solution.py:462
  12.9 0.6 %collective-permute-start.4 = (bf16[272,128]{1,0:T(8,128)(2,1)S(1)}, bf16[272,128]{1,0:T(8,128)(2,1)S(1)}, u32[]{:S(2)}, u32[]{:S(2)}) collective-permute-start(bf16[272,128]{1,0:T(8,128)(2,1)S(1)} %shard_map.57._), channel_id=1, source_target_pairs={{0,4},{4,0},{8,12},{12,8},{16,20},{20,16},{24,28},{28,24},{1,5},{5... | collective-permute-start | bytes 208904 | tf_op jit(solution)/shard_map/ppermute | solution.py:462
  13.5 2.2 %shard_map.58.refs_4_.weight_ref = bf16[2048,1024]{1,0:T(8,128)(2,1)S(1)} custom-call(bf16[2048,1024]{1,0:T(8,128)(2,1)} %weight_ref.1, bf16[272,128]{1,0:T(8,128)(2,1)S(1)} %shard_map.57._), custom_call_target="tpu_custom_call" | custom-call | bytes 8388608 | tf_op jit(solution)/shard_map/pallas_call | solution.py:344
  15.7 0.6 %collective-permute-done.6.refs_2_ = bf16[272,128]{1,0:T(8,128)(2,1)S(1)} collective-permute-done((bf16[272,128]{1,0:T(8,128)(2,1)S(1)}, bf16[272,128]{1,0:T(8,128)(2,1)S(1)}, u32[]{:S(2)}, u32[]{:S(2)}) %collective-permute-start.6) | collective-permute-done | bytes 69664 | tf_op jit(solution)/shard_map/ppermute | solution.py:462
  16.3 0.3 %collective-permute-done.5.refs_1_ = bf16[272,128]{1,0:T(8,128)(2,1)S(1)} collective-permute-done((bf16[272,128]{1,0:T(8,128)(2,1)S(1)}, bf16[272,128]{1,0:T(8,128)(2,1)S(1)}, u32[]{:S(2)}, u32[]{:S(2)}) %collective-permute-start.5) | collective-permute-done | bytes 69664 | tf_op jit(solution)/shard_map/ppermute | solution.py:462
  16.7 0.0 collective-permute-done.4.refs_0_
  16.7 0.3 %shard_map.59.att_ref = bf16[16,2048]{1,0:T(8,128)(2,1)S(1)} custom-call(bf16[272,128]{1,0:T(8,128)(2,1)S(1)} %collective-permute-done.4.refs_0_, bf16[272,128]{1,0:T(8,128)(2,1)S(1)} %collective-permute-done.5.refs_1_, bf16[272,128]{1,0:T(8,128)(2,1)S(1)} %collective-permute-done.6.refs_2_, bf16[272,128]{1,0:T(8,128)(2,1)S(1)} %collective-permute-done.7.refs_3_, ...), custom_call_target="tpu_custom_call" | custom-call | flops 262144 | bytes 262144 | tf_op jit(solution)/shard_map/pallas_call | solution.py:319
  17.0 0.2 collective-permute-start.8
  17.1 0.6 %shard_map.60.half_ref = f32[16,1024]{1,0:T(8,128)S(1)} custom-call(bf16[16,2048]{1,0:T(8,128)(2,1)S(1)} %shard_map.59.att_ref, bf16[2048,1024]{1,0:T(8,128)(2,1)S(1)} %shard_map.58.refs_4_.weight_ref), custom_call_target="tpu_custom_call" | custom-call | flops 67108864 | bytes 4194304 | tf_op jit(solution)/shard_map/pallas_call | solution.py:394
  17.8 0.5 %collective-permute-done.8.att_ref = bf16[16,2048]{1,0:T(8,128)(2,1)S(1)} collective-permute-done((bf16[16,2048]{1,0:T(8,128)(2,1)S(1)}, bf16[16,2048]{1,0:T(8,128)(2,1)S(1)}, u32[]{:S(2)}, u32[]{:S(2)}) %collective-permute-start.8) | collective-permute-done | bytes 65568 | tf_op jit(solution)/shard_map/ppermute | solution.py:462
  18.3 0.7 %shard_map.61 = (f32[2,4,1024]{2,1,0:T(4,128)S(1)}, bf16[2,4,1024]{2,1,0:T(4,128)(2,1)S(1)}, bf16[2,4,1024]{2,1,0:T(4,128)(2,1)S(1)}, bf16[2,4,1024]{2,1,0:T(4,128)(2,1)S(1)}, bf16[2,4,1024]{2,1,0:T(4,128)(2,1)S(1)}) custom-call(bf16[16,2048]{1,0:T(8,128)(2,1)S(1)} %collective-permute-done.8.att_ref, f32[16,1024]{1,0:T(8,128)S(1)} %shard_map.60.half_ref, ...), custom_call_target="tpu_custom_call" | custom-call | flops 67108864 | bytes 4194304 | tf_op jit(solution)/shard_map/pallas_call | solution.py:410
  19.0 0.2 collective-permute-start.9
  19.2 1.7 %collective-permute-start.10 = (bf16[2,4,1024]{2,1,0:T(4,128)(2,1)S(1)}, bf16[2,4,1024]{2,1,0:T(4,128)(2,1)S(1)}, u32[]{:S(2)}, u32[]{:S(2)}) collective-permute-start(bf16[2,4,1024]{2,1,0:T(4,128)(2,1)S(1)} %get-tuple-element.26), channel_id=1, source_target_pairs={{0,1},{1,2},{2,3},{3,0},{4,5},{5,7},{6,4},{7,6},{8,9},{9,10},{10,1... | collective-permute-start | bytes 49160 | tf_op jit(solution)/shard_map/ppermute | solution.py:457
  20.9 2.1 %collective-permute-start.11 = (bf16[2,4,1024]{2,1,0:T(4,128)(2,1)S(1)}, bf16[2,4,1024]{2,1,0:T(4,128)(2,1)S(1)}, u32[]{:S(2)}, u32[]{:S(2)}) collective-permute-start(bf16[2,4,1024]{2,1,0:T(4,128)(2,1)S(1)} %get-tuple-element.27), channel_id=1, source_target_pairs={{0,3},{1,0},{2,1},{3,2},{4,7},{5,6},{6,5},{7,4},{8,11},{9,8},{10,9... | collective-permute-start | bytes 49160 | tf_op jit(solution)/shard_map/ppermute | solution.py:457
  23.0 1.0 %collective-permute-start.12 = (bf16[2,4,1024]{2,1,0:T(4,128)(2,1)S(1)}, bf16[2,4,1024]{2,1,0:T(4,128)(2,1)S(1)}, u32[]{:S(2)}, u32[]{:S(2)}) collective-permute-start(bf16[2,4,1024]{2,1,0:T(4,128)(2,1)S(1)} %get-tuple-element.28), channel_id=1, source_target_pairs={{0,2},{1,3},{2,6},{3,1},{4,0},{5,4},{6,7},{7,5},{8,10},{9,11},{10,... | collective-permute-start | bytes 49160 | tf_op jit(solution)/shard_map/ppermute | solution.py:457
  24.0 0.0 collective-permute-done.9
  24.0 0.8 %collective-permute-done.10 = bf16[2,4,1024]{2,1,0:T(4,128)(2,1)S(1)} collective-permute-done((bf16[2,4,1024]{2,1,0:T(4,128)(2,1)S(1)}, bf16[2,4,1024]{2,1,0:T(4,128)(2,1)S(1)}, u32[]{:S(2)}, u32[]{:S(2)}) %collective-permute-start.10) | collective-permute-done | bytes 16416 | tf_op jit(solution)/shard_map/ppermute | solution.py:457
  24.8 0.6 %collective-permute-done.12 = bf16[2,4,1024]{2,1,0:T(4,128)(2,1)S(1)} collective-permute-done((bf16[2,4,1024]{2,1,0:T(4,128)(2,1)S(1)}, bf16[2,4,1024]{2,1,0:T(4,128)(2,1)S(1)}, u32[]{:S(2)}, u32[]{:S(2)}) %collective-permute-start.12) | collective-permute-done | bytes 16416 | tf_op jit(solution)/shard_map/ppermute | solution.py:457
  25.4 0.6 %add_convert_fusion = bf16[2,4,1024]{2,1,0:T(4,128)(2,1)} fusion(bf16[2,4,1024]{2,1,0:T(4,128)(2,1)S(1)} %collective-permute-done.12, bf16[2,4,1024]{2,1,0:T(4,128)(2,1)S(1)} %collective-permute-done.11, bf16[2,4,1024]{2,1,0:T(4,128)(2,1)S(1)} %collective-permute-done.10, f32[2,4,1024]{2,1,0:T(4,128)S(1)} %get-tuple-element.24, ...), kind=kLoop, calls=%fused_computation | loop fusion | flops 73728 | bytes 114688 | tf_op jit(solution)/shard_map/convert_element_type | solution.py:498
  (6 shorter events, 0.0 us)
Async XLA Ops:
  0.0 8.4 %copy-start = (bf16[4,1,2048]{2,0,1:T(4,128)(2,1)S(1)}, bf16[4,1,2048]{2,0,1:T(4,128)(2,1)}, u32[]{:S(2)}) copy-start(bf16[4,1,2048]{2,0,1:T(4,128)(2,1)} %param.5) | copy-start | bytes 49156
  0.0 9.3 %collective-permute-start.3 = (bf16[8,8,2,64,256]{4,3,2,1,0:T(8,128)(2,1)}, bf16[8,8,2,64,256]{4,3,2,1,0:T(8,128)(2,1)S(1)}, u32[]{:S(2)}, u32[]{:S(2)}) collective-permute-start(bf16[8,8,2,64,256]{4,3,2,1,0:T(8,128)(2,1)} %kv_in.1), channel_id=1, source_target_pairs={{0,4},{4,0},{8,12},{12,8},{16,20},{20,16},{24,28},{28,24},{1,5},{5... | collective-permute-start | bytes 12582920 | tf_op jit(solution)/shard_map/ppermute | solution.py:462
  0.5 6.4 %collective-permute-start.2 = (bf16[1,4,2048]{2,1,0:T(4,128)(2,1)}, bf16[1,4,2048]{2,1,0:T(4,128)(2,1)S(1)}, u32[]{:S(2)}, u32[]{:S(2)}) collective-permute-start(bf16[1,4,2048]{2,1,0:T(4,128)(2,1)} %bitcast.2), channel_id=1, source_target_pairs={{0,24},{4,28},{8,16},{12,20},{16,8},{20,12},{24,0},{28,4},{1,25},{... | collective-permute-start | bytes 49160 | tf_op jit(solution)/shard_map/ppermute | solution.py:462
  4.0 3.9 %collective-permute-start.1 = (bf16[1,4,2048]{2,1,0:T(4,128)(2,1)}, bf16[1,4,2048]{2,1,0:T(4,128)(2,1)S(1)}, u32[]{:S(2)}, u32[]{:S(2)}) collective-permute-start(bf16[1,4,2048]{2,1,0:T(4,128)(2,1)} %bitcast.3), channel_id=1, source_target_pairs={{0,16},{4,20},{8,24},{12,28},{16,0},{20,4},{24,8},{28,12},{1,17},{... | collective-permute-start | bytes 49160 | tf_op jit(solution)/shard_map/ppermute | solution.py:462
  4.5 3.9 %collective-permute-start = (bf16[1,4,2048]{2,1,0:T(4,128)(2,1)}, bf16[1,4,2048]{2,1,0:T(4,128)(2,1)S(1)}, u32[]{:S(2)}, u32[]{:S(2)}) collective-permute-start(bf16[1,4,2048]{2,1,0:T(4,128)(2,1)} %bitcast.4), channel_id=1, source_target_pairs={{0,8},{4,12},{8,0},{12,4},{16,24},{20,28},{24,16},{28,20},{1,9},{5... | collective-permute-start | bytes 49160 | tf_op jit(solution)/shard_map/ppermute | solution.py:462
  4.6 0.7 %copy-start.1 = (bf16[4,1,2,256]{3,2,1,0:T(2,128)(2,1)S(1)}, bf16[4,1,2,256]{3,2,1,0:T(2,128)(2,1)}, u32[]{:S(2)}) copy-start(bf16[4,1,2,256]{3,2,1,0:T(2,128)(2,1)} %param.7) | copy-start | bytes 12292
  10.1 5.6 %collective-permute-start.7 = (bf16[272,128]{1,0:T(8,128)(2,1)S(1)}, bf16[272,128]{1,0:T(8,128)(2,1)S(1)}, u32[]{:S(2)}, u32[]{:S(2)}) collective-permute-start(bf16[272,128]{1,0:T(8,128)(2,1)S(1)} %shard_map.57._), channel_id=1, source_target_pairs={{0,28},{4,24},{8,20},{12,16},{16,12},{20,8},{24,4},{28,0},{1,29},{... | collective-permute-start | bytes 208904 | tf_op jit(solution)/shard_map/ppermute | solution.py:462
  11.8 4.5 %collective-permute-start.6 = (bf16[272,128]{1,0:T(8,128)(2,1)S(1)}, bf16[272,128]{1,0:T(8,128)(2,1)S(1)}, u32[]{:S(2)}, u32[]{:S(2)}) collective-permute-start(bf16[272,128]{1,0:T(8,128)(2,1)S(1)} %shard_map.57._), channel_id=1, source_target_pairs={{0,20},{4,16},{8,28},{12,24},{16,4},{20,0},{24,12},{28,8},{1,21},{... | collective-permute-start | bytes 208904 | tf_op jit(solution)/shard_map/ppermute | solution.py:462
  12.3 4.4 %collective-permute-start.5 = (bf16[272,128]{1,0:T(8,128)(2,1)S(1)}, bf16[272,128]{1,0:T(8,128)(2,1)S(1)}, u32[]{:S(2)}, u32[]{:S(2)}) collective-permute-start(bf16[272,128]{1,0:T(8,128)(2,1)S(1)} %shard_map.57._), channel_id=1, source_target_pairs={{0,12},{4,8},{8,4},{12,0},{16,28},{20,24},{24,20},{28,16},{1,13},{... | collective-permute-start | bytes 208904 | tf_op jit(solution)/shard_map/ppermute | solution.py:462
  12.9 3.8 %collective-permute-start.4 = (bf16[272,128]{1,0:T(8,128)(2,1)S(1)}, bf16[272,128]{1,0:T(8,128)(2,1)S(1)}, u32[]{:S(2)}, u32[]{:S(2)}) collective-permute-start(bf16[272,128]{1,0:T(8,128)(2,1)S(1)} %shard_map.57._), channel_id=1, source_target_pairs={{0,4},{4,0},{8,12},{12,8},{16,20},{20,16},{24,28},{28,24},{1,5},{5... | collective-permute-start | bytes 208904 | tf_op jit(solution)/shard_map/ppermute | solution.py:462
  17.0 1.3 %collective-permute-start.8 = (bf16[16,2048]{1,0:T(8,128)(2,1)S(1)}, bf16[16,2048]{1,0:T(8,128)(2,1)S(1)}, u32[]{:S(2)}, u32[]{:S(2)}) collective-permute-start(bf16[16,2048]{1,0:T(8,128)(2,1)S(1)} %shard_map.59.att_ref), channel_id=1, source_target_pairs={{0,4},{4,0},{8,12},{12,8},{16,20},{20,16},{24,28},{28,24},{1,5},{5... | collective-permute-start | bytes 196616 | tf_op jit(solution)/shard_map/ppermute | solution.py:462
  19.0 5.0 %collective-permute-start.9 = (bf16[2,4,1024]{2,1,0:T(4,128)(2,1)S(1)}, bf16[2,4,1024]{2,1,0:T(4,128)(2,1)S(1)}, u32[]{:S(2)}, u32[]{:S(2)}) collective-permute-start(bf16[2,4,1024]{2,1,0:T(4,128)(2,1)S(1)} %get-tuple-element.25), channel_id=1, source_target_pairs={{0,4},{1,5},{2,0},{3,7},{4,6},{5,1},{6,2},{7,3},{8,12},{9,13},{10,... | collective-permute-start | bytes 49160 | tf_op jit(solution)/shard_map/ppermute | solution.py:457
  19.2 5.6 %collective-permute-start.10 = (bf16[2,4,1024]{2,1,0:T(4,128)(2,1)S(1)}, bf16[2,4,1024]{2,1,0:T(4,128)(2,1)S(1)}, u32[]{:S(2)}, u32[]{:S(2)}) collective-permute-start(bf16[2,4,1024]{2,1,0:T(4,128)(2,1)S(1)} %get-tuple-element.26), channel_id=1, source_target_pairs={{0,1},{1,2},{2,3},{3,0},{4,5},{5,7},{6,4},{7,6},{8,9},{9,10},{10,1... | collective-permute-start | bytes 49160 | tf_op jit(solution)/shard_map/ppermute | solution.py:457
  20.9 3.9 %collective-permute-start.11 = (bf16[2,4,1024]{2,1,0:T(4,128)(2,1)S(1)}, bf16[2,4,1024]{2,1,0:T(4,128)(2,1)S(1)}, u32[]{:S(2)}, u32[]{:S(2)}) collective-permute-start(bf16[2,4,1024]{2,1,0:T(4,128)(2,1)S(1)} %get-tuple-element.27), channel_id=1, source_target_pairs={{0,3},{1,0},{2,1},{3,2},{4,7},{5,6},{6,5},{7,4},{8,11},{9,8},{10,9... | collective-permute-start | bytes 49160 | tf_op jit(solution)/shard_map/ppermute | solution.py:457
  23.0 2.4 %collective-permute-start.12 = (bf16[2,4,1024]{2,1,0:T(4,128)(2,1)S(1)}, bf16[2,4,1024]{2,1,0:T(4,128)(2,1)S(1)}, u32[]{:S(2)}, u32[]{:S(2)}) collective-permute-start(bf16[2,4,1024]{2,1,0:T(4,128)(2,1)S(1)} %get-tuple-element.28), channel_id=1, source_target_pairs={{0,2},{1,3},{2,6},{3,1},{4,0},{5,4},{6,7},{7,5},{8,10},{9,11},{10,... | collective-permute-start | bytes 49160 | tf_op jit(solution)/shard_map/ppermute | solution.py:457

commit v10 on v9

--- a/solution.py
+++ b/solution.py
@@ -363,16 +363,20 @@
     seqs, steps, _ = out_refs[0].shape
     me = lax.axis_index("ctx")
     mine = lax.axis_index("head")
-    product = jnp.dot(att_ref[...], weight_ref[...], preferred_element_type=jnp.float32)
     for i in range(rows_all.shape[0] // 2):
-        rows_all[2 * i, :steps, :] = product[i * steps : (i + 1) * steps]
         rows_all[2 * i + 1, :steps, :] = half_ref[i * steps : (i + 1) * steps, :]
-    for k, ref in enumerate(out_refs):
+    picks = []
+    for k in range(len(out_refs)):
         target = mine
         if k > 0:
             for core, row in enumerate(targets[k - 1]):
                 for z, t in enumerate(row):
                     target = jnp.where((me % 2 == core) & (mine == z), t, target)
+        picks.append(target)
+    product = jnp.dot(att_ref[...], weight_ref[...], preferred_element_type=jnp.float32)
+    for i in range(rows_all.shape[0] // 2):
+        rows_all[2 * i, :steps, :] = product[i * steps : (i + 1) * steps]
+    for k, (ref, target) in enumerate(zip(out_refs, picks)):
         for j in range(seqs):
             found = rows_all[(jnp.maximum(target, 0) * seqs + j) ^ me, :steps]
             if k > 0 and any(t < 0 for row in targets[k - 1] for t in row):

time: 26.4 us -> 26.4 us (level)
  no operation moved by 1% of the time
where the time goes in v10:
time: 26.4 us; the launch traced here: 26.1 us
  starting transfers between devices  13.2 us (50%)
  Pallas kernels  7.1 us (27%)
  waiting for transfers between devices  4.39 us (17%)
  local copies, waits for them, and re-layouts  0.69 us (3%)
  other arithmetic  0.63 us (2%)
    ppermute x9, starting transfers between devices, swap(): return lax.ppermute(x, axis, [(i, i ^ r) for i in range(size)])  8.17 us
    ppermute x4, starting transfers between devices, send_by(): return lax.ppermute(x, ('ctx', 'head'), pairs)  5 us
    ppermute x9, waiting for transfers between devices, swap(): return lax.ppermute(x, axis, [(i, i ^ r) for i in range(size)])  2.95 us
    pallas_call x1, Pallas kernels, load_weight(): pl.pallas_call(load_kernel, out_shape=jax.ShapeDtypeStruct(out_weight.sha...  2.2 us
    pallas_call x1, Pallas kernels, own_side(): pl.pallas_call(own_kernel, out_shape=[jax.ShapeDtypeStruct((m,) + kv_cach...  1.58 us
    ppermute x4, waiting for transfers between devices, send_by(): return lax.ppermute(x, ('ctx', 'head'), pairs)  1.44 us
    pallas_call x1, Pallas kernels, partials(): pl.pallas_call(functools.partial(first_kernel, heads), out_shape=[jax.Sha...  0.92 us
    pallas_call x1, Pallas kernels, partials(): pl.pallas_call(functools.partial(second_kernel, steps, heads), out_shape=...  0.76 us
  transfers between devices with their start and end apart: 13, of which 7 were waited for; matrix products, arithmetic and copies ran while one was open for 0% of the time, Pallas kernels for 20%

profile of v10, /device:TPU:0, one launch (start us, length us, event | category | flops | bytes accessed | tf_op | source)
XLA Modules:
  0.0 26.1 jit_solution(1237474480882378234)
XLA Ops:
  0.0 0.5 %collective-permute-start.3 = (bf16[8,8,2,64,256]{4,3,2,1,0:T(8,128)(2,1)}, bf16[8,8,2,64,256]{4,3,2,1,0:T(8,128)(2,1)S(1)}, u32[]{:S(2)}, u32[]{:S(2)}) collective-permute-start(bf16[8,8,2,64,256]{4,3,2,1,0:T(8,128)(2,1)} %kv_in.1), channel_id=1, source_target_pairs={{0,4},{4,0},{8,12},{12,8},{16,20},{20,16},{24,28},{28,24},{1,5},{5... | collective-permute-start | bytes 12582920 | tf_op jit(solution)/shard_map/ppermute | solution.py:466
  0.5 3.5 %collective-permute-start.2 = (bf16[1,4,2048]{2,1,0:T(4,128)(2,1)}, bf16[1,4,2048]{2,1,0:T(4,128)(2,1)S(1)}, u32[]{:S(2)}, u32[]{:S(2)}) collective-permute-start(bf16[1,4,2048]{2,1,0:T(4,128)(2,1)} %bitcast.2), channel_id=1, source_target_pairs={{0,24},{4,28},{8,16},{12,20},{16,8},{20,12},{24,0},{28,4},{1,25},{... | collective-permute-start | bytes 49160 | tf_op jit(solution)/shard_map/ppermute | solution.py:466
  4.0 0.5 %collective-permute-start.1 = (bf16[1,4,2048]{2,1,0:T(4,128)(2,1)}, bf16[1,4,2048]{2,1,0:T(4,128)(2,1)S(1)}, u32[]{:S(2)}, u32[]{:S(2)}) collective-permute-start(bf16[1,4,2048]{2,1,0:T(4,128)(2,1)} %bitcast.3), channel_id=1, source_target_pairs={{0,16},{4,20},{8,24},{12,28},{16,0},{20,4},{24,8},{28,12},{1,17},{... | collective-permute-start | bytes 49160 | tf_op jit(solution)/shard_map/ppermute | solution.py:466
  4.5 0.1 collective-permute-start
  4.6 0.7 %copy-done.1 = bf16[4,1,2,256]{3,2,1,0:T(2,128)(2,1)S(1)} copy-done((bf16[4,1,2,256]{3,2,1,0:T(2,128)(2,1)S(1)}, bf16[4,1,2,256]{3,2,1,0:T(2,128)(2,1)}, u32[]{:S(2)}) %copy-start.1) | copy-done | bytes 4120
  5.3 1.6 %shard_map.55 = (bf16[4,8,2,64,256]{4,3,2,1,0:T(8,128)(2,1)S(1)}, s32[2,4,2,8,128]{4,3,2,1,0:T(8,128)S(1)}, bf16[2,16,256]{2,1,0:T(8,128)(2,1)S(1)}) custom-call(bf16[8,8,2,64,256]{4,3,2,1,0:T(8,128)(2,1)} %kv_in.1, s32[4,8,2,8]{3,2,1,0:T(2,128)} %selected_in.1, bf16[4,2,256]{2,1,0:T(2,128)(2,1)S(1)} %bitcast.6), custom_call_target="tpu_custom_call" | custom-call | flops 1048576 | bytes 4194304 | tf_op jit(solution)/shard_map/pallas_call | solution.py:118
  6.9 0.0 collective-permute-done.2.refs_3_
  6.9 1.0 %collective-permute-done.1.refs_2_ = bf16[1,4,2048]{2,1,0:T(4,128)(2,1)S(1)} collective-permute-done((bf16[1,4,2048]{2,1,0:T(4,128)(2,1)}, bf16[1,4,2048]{2,1,0:T(4,128)(2,1)S(1)}, u32[]{:S(2)}, u32[]{:S(2)}) %collective-permute-start.1) | collective-permute-done | bytes 16416 | tf_op jit(solution)/shard_map/ppermute | solution.py:466
  7.9 0.5 %collective-permute-done.refs_1_ = bf16[1,4,2048]{2,1,0:T(4,128)(2,1)S(1)} collective-permute-done((bf16[1,4,2048]{2,1,0:T(4,128)(2,1)}, bf16[1,4,2048]{2,1,0:T(4,128)(2,1)S(1)}, u32[]{:S(2)}, u32[]{:S(2)}) %collective-permute-start) | collective-permute-done | bytes 16416 | tf_op jit(solution)/shard_map/ppermute | solution.py:466
  8.4 0.9 %shard_map.56 = (bf16[4,64,256]{2,1,0:T(8,128)(2,1)S(1)}, f32[4,64,128]{2,1,0:T(8,128)S(1)}, f32[4,64,128]{2,1,0:T(8,128)S(1)}, f32[4,64,128]{2,1,0:T(8,128)S(1)}) custom-call(s32[2,4,2,8,128]{4,3,2,1,0:T(8,128)S(1)} %get-tuple-element.17.bits_ref, bf16[2,16,256]{2,1,0:T(8,128)(2,1)S(1)} %get-tuple-element.18.new_ref, ...), custom_call_target="tpu_custom_call" | custom-call | flops 134217728 | bytes 1048576 | tf_op jit(solution)/shard_map/pallas_call | solution.py:248
  9.3 0.0 collective-permute-done.3.other_ref
  9.4 0.8 %shard_map.57._ = bf16[272,128]{1,0:T(8,128)(2,1)S(1)} custom-call(s32[2,4,2,8,128]{4,3,2,1,0:T(8,128)S(1)} %get-tuple-element.17.bits_ref, bf16[4,64,256]{2,1,0:T(8,128)(2,1)S(1)} %get-tuple-element.20.spread_ref, f32[4,64,128]{2,1,0:T(8,128)S(1)} %get-tuple-element.21.sum_ref, f32[4,64,128]{2,1,0:T(8,128)S(1)} %get-tuple-element.22.top_ref, ...), custom_call_target="tpu_custom_call" | custom-call | flops 134217728 | bytes 1048576 | tf_op jit(solution)/shard_map/pallas_call | solution.py:261
  10.1 1.7 %collective-permute-start.7 = (bf16[272,128]{1,0:T(8,128)(2,1)S(1)}, bf16[272,128]{1,0:T(8,128)(2,1)S(1)}, u32[]{:S(2)}, u32[]{:S(2)}) collective-permute-start(bf16[272,128]{1,0:T(8,128)(2,1)S(1)} %shard_map.57._), channel_id=1, source_target_pairs={{0,28},{4,24},{8,20},{12,16},{16,12},{20,8},{24,4},{28,0},{1,29},{... | collective-permute-start | bytes 208904 | tf_op jit(solution)/shard_map/ppermute | solution.py:466
  11.8 0.5 %collective-permute-start.6 = (bf16[272,128]{1,0:T(8,128)(2,1)S(1)}, bf16[272,128]{1,0:T(8,128)(2,1)S(1)}, u32[]{:S(2)}, u32[]{:S(2)}) collective-permute-start(bf16[272,128]{1,0:T(8,128)(2,1)S(1)} %shard_map.57._), channel_id=1, source_target_pairs={{0,20},{4,16},{8,28},{12,24},{16,4},{20,0},{24,12},{28,8},{1,21},{... | collective-permute-start | bytes 208904 | tf_op jit(solution)/shard_map/ppermute | solution.py:466
  12.3 0.6 %collective-permute-start.5 = (bf16[272,128]{1,0:T(8,128)(2,1)S(1)}, bf16[272,128]{1,0:T(8,128)(2,1)S(1)}, u32[]{:S(2)}, u32[]{:S(2)}) collective-permute-start(bf16[272,128]{1,0:T(8,128)(2,1)S(1)} %shard_map.57._), channel_id=1, source_target_pairs={{0,12},{4,8},{8,4},{12,0},{16,28},{20,24},{24,20},{28,16},{1,13},{... | collective-permute-start | bytes 208904 | tf_op jit(solution)/shard_map/ppermute | solution.py:466
  12.9 0.6 %collective-permute-start.4 = (bf16[272,128]{1,0:T(8,128)(2,1)S(1)}, bf16[272,128]{1,0:T(8,128)(2,1)S(1)}, u32[]{:S(2)}, u32[]{:S(2)}) collective-permute-start(bf16[272,128]{1,0:T(8,128)(2,1)S(1)} %shard_map.57._), channel_id=1, source_target_pairs={{0,4},{4,0},{8,12},{12,8},{16,20},{20,16},{24,28},{28,24},{1,5},{5... | collective-permute-start | bytes 208904 | tf_op jit(solution)/shard_map/ppermute | solution.py:466
  13.5 2.2 %shard_map.58.refs_4_.weight_ref = bf16[2048,1024]{1,0:T(8,128)(2,1)S(1)} custom-call(bf16[2048,1024]{1,0:T(8,128)(2,1)} %weight_ref.1, bf16[272,128]{1,0:T(8,128)(2,1)S(1)} %shard_map.57._), custom_call_target="tpu_custom_call" | custom-call | bytes 8388608 | tf_op jit(solution)/shard_map/pallas_call | solution.py:344
  15.7 0.6 %collective-permute-done.6.refs_2_ = bf16[272,128]{1,0:T(8,128)(2,1)S(1)} collective-permute-done((bf16[272,128]{1,0:T(8,128)(2,1)S(1)}, bf16[272,128]{1,0:T(8,128)(2,1)S(1)}, u32[]{:S(2)}, u32[]{:S(2)}) %collective-permute-start.6) | collective-permute-done | bytes 69664 | tf_op jit(solution)/shard_map/ppermute | solution.py:466
  16.3 0.3 %collective-permute-done.5.refs_1_ = bf16[272,128]{1,0:T(8,128)(2,1)S(1)} collective-permute-done((bf16[272,128]{1,0:T(8,128)(2,1)S(1)}, bf16[272,128]{1,0:T(8,128)(2,1)S(1)}, u32[]{:S(2)}, u32[]{:S(2)}) %collective-permute-start.5) | collective-permute-done | bytes 69664 | tf_op jit(solution)/shard_map/ppermute | solution.py:466
  16.7 0.0 collective-permute-done.4.refs_0_
  16.7 0.3 %shard_map.59.att_ref = bf16[16,2048]{1,0:T(8,128)(2,1)S(1)} custom-call(bf16[272,128]{1,0:T(8,128)(2,1)S(1)} %collective-permute-done.4.refs_0_, bf16[272,128]{1,0:T(8,128)(2,1)S(1)} %collective-permute-done.5.refs_1_, bf16[272,128]{1,0:T(8,128)(2,1)S(1)} %collective-permute-done.6.refs_2_, bf16[272,128]{1,0:T(8,128)(2,1)S(1)} %collective-permute-done.7.refs_3_, ...), custom_call_target="tpu_custom_call" | custom-call | flops 262144 | bytes 262144 | tf_op jit(solution)/shard_map/pallas_call | solution.py:319
  17.0 0.2 collective-permute-start.8
  17.1 0.6 %shard_map.60.half_ref = f32[16,1024]{1,0:T(8,128)S(1)} custom-call(bf16[16,2048]{1,0:T(8,128)(2,1)S(1)} %shard_map.59.att_ref, bf16[2048,1024]{1,0:T(8,128)(2,1)S(1)} %shard_map.58.refs_4_.weight_ref), custom_call_target="tpu_custom_call" | custom-call | flops 67108864 | bytes 4194304 | tf_op jit(solution)/shard_map/pallas_call | solution.py:398
  17.8 0.5 %collective-permute-done.8.att_ref = bf16[16,2048]{1,0:T(8,128)(2,1)S(1)} collective-permute-done((bf16[16,2048]{1,0:T(8,128)(2,1)S(1)}, bf16[16,2048]{1,0:T(8,128)(2,1)S(1)}, u32[]{:S(2)}, u32[]{:S(2)}) %collective-permute-start.8) | collective-permute-done | bytes 65568 | tf_op jit(solution)/shard_map/ppermute | solution.py:466
  18.3 0.7 %shard_map.61 = (f32[2,4,1024]{2,1,0:T(4,128)S(1)}, bf16[2,4,1024]{2,1,0:T(4,128)(2,1)S(1)}, bf16[2,4,1024]{2,1,0:T(4,128)(2,1)S(1)}, bf16[2,4,1024]{2,1,0:T(4,128)(2,1)S(1)}, bf16[2,4,1024]{2,1,0:T(4,128)(2,1)S(1)}) custom-call(bf16[16,2048]{1,0:T(8,128)(2,1)S(1)} %collective-permute-done.8.att_ref, f32[16,1024]{1,0:T(8,128)S(1)} %shard_map.60.half_ref, ...), custom_call_target="tpu_custom_call" | custom-call | flops 67108864 | bytes 4194304 | tf_op jit(solution)/shard_map/pallas_call | solution.py:414
  19.0 0.2 collective-permute-start.9
  19.2 1.7 %collective-permute-start.10 = (bf16[2,4,1024]{2,1,0:T(4,128)(2,1)S(1)}, bf16[2,4,1024]{2,1,0:T(4,128)(2,1)S(1)}, u32[]{:S(2)}, u32[]{:S(2)}) collective-permute-start(bf16[2,4,1024]{2,1,0:T(4,128)(2,1)S(1)} %get-tuple-element.26), channel_id=1, source_target_pairs={{0,1},{1,2},{2,3},{3,0},{4,5},{5,7},{6,4},{7,6},{8,9},{9,10},{10,1... | collective-permute-start | bytes 49160 | tf_op jit(solution)/shard_map/ppermute | solution.py:461
  20.9 2.1 %collective-permute-start.11 = (bf16[2,4,1024]{2,1,0:T(4,128)(2,1)S(1)}, bf16[2,4,1024]{2,1,0:T(4,128)(2,1)S(1)}, u32[]{:S(2)}, u32[]{:S(2)}) collective-permute-start(bf16[2,4,1024]{2,1,0:T(4,128)(2,1)S(1)} %get-tuple-element.27), channel_id=1, source_target_pairs={{0,3},{1,0},{2,1},{3,2},{4,7},{5,6},{6,5},{7,4},{8,11},{9,8},{10,9... | collective-permute-start | bytes 49160 | tf_op jit(solution)/shard_map/ppermute | solution.py:461
  23.0 1.0 %collective-permute-start.12 = (bf16[2,4,1024]{2,1,0:T(4,128)(2,1)S(1)}, bf16[2,4,1024]{2,1,0:T(4,128)(2,1)S(1)}, u32[]{:S(2)}, u32[]{:S(2)}) collective-permute-start(bf16[2,4,1024]{2,1,0:T(4,128)(2,1)S(1)} %get-tuple-element.28), channel_id=1, source_target_pairs={{0,2},{1,3},{2,6},{3,1},{4,0},{5,4},{6,7},{7,5},{8,10},{9,11},{10,... | collective-permute-start | bytes 49160 | tf_op jit(solution)/shard_map/ppermute | solution.py:461
  24.0 0.8 %collective-permute-done.10 = bf16[2,4,1024]{2,1,0:T(4,128)(2,1)S(1)} collective-permute-done((bf16[2,4,1024]{2,1,0:T(4,128)(2,1)S(1)}, bf16[2,4,1024]{2,1,0:T(4,128)(2,1)S(1)}, u32[]{:S(2)}, u32[]{:S(2)}) %collective-permute-start.10) | collective-permute-done | bytes 16416 | tf_op jit(solution)/shard_map/ppermute | solution.py:461
  24.8 0.6 %collective-permute-done.12 = bf16[2,4,1024]{2,1,0:T(4,128)(2,1)S(1)} collective-permute-done((bf16[2,4,1024]{2,1,0:T(4,128)(2,1)S(1)}, bf16[2,4,1024]{2,1,0:T(4,128)(2,1)S(1)}, u32[]{:S(2)}, u32[]{:S(2)}) %collective-permute-start.12) | collective-permute-done | bytes 16416 | tf_op jit(solution)/shard_map/ppermute | solution.py:461
  25.4 0.6 %add_convert_fusion = bf16[2,4,1024]{2,1,0:T(4,128)(2,1)} fusion(bf16[2,4,1024]{2,1,0:T(4,128)(2,1)S(1)} %collective-permute-done.12, bf16[2,4,1024]{2,1,0:T(4,128)(2,1)S(1)} %collective-permute-done.11, bf16[2,4,1024]{2,1,0:T(4,128)(2,1)S(1)} %collective-permute-done.10, f32[2,4,1024]{2,1,0:T(4,128)S(1)} %get-tuple-element.24, ...), kind=kLoop, calls=%fused_computation | loop fusion | flops 73728 | bytes 114688 | tf_op jit(solution)/shard_map/convert_element_type | solution.py:502
  (6 shorter events, 0.0 us)
Async XLA Ops:
  0.0 8.4 %copy-start = (bf16[4,1,2048]{2,0,1:T(4,128)(2,1)S(1)}, bf16[4,1,2048]{2,0,1:T(4,128)(2,1)}, u32[]{:S(2)}) copy-start(bf16[4,1,2048]{2,0,1:T(4,128)(2,1)} %param.5) | copy-start | bytes 49156
  0.0 9.3 %collective-permute-start.3 = (bf16[8,8,2,64,256]{4,3,2,1,0:T(8,128)(2,1)}, bf16[8,8,2,64,256]{4,3,2,1,0:T(8,128)(2,1)S(1)}, u32[]{:S(2)}, u32[]{:S(2)}) collective-permute-start(bf16[8,8,2,64,256]{4,3,2,1,0:T(8,128)(2,1)} %kv_in.1), channel_id=1, source_target_pairs={{0,4},{4,0},{8,12},{12,8},{16,20},{20,16},{24,28},{28,24},{1,5},{5... | collective-permute-start | bytes 12582920 | tf_op jit(solution)/shard_map/ppermute | solution.py:466
  0.5 6.4 %collective-permute-start.2 = (bf16[1,4,2048]{2,1,0:T(4,128)(2,1)}, bf16[1,4,2048]{2,1,0:T(4,128)(2,1)S(1)}, u32[]{:S(2)}, u32[]{:S(2)}) collective-permute-start(bf16[1,4,2048]{2,1,0:T(4,128)(2,1)} %bitcast.2), channel_id=1, source_target_pairs={{0,24},{4,28},{8,16},{12,20},{16,8},{20,12},{24,0},{28,4},{1,25},{... | collective-permute-start | bytes 49160 | tf_op jit(solution)/shard_map/ppermute | solution.py:466
  4.0 3.9 %collective-permute-start.1 = (bf16[1,4,2048]{2,1,0:T(4,128)(2,1)}, bf16[1,4,2048]{2,1,0:T(4,128)(2,1)S(1)}, u32[]{:S(2)}, u32[]{:S(2)}) collective-permute-start(bf16[1,4,2048]{2,1,0:T(4,128)(2,1)} %bitcast.3), channel_id=1, source_target_pairs={{0,16},{4,20},{8,24},{12,28},{16,0},{20,4},{24,8},{28,12},{1,17},{... | collective-permute-start | bytes 49160 | tf_op jit(solution)/shard_map/ppermute | solution.py:466
  4.5 3.9 %collective-permute-start = (bf16[1,4,2048]{2,1,0:T(4,128)(2,1)}, bf16[1,4,2048]{2,1,0:T(4,128)(2,1)S(1)}, u32[]{:S(2)}, u32[]{:S(2)}) collective-permute-start(bf16[1,4,2048]{2,1,0:T(4,128)(2,1)} %bitcast.4), channel_id=1, source_target_pairs={{0,8},{4,12},{8,0},{12,4},{16,24},{20,28},{24,16},{28,20},{1,9},{5... | collective-permute-start | bytes 49160 | tf_op jit(solution)/shard_map/ppermute | solution.py:466
  4.6 0.7 %copy-start.1 = (bf16[4,1,2,256]{3,2,1,0:T(2,128)(2,1)S(1)}, bf16[4,1,2,256]{3,2,1,0:T(2,128)(2,1)}, u32[]{:S(2)}) copy-start(bf16[4,1,2,256]{3,2,1,0:T(2,128)(2,1)} %param.7) | copy-start | bytes 12292
  10.1 5.6 %collective-permute-start.7 = (bf16[272,128]{1,0:T(8,128)(2,1)S(1)}, bf16[272,128]{1,0:T(8,128)(2,1)S(1)}, u32[]{:S(2)}, u32[]{:S(2)}) collective-permute-start(bf16[272,128]{1,0:T(8,128)(2,1)S(1)} %shard_map.57._), channel_id=1, source_target_pairs={{0,28},{4,24},{8,20},{12,16},{16,12},{20,8},{24,4},{28,0},{1,29},{... | collective-permute-start | bytes 208904 | tf_op jit(solution)/shard_map/ppermute | solution.py:466
  11.8 4.5 %collective-permute-start.6 = (bf16[272,128]{1,0:T(8,128)(2,1)S(1)}, bf16[272,128]{1,0:T(8,128)(2,1)S(1)}, u32[]{:S(2)}, u32[]{:S(2)}) collective-permute-start(bf16[272,128]{1,0:T(8,128)(2,1)S(1)} %shard_map.57._), channel_id=1, source_target_pairs={{0,20},{4,16},{8,28},{12,24},{16,4},{20,0},{24,12},{28,8},{1,21},{... | collective-permute-start | bytes 208904 | tf_op jit(solution)/shard_map/ppermute | solution.py:466
  12.3 4.4 %collective-permute-start.5 = (bf16[272,128]{1,0:T(8,128)(2,1)S(1)}, bf16[272,128]{1,0:T(8,128)(2,1)S(1)}, u32[]{:S(2)}, u32[]{:S(2)}) collective-permute-start(bf16[272,128]{1,0:T(8,128)(2,1)S(1)} %shard_map.57._), channel_id=1, source_target_pairs={{0,12},{4,8},{8,4},{12,0},{16,28},{20,24},{24,20},{28,16},{1,13},{... | collective-permute-start | bytes 208904 | tf_op jit(solution)/shard_map/ppermute | solution.py:466
  12.9 3.8 %collective-permute-start.4 = (bf16[272,128]{1,0:T(8,128)(2,1)S(1)}, bf16[272,128]{1,0:T(8,128)(2,1)S(1)}, u32[]{:S(2)}, u32[]{:S(2)}) collective-permute-start(bf16[272,128]{1,0:T(8,128)(2,1)S(1)} %shard_map.57._), channel_id=1, source_target_pairs={{0,4},{4,0},{8,12},{12,8},{16,20},{20,16},{24,28},{28,24},{1,5},{5... | collective-permute-start | bytes 208904 | tf_op jit(solution)/shard_map/ppermute | solution.py:466
  17.0 1.3 %collective-permute-start.8 = (bf16[16,2048]{1,0:T(8,128)(2,1)S(1)}, bf16[16,2048]{1,0:T(8,128)(2,1)S(1)}, u32[]{:S(2)}, u32[]{:S(2)}) collective-permute-start(bf16[16,2048]{1,0:T(8,128)(2,1)S(1)} %shard_map.59.att_ref), channel_id=1, source_target_pairs={{0,4},{4,0},{8,12},{12,8},{16,20},{20,16},{24,28},{28,24},{1,5},{5... | collective-permute-start | bytes 196616 | tf_op jit(solution)/shard_map/ppermute | solution.py:466
  19.0 5.0 %collective-permute-start.9 = (bf16[2,4,1024]{2,1,0:T(4,128)(2,1)S(1)}, bf16[2,4,1024]{2,1,0:T(4,128)(2,1)S(1)}, u32[]{:S(2)}, u32[]{:S(2)}) collective-permute-start(bf16[2,4,1024]{2,1,0:T(4,128)(2,1)S(1)} %get-tuple-element.25), channel_id=1, source_target_pairs={{0,4},{1,5},{2,0},{3,7},{4,6},{5,1},{6,2},{7,3},{8,12},{9,13},{10,... | collective-permute-start | bytes 49160 | tf_op jit(solution)/shard_map/ppermute | solution.py:461
  19.2 5.6 %collective-permute-start.10 = (bf16[2,4,1024]{2,1,0:T(4,128)(2,1)S(1)}, bf16[2,4,1024]{2,1,0:T(4,128)(2,1)S(1)}, u32[]{:S(2)}, u32[]{:S(2)}) collective-permute-start(bf16[2,4,1024]{2,1,0:T(4,128)(2,1)S(1)} %get-tuple-element.26), channel_id=1, source_target_pairs={{0,1},{1,2},{2,3},{3,0},{4,5},{5,7},{6,4},{7,6},{8,9},{9,10},{10,1... | collective-permute-start | bytes 49160 | tf_op jit(solution)/shard_map/ppermute | solution.py:461
  20.9 3.9 %collective-permute-start.11 = (bf16[2,4,1024]{2,1,0:T(4,128)(2,1)S(1)}, bf16[2,4,1024]{2,1,0:T(4,128)(2,1)S(1)}, u32[]{:S(2)}, u32[]{:S(2)}) collective-permute-start(bf16[2,4,1024]{2,1,0:T(4,128)(2,1)S(1)} %get-tuple-element.27), channel_id=1, source_target_pairs={{0,3},{1,0},{2,1},{3,2},{4,7},{5,6},{6,5},{7,4},{8,11},{9,8},{10,9... | collective-permute-start | bytes 49160 | tf_op jit(solution)/shard_map/ppermute | solution.py:461
  23.0 2.4 %collective-permute-start.12 = (bf16[2,4,1024]{2,1,0:T(4,128)(2,1)S(1)}, bf16[2,4,1024]{2,1,0:T(4,128)(2,1)S(1)}, u32[]{:S(2)}, u32[]{:S(2)}) collective-permute-start(bf16[2,4,1024]{2,1,0:T(4,128)(2,1)S(1)} %get-tuple-element.28), channel_id=1, source_target_pairs={{0,2},{1,3},{2,6},{3,1},{4,0},{5,4},{6,7},{7,5},{8,10},{9,11},{10,... | collective-permute-start | bytes 49160 | tf_op jit(solution)/shard_map/ppermute | solution.py:461

commit v11 on v10

--- a/solution.py
+++ b/solution.py
@@ -201,7 +201,7 @@
         total_ref[i] = jnp.broadcast_to(total, (rows, 128))
         sum_ref[i] = own_heads(weighted, heads)
 
-    staged(len(q_refs), 1, begin, end)
+    staged(len(q_refs), len(q_refs) if len(q_refs) <= 4 else 2, begin, end)
 
 
 def second_kernel(

time: 26.4 us -> 26.4 us (level)
  no operation moved by 1% of the time
where the time goes in v11:
time: 26.4 us; the launch traced here: 26.1 us
  starting transfers between devices  13.2 us (50%)
  Pallas kernels  6.89 us (26%)
  waiting for transfers between devices  4.61 us (17%)
  local copies, waits for them, and re-layouts  0.69 us (3%)
  other arithmetic  0.63 us (2%)
    ppermute x9, starting transfers between devices, swap(): return lax.ppermute(x, axis, [(i, i ^ r) for i in range(size)])  8.17 us
    ppermute x4, starting transfers between devices, send_by(): return lax.ppermute(x, ('ctx', 'head'), pairs)  5 us
    ppermute x9, waiting for transfers between devices, swap(): return lax.ppermute(x, axis, [(i, i ^ r) for i in range(size)])  3.16 us
    pallas_call x1, Pallas kernels, load_weight(): pl.pallas_call(load_kernel, out_shape=jax.ShapeDtypeStruct(out_weight.sha...  2.2 us
    pallas_call x1, Pallas kernels, own_side(): pl.pallas_call(own_kernel, out_shape=[jax.ShapeDtypeStruct((m,) + kv_cach...  1.58 us
    ppermute x4, waiting for transfers between devices, send_by(): return lax.ppermute(x, ('ctx', 'head'), pairs)  1.44 us
    pallas_call x1, Pallas kernels, partials(): pl.pallas_call(functools.partial(second_kernel, steps, heads), out_shape=...  0.76 us
    pallas_call x1, Pallas kernels, partials(): pl.pallas_call(functools.partial(first_kernel, heads), out_shape=[jax.Sha...  0.7 us
  transfers between devices with their start and end apart: 13, of which 7 were waited for; matrix products, arithmetic and copies ran while one was open for 0% of the time, Pallas kernels for 20%

profile of v11, /device:TPU:0, one launch (start us, length us, event | category | flops | bytes accessed | tf_op | source)
XLA Modules:
  0.0 26.1 jit_solution(14235287534934787485)
XLA Ops:
  0.0 0.5 %collective-permute-start.3 = (bf16[8,8,2,64,256]{4,3,2,1,0:T(8,128)(2,1)}, bf16[8,8,2,64,256]{4,3,2,1,0:T(8,128)(2,1)S(1)}, u32[]{:S(2)}, u32[]{:S(2)}) collective-permute-start(bf16[8,8,2,64,256]{4,3,2,1,0:T(8,128)(2,1)} %kv_in.1), channel_id=1, source_target_pairs={{0,4},{4,0},{8,12},{12,8},{16,20},{20,16},{24,28},{28,24},{1,5},{5... | collective-permute-start | bytes 12582920 | tf_op jit(solution)/shard_map/ppermute | solution.py:466
  0.5 3.5 %collective-permute-start.2 = (bf16[1,4,2048]{2,1,0:T(4,128)(2,1)}, bf16[1,4,2048]{2,1,0:T(4,128)(2,1)S(1)}, u32[]{:S(2)}, u32[]{:S(2)}) collective-permute-start(bf16[1,4,2048]{2,1,0:T(4,128)(2,1)} %bitcast.2), channel_id=1, source_target_pairs={{0,24},{4,28},{8,16},{12,20},{16,8},{20,12},{24,0},{28,4},{1,25},{... | collective-permute-start | bytes 49160 | tf_op jit(solution)/shard_map/ppermute | solution.py:466
  4.0 0.5 %collective-permute-start.1 = (bf16[1,4,2048]{2,1,0:T(4,128)(2,1)}, bf16[1,4,2048]{2,1,0:T(4,128)(2,1)S(1)}, u32[]{:S(2)}, u32[]{:S(2)}) collective-permute-start(bf16[1,4,2048]{2,1,0:T(4,128)(2,1)} %bitcast.3), channel_id=1, source_target_pairs={{0,16},{4,20},{8,24},{12,28},{16,0},{20,4},{24,8},{28,12},{1,17},{... | collective-permute-start | bytes 49160 | tf_op jit(solution)/shard_map/ppermute | solution.py:466
  4.5 0.1 collective-permute-start
  4.6 0.7 %copy-done.1 = bf16[4,1,2,256]{3,2,1,0:T(2,128)(2,1)S(1)} copy-done((bf16[4,1,2,256]{3,2,1,0:T(2,128)(2,1)S(1)}, bf16[4,1,2,256]{3,2,1,0:T(2,128)(2,1)}, u32[]{:S(2)}) %copy-start.1) | copy-done | bytes 4120
  5.3 1.6 %shard_map.55 = (bf16[4,8,2,64,256]{4,3,2,1,0:T(8,128)(2,1)S(1)}, s32[2,4,2,8,128]{4,3,2,1,0:T(8,128)S(1)}, bf16[2,16,256]{2,1,0:T(8,128)(2,1)S(1)}) custom-call(bf16[8,8,2,64,256]{4,3,2,1,0:T(8,128)(2,1)} %kv_in.1, s32[4,8,2,8]{3,2,1,0:T(2,128)} %selected_in.1, bf16[4,2,256]{2,1,0:T(2,128)(2,1)S(1)} %bitcast.6), custom_call_target="tpu_custom_call" | custom-call | flops 1048576 | bytes 4194304 | tf_op jit(solution)/shard_map/pallas_call | solution.py:118
  6.9 0.0 collective-permute-done.2.refs_3_
  6.9 1.0 %collective-permute-done.1.refs_2_ = bf16[1,4,2048]{2,1,0:T(4,128)(2,1)S(1)} collective-permute-done((bf16[1,4,2048]{2,1,0:T(4,128)(2,1)}, bf16[1,4,2048]{2,1,0:T(4,128)(2,1)S(1)}, u32[]{:S(2)}, u32[]{:S(2)}) %collective-permute-start.1) | collective-permute-done | bytes 16416 | tf_op jit(solution)/shard_map/ppermute | solution.py:466
  7.9 0.5 %collective-permute-done.refs_1_ = bf16[1,4,2048]{2,1,0:T(4,128)(2,1)S(1)} collective-permute-done((bf16[1,4,2048]{2,1,0:T(4,128)(2,1)}, bf16[1,4,2048]{2,1,0:T(4,128)(2,1)S(1)}, u32[]{:S(2)}, u32[]{:S(2)}) %collective-permute-start) | collective-permute-done | bytes 16416 | tf_op jit(solution)/shard_map/ppermute | solution.py:466
  8.4 0.7 %shard_map.56 = (bf16[4,64,256]{2,1,0:T(8,128)(2,1)S(1)}, f32[4,64,128]{2,1,0:T(8,128)S(1)}, f32[4,64,128]{2,1,0:T(8,128)S(1)}, f32[4,64,128]{2,1,0:T(8,128)S(1)}) custom-call(s32[2,4,2,8,128]{4,3,2,1,0:T(8,128)S(1)} %get-tuple-element.17.bits_ref, bf16[2,16,256]{2,1,0:T(8,128)(2,1)S(1)} %get-tuple-element.18.new_ref, ...), custom_call_target="tpu_custom_call" | custom-call | flops 134217728 | bytes 1048576 | tf_op jit(solution)/shard_map/pallas_call | solution.py:248
  9.1 0.0 collective-permute-done.3.other_ref
  9.1 0.8 %shard_map.57._ = bf16[272,128]{1,0:T(8,128)(2,1)S(1)} custom-call(s32[2,4,2,8,128]{4,3,2,1,0:T(8,128)S(1)} %get-tuple-element.17.bits_ref, bf16[4,64,256]{2,1,0:T(8,128)(2,1)S(1)} %get-tuple-element.20.spread_ref, f32[4,64,128]{2,1,0:T(8,128)S(1)} %get-tuple-element.21.sum_ref, f32[4,64,128]{2,1,0:T(8,128)S(1)} %get-tuple-element.22.top_ref, ...), custom_call_target="tpu_custom_call" | custom-call | flops 134217728 | bytes 1048576 | tf_op jit(solution)/shard_map/pallas_call | solution.py:261
  9.9 1.9 %collective-permute-start.7 = (bf16[272,128]{1,0:T(8,128)(2,1)S(1)}, bf16[272,128]{1,0:T(8,128)(2,1)S(1)}, u32[]{:S(2)}, u32[]{:S(2)}) collective-permute-start(bf16[272,128]{1,0:T(8,128)(2,1)S(1)} %shard_map.57._), channel_id=1, source_target_pairs={{0,28},{4,24},{8,20},{12,16},{16,12},{20,8},{24,4},{28,0},{1,29},{... | collective-permute-start | bytes 208904 | tf_op jit(solution)/shard_map/ppermute | solution.py:466
  11.8 0.5 %collective-permute-start.6 = (bf16[272,128]{1,0:T(8,128)(2,1)S(1)}, bf16[272,128]{1,0:T(8,128)(2,1)S(1)}, u32[]{:S(2)}, u32[]{:S(2)}) collective-permute-start(bf16[272,128]{1,0:T(8,128)(2,1)S(1)} %shard_map.57._), channel_id=1, source_target_pairs={{0,20},{4,16},{8,28},{12,24},{16,4},{20,0},{24,12},{28,8},{1,21},{... | collective-permute-start | bytes 208904 | tf_op jit(solution)/shard_map/ppermute | solution.py:466
  12.3 0.4 %collective-permute-start.5 = (bf16[272,128]{1,0:T(8,128)(2,1)S(1)}, bf16[272,128]{1,0:T(8,128)(2,1)S(1)}, u32[]{:S(2)}, u32[]{:S(2)}) collective-permute-start(bf16[272,128]{1,0:T(8,128)(2,1)S(1)} %shard_map.57._), channel_id=1, source_target_pairs={{0,12},{4,8},{8,4},{12,0},{16,28},{20,24},{24,20},{28,16},{1,13},{... | collective-permute-start | bytes 208904 | tf_op jit(solution)/shard_map/ppermute | solution.py:466
  12.7 0.6 %collective-permute-start.4 = (bf16[272,128]{1,0:T(8,128)(2,1)S(1)}, bf16[272,128]{1,0:T(8,128)(2,1)S(1)}, u32[]{:S(2)}, u32[]{:S(2)}) collective-permute-start(bf16[272,128]{1,0:T(8,128)(2,1)S(1)} %shard_map.57._), channel_id=1, source_target_pairs={{0,4},{4,0},{8,12},{12,8},{16,20},{20,16},{24,28},{28,24},{1,5},{5... | collective-permute-start | bytes 208904 | tf_op jit(solution)/shard_map/ppermute | solution.py:466
  13.3 2.2 %shard_map.58.refs_4_.weight_ref = bf16[2048,1024]{1,0:T(8,128)(2,1)S(1)} custom-call(bf16[2048,1024]{1,0:T(8,128)(2,1)} %weight_ref.1, bf16[272,128]{1,0:T(8,128)(2,1)S(1)} %shard_map.57._), custom_call_target="tpu_custom_call" | custom-call | bytes 8388608 | tf_op jit(solution)/shard_map/pallas_call | solution.py:344
  15.5 0.8 %collective-permute-done.6.refs_2_ = bf16[272,128]{1,0:T(8,128)(2,1)S(1)} collective-permute-done((bf16[272,128]{1,0:T(8,128)(2,1)S(1)}, bf16[272,128]{1,0:T(8,128)(2,1)S(1)}, u32[]{:S(2)}, u32[]{:S(2)}) %collective-permute-start.6) | collective-permute-done | bytes 69664 | tf_op jit(solution)/shard_map/ppermute | solution.py:466
  16.3 0.3 %collective-permute-done.5.refs_1_ = bf16[272,128]{1,0:T(8,128)(2,1)S(1)} collective-permute-done((bf16[272,128]{1,0:T(8,128)(2,1)S(1)}, bf16[272,128]{1,0:T(8,128)(2,1)S(1)}, u32[]{:S(2)}, u32[]{:S(2)}) %collective-permute-start.5) | collective-permute-done | bytes 69664 | tf_op jit(solution)/shard_map/ppermute | solution.py:466
  16.7 0.0 collective-permute-done.4.refs_0_
  16.7 0.3 %shard_map.59.att_ref = bf16[16,2048]{1,0:T(8,128)(2,1)S(1)} custom-call(bf16[272,128]{1,0:T(8,128)(2,1)S(1)} %collective-permute-done.4.refs_0_, bf16[272,128]{1,0:T(8,128)(2,1)S(1)} %collective-permute-done.5.refs_1_, bf16[272,128]{1,0:T(8,128)(2,1)S(1)} %collective-permute-done.6.refs_2_, bf16[272,128]{1,0:T(8,128)(2,1)S(1)} %collective-permute-done.7.refs_3_, ...), custom_call_target="tpu_custom_call" | custom-call | flops 262144 | bytes 262144 | tf_op jit(solution)/shard_map/pallas_call | solution.py:319
  17.0 0.2 collective-permute-start.8
  17.1 0.6 %shard_map.60.half_ref = f32[16,1024]{1,0:T(8,128)S(1)} custom-call(bf16[16,2048]{1,0:T(8,128)(2,1)S(1)} %shard_map.59.att_ref, bf16[2048,1024]{1,0:T(8,128)(2,1)S(1)} %shard_map.58.refs_4_.weight_ref), custom_call_target="tpu_custom_call" | custom-call | flops 67108864 | bytes 4194304 | tf_op jit(solution)/shard_map/pallas_call | solution.py:398
  17.8 0.5 %collective-permute-done.8.att_ref = bf16[16,2048]{1,0:T(8,128)(2,1)S(1)} collective-permute-done((bf16[16,2048]{1,0:T(8,128)(2,1)S(1)}, bf16[16,2048]{1,0:T(8,128)(2,1)S(1)}, u32[]{:S(2)}, u32[]{:S(2)}) %collective-permute-start.8) | collective-permute-done | bytes 65568 | tf_op jit(solution)/shard_map/ppermute | solution.py:466
  18.3 0.7 %shard_map.61 = (f32[2,4,1024]{2,1,0:T(4,128)S(1)}, bf16[2,4,1024]{2,1,0:T(4,128)(2,1)S(1)}, bf16[2,4,1024]{2,1,0:T(4,128)(2,1)S(1)}, bf16[2,4,1024]{2,1,0:T(4,128)(2,1)S(1)}, bf16[2,4,1024]{2,1,0:T(4,128)(2,1)S(1)}) custom-call(bf16[16,2048]{1,0:T(8,128)(2,1)S(1)} %collective-permute-done.8.att_ref, f32[16,1024]{1,0:T(8,128)S(1)} %shard_map.60.half_ref, ...), custom_call_target="tpu_custom_call" | custom-call | flops 67108864 | bytes 4194304 | tf_op jit(solution)/shard_map/pallas_call | solution.py:414
  19.0 0.2 collective-permute-start.9
  19.2 1.7 %collective-permute-start.10 = (bf16[2,4,1024]{2,1,0:T(4,128)(2,1)S(1)}, bf16[2,4,1024]{2,1,0:T(4,128)(2,1)S(1)}, u32[]{:S(2)}, u32[]{:S(2)}) collective-permute-start(bf16[2,4,1024]{2,1,0:T(4,128)(2,1)S(1)} %get-tuple-element.26), channel_id=1, source_target_pairs={{0,1},{1,2},{2,3},{3,0},{4,5},{5,7},{6,4},{7,6},{8,9},{9,10},{10,1... | collective-permute-start | bytes 49160 | tf_op jit(solution)/shard_map/ppermute | solution.py:461
  20.9 2.1 %collective-permute-start.11 = (bf16[2,4,1024]{2,1,0:T(4,128)(2,1)S(1)}, bf16[2,4,1024]{2,1,0:T(4,128)(2,1)S(1)}, u32[]{:S(2)}, u32[]{:S(2)}) collective-permute-start(bf16[2,4,1024]{2,1,0:T(4,128)(2,1)S(1)} %get-tuple-element.27), channel_id=1, source_target_pairs={{0,3},{1,0},{2,1},{3,2},{4,7},{5,6},{6,5},{7,4},{8,11},{9,8},{10,9... | collective-permute-start | bytes 49160 | tf_op jit(solution)/shard_map/ppermute | solution.py:461
  23.0 1.0 %collective-permute-start.12 = (bf16[2,4,1024]{2,1,0:T(4,128)(2,1)S(1)}, bf16[2,4,1024]{2,1,0:T(4,128)(2,1)S(1)}, u32[]{:S(2)}, u32[]{:S(2)}) collective-permute-start(bf16[2,4,1024]{2,1,0:T(4,128)(2,1)S(1)} %get-tuple-element.28), channel_id=1, source_target_pairs={{0,2},{1,3},{2,6},{3,1},{4,0},{5,4},{6,7},{7,5},{8,10},{9,11},{10,... | collective-permute-start | bytes 49160 | tf_op jit(solution)/shard_map/ppermute | solution.py:461
  24.0 0.8 %collective-permute-done.10 = bf16[2,4,1024]{2,1,0:T(4,128)(2,1)S(1)} collective-permute-done((bf16[2,4,1024]{2,1,0:T(4,128)(2,1)S(1)}, bf16[2,4,1024]{2,1,0:T(4,128)(2,1)S(1)}, u32[]{:S(2)}, u32[]{:S(2)}) %collective-permute-start.10) | collective-permute-done | bytes 16416 | tf_op jit(solution)/shard_map/ppermute | solution.py:461
  24.8 0.6 %collective-permute-done.12 = bf16[2,4,1024]{2,1,0:T(4,128)(2,1)S(1)} collective-permute-done((bf16[2,4,1024]{2,1,0:T(4,128)(2,1)S(1)}, bf16[2,4,1024]{2,1,0:T(4,128)(2,1)S(1)}, u32[]{:S(2)}, u32[]{:S(2)}) %collective-permute-start.12) | collective-permute-done | bytes 16416 | tf_op jit(solution)/shard_map/ppermute | solution.py:461
  25.4 0.6 %add_convert_fusion = bf16[2,4,1024]{2,1,0:T(4,128)(2,1)} fusion(bf16[2,4,1024]{2,1,0:T(4,128)(2,1)S(1)} %collective-permute-done.12, bf16[2,4,1024]{2,1,0:T(4,128)(2,1)S(1)} %collective-permute-done.11, bf16[2,4,1024]{2,1,0:T(4,128)(2,1)S(1)} %collective-permute-done.10, f32[2,4,1024]{2,1,0:T(4,128)S(1)} %get-tuple-element.24, ...), kind=kLoop, calls=%fused_computation | loop fusion | flops 73728 | bytes 114688 | tf_op jit(solution)/shard_map/convert_element_type | solution.py:502
  (6 shorter events, 0.0 us)
Async XLA Ops:
  0.0 8.4 %copy-start = (bf16[4,1,2048]{2,0,1:T(4,128)(2,1)S(1)}, bf16[4,1,2048]{2,0,1:T(4,128)(2,1)}, u32[]{:S(2)}) copy-start(bf16[4,1,2048]{2,0,1:T(4,128)(2,1)} %param.5) | copy-start | bytes 49156
  0.0 9.1 %collective-permute-start.3 = (bf16[8,8,2,64,256]{4,3,2,1,0:T(8,128)(2,1)}, bf16[8,8,2,64,256]{4,3,2,1,0:T(8,128)(2,1)S(1)}, u32[]{:S(2)}, u32[]{:S(2)}) collective-permute-start(bf16[8,8,2,64,256]{4,3,2,1,0:T(8,128)(2,1)} %kv_in.1), channel_id=1, source_target_pairs={{0,4},{4,0},{8,12},{12,8},{16,20},{20,16},{24,28},{28,24},{1,5},{5... | collective-permute-start | bytes 12582920 | tf_op jit(solution)/shard_map/ppermute | solution.py:466
  0.5 6.4 %collective-permute-start.2 = (bf16[1,4,2048]{2,1,0:T(4,128)(2,1)}, bf16[1,4,2048]{2,1,0:T(4,128)(2,1)S(1)}, u32[]{:S(2)}, u32[]{:S(2)}) collective-permute-start(bf16[1,4,2048]{2,1,0:T(4,128)(2,1)} %bitcast.2), channel_id=1, source_target_pairs={{0,24},{4,28},{8,16},{12,20},{16,8},{20,12},{24,0},{28,4},{1,25},{... | collective-permute-start | bytes 49160 | tf_op jit(solution)/shard_map/ppermute | solution.py:466
  4.0 3.9 %collective-permute-start.1 = (bf16[1,4,2048]{2,1,0:T(4,128)(2,1)}, bf16[1,4,2048]{2,1,0:T(4,128)(2,1)S(1)}, u32[]{:S(2)}, u32[]{:S(2)}) collective-permute-start(bf16[1,4,2048]{2,1,0:T(4,128)(2,1)} %bitcast.3), channel_id=1, source_target_pairs={{0,16},{4,20},{8,24},{12,28},{16,0},{20,4},{24,8},{28,12},{1,17},{... | collective-permute-start | bytes 49160 | tf_op jit(solution)/shard_map/ppermute | solution.py:466
  4.5 3.9 %collective-permute-start = (bf16[1,4,2048]{2,1,0:T(4,128)(2,1)}, bf16[1,4,2048]{2,1,0:T(4,128)(2,1)S(1)}, u32[]{:S(2)}, u32[]{:S(2)}) collective-permute-start(bf16[1,4,2048]{2,1,0:T(4,128)(2,1)} %bitcast.4), channel_id=1, source_target_pairs={{0,8},{4,12},{8,0},{12,4},{16,24},{20,28},{24,16},{28,20},{1,9},{5... | collective-permute-start | bytes 49160 | tf_op jit(solution)/shard_map/ppermute | solution.py:466
  4.6 0.7 %copy-start.1 = (bf16[4,1,2,256]{3,2,1,0:T(2,128)(2,1)S(1)}, bf16[4,1,2,256]{3,2,1,0:T(2,128)(2,1)}, u32[]{:S(2)}) copy-start(bf16[4,1,2,256]{3,2,1,0:T(2,128)(2,1)} %param.7) | copy-start | bytes 12292
  9.9 5.6 %collective-permute-start.7 = (bf16[272,128]{1,0:T(8,128)(2,1)S(1)}, bf16[272,128]{1,0:T(8,128)(2,1)S(1)}, u32[]{:S(2)}, u32[]{:S(2)}) collective-permute-start(bf16[272,128]{1,0:T(8,128)(2,1)S(1)} %shard_map.57._), channel_id=1, source_target_pairs={{0,28},{4,24},{8,20},{12,16},{16,12},{20,8},{24,4},{28,0},{1,29},{... | collective-permute-start | bytes 208904 | tf_op jit(solution)/shard_map/ppermute | solution.py:466
  11.8 4.5 %collective-permute-start.6 = (bf16[272,128]{1,0:T(8,128)(2,1)S(1)}, bf16[272,128]{1,0:T(8,128)(2,1)S(1)}, u32[]{:S(2)}, u32[]{:S(2)}) collective-permute-start(bf16[272,128]{1,0:T(8,128)(2,1)S(1)} %shard_map.57._), channel_id=1, source_target_pairs={{0,20},{4,16},{8,28},{12,24},{16,4},{20,0},{24,12},{28,8},{1,21},{... | collective-permute-start | bytes 208904 | tf_op jit(solution)/shard_map/ppermute | solution.py:466
  12.3 4.4 %collective-permute-start.5 = (bf16[272,128]{1,0:T(8,128)(2,1)S(1)}, bf16[272,128]{1,0:T(8,128)(2,1)S(1)}, u32[]{:S(2)}, u32[]{:S(2)}) collective-permute-start(bf16[272,128]{1,0:T(8,128)(2,1)S(1)} %shard_map.57._), channel_id=1, source_target_pairs={{0,12},{4,8},{8,4},{12,0},{16,28},{20,24},{24,20},{28,16},{1,13},{... | collective-permute-start | bytes 208904 | tf_op jit(solution)/shard_map/ppermute | solution.py:466
  12.7 4.0 %collective-permute-start.4 = (bf16[272,128]{1,0:T(8,128)(2,1)S(1)}, bf16[272,128]{1,0:T(8,128)(2,1)S(1)}, u32[]{:S(2)}, u32[]{:S(2)}) collective-permute-start(bf16[272,128]{1,0:T(8,128)(2,1)S(1)} %shard_map.57._), channel_id=1, source_target_pairs={{0,4},{4,0},{8,12},{12,8},{16,20},{20,16},{24,28},{28,24},{1,5},{5... | collective-permute-start | bytes 208904 | tf_op jit(solution)/shard_map/ppermute | solution.py:466
  17.0 1.3 %collective-permute-start.8 = (bf16[16,2048]{1,0:T(8,128)(2,1)S(1)}, bf16[16,2048]{1,0:T(8,128)(2,1)S(1)}, u32[]{:S(2)}, u32[]{:S(2)}) collective-permute-start(bf16[16,2048]{1,0:T(8,128)(2,1)S(1)} %shard_map.59.att_ref), channel_id=1, source_target_pairs={{0,4},{4,0},{8,12},{12,8},{16,20},{20,16},{24,28},{28,24},{1,5},{5... | collective-permute-start | bytes 196616 | tf_op jit(solution)/shard_map/ppermute | solution.py:466
  19.0 5.0 %collective-permute-start.9 = (bf16[2,4,1024]{2,1,0:T(4,128)(2,1)S(1)}, bf16[2,4,1024]{2,1,0:T(4,128)(2,1)S(1)}, u32[]{:S(2)}, u32[]{:S(2)}) collective-permute-start(bf16[2,4,1024]{2,1,0:T(4,128)(2,1)S(1)} %get-tuple-element.25), channel_id=1, source_target_pairs={{0,4},{1,5},{2,0},{3,7},{4,6},{5,1},{6,2},{7,3},{8,12},{9,13},{10,... | collective-permute-start | bytes 49160 | tf_op jit(solution)/shard_map/ppermute | solution.py:461
  19.2 5.6 %collective-permute-start.10 = (bf16[2,4,1024]{2,1,0:T(4,128)(2,1)S(1)}, bf16[2,4,1024]{2,1,0:T(4,128)(2,1)S(1)}, u32[]{:S(2)}, u32[]{:S(2)}) collective-permute-start(bf16[2,4,1024]{2,1,0:T(4,128)(2,1)S(1)} %get-tuple-element.26), channel_id=1, source_target_pairs={{0,1},{1,2},{2,3},{3,0},{4,5},{5,7},{6,4},{7,6},{8,9},{9,10},{10,1... | collective-permute-start | bytes 49160 | tf_op jit(solution)/shard_map/ppermute | solution.py:461
  20.9 3.9 %collective-permute-start.11 = (bf16[2,4,1024]{2,1,0:T(4,128)(2,1)S(1)}, bf16[2,4,1024]{2,1,0:T(4,128)(2,1)S(1)}, u32[]{:S(2)}, u32[]{:S(2)}) collective-permute-start(bf16[2,4,1024]{2,1,0:T(4,128)(2,1)S(1)} %get-tuple-element.27), channel_id=1, source_target_pairs={{0,3},{1,0},{2,1},{3,2},{4,7},{5,6},{6,5},{7,4},{8,11},{9,8},{10,9... | collective-permute-start | bytes 49160 | tf_op jit(solution)/shard_map/ppermute | solution.py:461
  23.0 2.4 %collective-permute-start.12 = (bf16[2,4,1024]{2,1,0:T(4,128)(2,1)S(1)}, bf16[2,4,1024]{2,1,0:T(4,128)(2,1)S(1)}, u32[]{:S(2)}, u32[]{:S(2)}) collective-permute-start(bf16[2,4,1024]{2,1,0:T(4,128)(2,1)S(1)} %get-tuple-element.28), channel_id=1, source_target_pairs={{0,2},{1,3},{2,6},{3,1},{4,0},{5,4},{6,7},{7,5},{8,10},{9,11},{10,... | collective-permute-start | bytes 49160 | tf_op jit(solution)/shard_map/ppermute | solution.py:461
